TPU v7x, 32 devices: a whole 2x2x4 slice. The times are simulated.
32 devices in a mesh: ctx: 4 (over z), fsdp: 8 (over y, x, core).
Axes of the slice: x: 2, y: 2, z: 4, core: 2. Of those that a mesh axis runs over, the one named last changes fastest.
Arguments:
- inputs: bfloat16 [8, 1024, 2048], P('fsdp', 'ctx'), may hold values from -6 to 6
- block_ids: int32 [8, 1024], P('fsdp'), may hold values from 0 to 3, never falling along the last dimension, each value on 1 to 512 neighbouring positions
- expert_ids: int32 [8, 1024, 8], P('fsdp', 'ctx'), may hold values from 0 to 31, all different within a row
- drop_order: int32 [8, 4, 256], P('fsdp', 'ctx'), may hold values from 0 to 255, each once within a row
- attn_gain: bfloat16 [2048], P('fsdp'), may hold values from 0.5 to 1.5
- w_query: bfloat16 [2048, 4096], P('fsdp'), may hold values from -0.125 to 0.125
- key_projection_weight: bfloat16 [2048, 512], P('fsdp'), may hold values from -0.125 to 0.125
- value_projection_weight: bfloat16 [2048, 512], P('fsdp'), may hold values from -0.125 to 0.125
- q_gain: bfloat16 [128], P('fsdp'), may hold values from 0.099609375 to 1.8984375
- key_norm_gain: bfloat16 [128], P('fsdp'), may hold values from 0.099609375 to 1.8984375
- w_out: bfloat16 [4096, 2048], P('fsdp'), may hold values from -0.75 to 0.75
- ffn_gain: bfloat16 [2048], P('fsdp'), may hold values from 0.5 to 1.5
- w_router: bfloat16 [2048, 32], P('fsdp'), may hold values from -0.06591797 to 0.06591797
- expert_gate: bfloat16 [32, 2048, 768], P(('ctx', 'fsdp')), may hold values from -0.125 to 0.125
- expert_up: bfloat16 [32, 2048, 768], P(('ctx', 'fsdp')), may hold values from -0.125 to 0.125
- expert_down: bfloat16 [32, 768, 2048], P(('ctx', 'fsdp')), may hold values from -0.875 to 0.875
- cotangent: bfloat16 [8, 1024, 2048], P('fsdp', 'ctx'), may hold values from -6 to 6
Outputs:
- output: bfloat16 [8, 1024, 2048], P('fsdp', 'ctx')
- input_grad: bfloat16 [8, 1024, 2048], P('fsdp', 'ctx')
- attn_gain_grad: float32 [2048], P('fsdp')
- w_query_grad: float32 [2048, 4096], P('fsdp')
- w_key_grad: float32 [2048, 512], P('fsdp')
- w_value_grad: float32 [2048, 512], P('fsdp')
- q_gain_grad: float32 [128], P('fsdp')
- k_gain_grad: float32 [128], P('fsdp')
- w_out_grad: float32 [4096, 2048], P('fsdp')
- ffn_gain_grad: float32 [2048], P('fsdp')
- w_router_grad: float32 [2048, 32], P('fsdp')
- expert_gate_grad: float32 [32, 2048, 768], P(('ctx', 'fsdp'))
- expert_up_grad: float32 [32, 2048, 768], P(('ctx', 'fsdp'))
- expert_down_grad: float32 [32, 768, 2048], P(('ctx', 'fsdp'))
Inputs may be any that keep to these rules, and one draw needn't show every extreme that they name: `block_ids`: block numbers never fall along a sequence; a block holds 1 to 512 positions. `expert_ids`: each token names 8 different experts. `drop_order`: for each device's group of 256 tokens the ranks are a permutation.
All inputs are finite; a program needn't handle non-finite values.
Results may differ from a plain program's by a relative error of at most 0.025.
Values may be sent and summed in bfloat16 or wider, within the bound.
A program may use at most 320 MiB of HBM per device.

v0:
```python
import jax
import jax.numpy as jnp
from jax import lax
from jax.sharding import PartitionSpec as P

MODEL_WIDTH = 2048
QUERY_HEADS = 32
KEY_VALUE_HEADS = 4
HEAD_SIZE = 128
TOP = 8


EPSILON = 1e-06
ROPE_BASE = 1000000.0
MASKED = -1000000000.0


def normalized_rows(values, gain_scale_apply):
    return (
        values
        * lax.rsqrt(jnp.mean(values * values, axis=-1, keepdims=True) + EPSILON)
        * gain_scale_apply
    )


def apply_rotation(values, token_positions):
    half_dim = values.shape[-1] // 2
    exponent = jnp.arange(half_dim, dtype=jnp.float32) * (2.0 / values.shape[-1])
    angles = token_positions.astype(jnp.float32)[:, None] * (ROPE_BASE ** (-exponent))[None, :]
    cosine = jnp.cos(angles)[:, None, :]
    sine_part = jnp.sin(angles)[:, None, :]
    first_half = values[..., :half_dim]
    second = values[..., half_dim:]
    return jnp.concatenate(
        [first_half * cosine - second * sine_part, second * cosine + first_half * sine_part],
        axis=-1,
    )


def reshape_to_heads(unnormalized_rows, gain_scale_apply, token_positions, heads):
    return apply_rotation(
        normalized_rows(
            unnormalized_rows.reshape(unnormalized_rows.shape[0], heads, -1), gain_scale_apply
        ),
        token_positions,
    )


def route_rows(buffer):
    return lax.all_to_all(buffer, ("ctx", "fsdp"), split_axis=0, concat_axis=0, tiled=True)


def on_device(
    inputs,
    block_ids,
    expert_ids,
    drop_order,
    attn_gain,
    w_query,
    key_projection_weight,
    value_projection_weight,
    q_gain,
    key_norm_gain,
    w_out,
    ffn_gain,
    w_router,
    expert_gate,
    expert_up,
    expert_down,
    cotangent,
):
    sequence_count = inputs.shape[0]
    span_length = inputs.shape[1]
    token_count = sequence_count * span_length
    sequence_length = block_ids.shape[1]
    group_width = QUERY_HEADS // KEY_VALUE_HEADS
    score_scale = HEAD_SIZE ** (-0.5)
    expert_count = lax.axis_size("ctx") * lax.axis_size("fsdp")
    capacity = 5 * token_count * TOP // (4 * expert_count)
    total_slots = expert_count * capacity
    ctx_index = lax.axis_index("ctx")
    gathered = (
        lax.all_gather(attn_gain, "fsdp", axis=0, tiled=True),
        lax.all_gather(w_query, "fsdp", axis=0, tiled=True),
        lax.all_gather(key_projection_weight, "fsdp", axis=0, tiled=True),
        lax.all_gather(value_projection_weight, "fsdp", axis=0, tiled=True),
        lax.all_gather(q_gain, "fsdp", axis=0, tiled=True),
        lax.all_gather(key_norm_gain, "fsdp", axis=0, tiled=True),
        lax.all_gather(w_out, "fsdp", axis=0, tiled=True),
        lax.all_gather(ffn_gain, "fsdp", axis=0, tiled=True),
        lax.all_gather(w_router, "fsdp", axis=0, tiled=True),
    )
    (
        gain_attn,
        full_query,
        full_key,
        full_value,
        gain_query,
        key_gain_name,
        full_out,
        gain_ffn,
        full_router,
    ) = gathered
    gain_attn = gain_attn.astype(jnp.float32)
    gain_query = gain_query.astype(jnp.float32)
    key_gain_name = key_gain_name.astype(jnp.float32)
    gain_ffn = gain_ffn.astype(jnp.float32)
    resid_in = inputs.astype(jnp.float32).reshape(token_count, MODEL_WIDTH)
    token_positions = jnp.tile(
        jnp.arange(span_length, dtype=jnp.int32) + ctx_index * span_length, sequence_count
    )
    hidden = normalized_rows(resid_in, gain_attn).astype(jnp.bfloat16)
    q_raw = jnp.dot(hidden, full_query, preferred_element_type=jnp.float32)
    key_unrotated = jnp.dot(hidden, full_key, preferred_element_type=jnp.float32)
    value_unprojected = jnp.dot(hidden, full_value, preferred_element_type=jnp.float32)
    query_matrix = reshape_to_heads(q_raw, gain_query, token_positions, QUERY_HEADS).astype(
        jnp.bfloat16
    )
    keys_local = (
        reshape_to_heads(key_unrotated, key_gain_name, token_positions, KEY_VALUE_HEADS)
        .astype(jnp.bfloat16)
        .reshape(sequence_count, span_length, KEY_VALUE_HEADS * HEAD_SIZE)
    )
    value_rows_local = value_unprojected.astype(jnp.bfloat16).reshape(
        sequence_count, span_length, KEY_VALUE_HEADS * HEAD_SIZE
    )
    key_rows_gathered, value_rows_gathered = (
        lax.all_gather(keys_local, "ctx", axis=1, tiled=True),
        lax.all_gather(value_rows_local, "ctx", axis=1, tiled=True),
    )
    own_blocks = lax.dynamic_slice_in_dim(block_ids, ctx_index * span_length, span_length, 1)
    visible = block_ids[:, None, None, :] <= own_blocks[:, None, :, None]
    query_head_rows = query_matrix.reshape(
        sequence_count, span_length, KEY_VALUE_HEADS, group_width, HEAD_SIZE
    ).transpose(2, 0, 3, 1, 4)
    key_head_rows = key_rows_gathered.reshape(
        sequence_count, sequence_length, KEY_VALUE_HEADS, HEAD_SIZE
    ).transpose(2, 0, 1, 3)
    value_head_rows = value_rows_gathered.reshape(
        sequence_count, sequence_length, KEY_VALUE_HEADS, HEAD_SIZE
    ).transpose(2, 0, 1, 3)

    def head_scores(q_head, k_head):
        scores = (
            jnp.einsum("sgqd,skd->sgqk", q_head, k_head, preferred_element_type=jnp.float32)
            * score_scale
        )
        return jnp.where(visible, scores, MASKED)

    def head_forward(operands):
        q_head, k_head, v_head = operands
        scores = head_scores(q_head, k_head)
        row_max = jnp.max(scores, axis=-1, keepdims=True)
        log_total = row_max + jnp.log(jnp.sum(jnp.exp(scores - row_max), axis=-1, keepdims=True))
        weights = jnp.exp(scores - log_total).astype(jnp.bfloat16)
        mixed_head = jnp.einsum(
            "sgqk,skd->sgqd", weights, v_head, preferred_element_type=jnp.float32
        )
        return (mixed_head.astype(jnp.bfloat16), log_total)

    mixed_heads, log_totals = lax.map(
        head_forward, (query_head_rows, key_head_rows, value_head_rows)
    )
    mixed = mixed_heads.transpose(1, 3, 0, 2, 4).reshape(token_count, QUERY_HEADS * HEAD_SIZE)
    attn_out = jnp.dot(mixed, full_out, preferred_element_type=jnp.float32)
    resid = resid_in + attn_out
    normed = normalized_rows(resid, gain_ffn).astype(jnp.bfloat16)
    logits = jnp.dot(normed, full_router, preferred_element_type=jnp.float32)
    routed = expert_ids.reshape(token_count, TOP)
    gate_mix = jax.nn.softmax(jnp.take_along_axis(logits, routed, axis=1), axis=-1)
    ranks = drop_order.reshape(token_count)
    chosen = routed[:, :, None] == jnp.arange(expert_count, dtype=jnp.int32)
    member = jnp.sum(chosen.astype(jnp.bfloat16), axis=1)
    before = (ranks[None, :] < ranks[:, None]).astype(jnp.bfloat16)
    position = jnp.dot(before, member, preferred_element_type=jnp.float32)
    placed = jnp.sum(jnp.where(chosen, position[:, None, :], 0.0), axis=-1).astype(jnp.int32)
    slot_ids = jnp.where(placed < capacity, routed * capacity + placed, total_slots)
    kept_mask = slot_ids < total_slots
    flat_slots = slot_ids.reshape(-1)
    token_ids = jnp.repeat(jnp.arange(token_count, dtype=jnp.int32), TOP)
    owner_row = jnp.zeros(total_slots, jnp.int32).at[flat_slots].set(token_ids, mode="drop")
    mix_weight = jnp.where(kept_mask, gate_mix, 0.0)
    slot_gate = (
        jnp.zeros(total_slots, jnp.float32).at[flat_slots].set(mix_weight.reshape(-1), mode="drop")
    )
    filled = jnp.zeros(total_slots, jnp.bfloat16).at[flat_slots].set(1.0, mode="drop")
    outgoing = (normed[owner_row] * filled[:, None]).reshape(expert_count, capacity, MODEL_WIDTH)
    received_rows = route_rows(outgoing).reshape(total_slots, MODEL_WIDTH)
    gate_act = jnp.dot(received_rows, expert_gate[0], preferred_element_type=jnp.float32)
    up_act = jnp.dot(received_rows, expert_up[0], preferred_element_type=jnp.float32)
    inner_act = (jax.nn.silu(gate_act) * up_act).astype(jnp.bfloat16)
    result = jnp.dot(inner_act, expert_down[0], preferred_element_type=jnp.float32).astype(
        jnp.bfloat16
    )
    returned = route_rows(result.reshape(expert_count, capacity, MODEL_WIDTH)).reshape(
        total_slots, MODEL_WIDTH
    )
    clipped = jnp.minimum(slot_ids, total_slots - 1)
    picked = returned[clipped].astype(jnp.float32)
    moe_out = jnp.einsum("tk,tkd->td", mix_weight, picked)
    output = (
        (resid + moe_out).astype(jnp.bfloat16).reshape(sequence_count, span_length, MODEL_WIDTH)
    )
    out_grad = cotangent.astype(jnp.float32).reshape(token_count, MODEL_WIDTH)
    mix_grad = jnp.where(kept_mask, jnp.einsum("td,tkd->tk", out_grad, picked), 0.0)
    chosen_grad = gate_mix * (mix_grad - jnp.sum(gate_mix * mix_grad, axis=-1, keepdims=True))
    logit_grad = jnp.sum(jnp.where(chosen, chosen_grad[:, :, None], 0.0), axis=1).astype(
        jnp.bfloat16
    )
    result_grad = (out_grad[owner_row] * slot_gate[:, None]).astype(jnp.bfloat16)
    slot_grad = route_rows(result_grad.reshape(expert_count, capacity, MODEL_WIDTH)).reshape(
        total_slots, MODEL_WIDTH
    )
    down_grad = jnp.einsum("rf,rd->fd", inner_act, slot_grad, preferred_element_type=jnp.float32)
    inner_grad = jnp.einsum(
        "rd,fd->rf", slot_grad, expert_down[0], preferred_element_type=jnp.float32
    )
    gate_sig = jax.nn.sigmoid(gate_act)
    gate_grad = (inner_grad * up_act * gate_sig * (1.0 + gate_act * (1.0 - gate_sig))).astype(
        jnp.bfloat16
    )
    up_projection_gradient = (inner_grad * gate_act * gate_sig).astype(jnp.bfloat16)
    egate_grad = jnp.einsum(
        "gn,go->no", received_rows, gate_grad, preferred_element_type=jnp.float32
    )
    expert_up_gradient = jnp.einsum(
        "gn,go->no", received_rows, up_projection_gradient, preferred_element_type=jnp.float32
    )
    arrived_grad = jnp.einsum(
        "rf,df->rd", gate_grad, expert_gate[0], preferred_element_type=jnp.float32
    )
    arrived_grad = arrived_grad + jnp.einsum(
        "rf,df->rd", up_projection_gradient, expert_up[0], preferred_element_type=jnp.float32
    )
    sent_grad = route_rows(
        arrived_grad.astype(jnp.bfloat16).reshape(expert_count, capacity, MODEL_WIDTH)
    ).reshape(total_slots, MODEL_WIDTH)
    normed_grad = jnp.einsum(
        "tk,tkd->td", kept_mask.astype(jnp.float32), sent_grad[clipped].astype(jnp.float32)
    )
    normed_grad = normed_grad + jnp.einsum(
        "te,de->td", logit_grad, full_router, preferred_element_type=jnp.float32
    )
    resid_back = jax.vjp(normalized_rows, resid, gain_ffn)[1]
    resid_part, ffn_gain_part = resid_back(normed_grad)
    resid_grad = out_grad + resid_part
    attn_grad = resid_grad.astype(jnp.bfloat16)
    mixed_gradient = jnp.einsum(
        "td,cd->tc", attn_grad, full_out, preferred_element_type=jnp.float32
    ).astype(jnp.bfloat16)
    mixed_head_gradient = mixed_gradient.reshape(
        sequence_count, span_length, KEY_VALUE_HEADS, group_width, HEAD_SIZE
    ).transpose(2, 0, 3, 1, 4)

    def head_backward(operands):
        q_head, k_head, v_head, log_total, grad_head = operands
        scores = head_scores(q_head, k_head)
        weights = jnp.exp(scores - log_total)
        weight_grad = jnp.einsum(
            "sgqd,skd->sgqk", grad_head, v_head, preferred_element_type=jnp.float32
        )
        row_dot = jnp.sum(weights * weight_grad, axis=-1, keepdims=True)
        score_grad = (weights * (weight_grad - row_dot)).astype(jnp.bfloat16)
        query_grad = (
            jnp.einsum("sgqk,skd->sgqd", score_grad, k_head, preferred_element_type=jnp.float32)
            * score_scale
        )
        key_grad = (
            jnp.einsum("sgqk,sgqd->skd", score_grad, q_head, preferred_element_type=jnp.float32)
            * score_scale
        )
        value_grad = jnp.einsum(
            "sgqk,sgqd->skd",
            weights.astype(jnp.bfloat16),
            grad_head,
            preferred_element_type=jnp.float32,
        )
        return (query_grad, key_grad, value_grad)

    query_heads_grad, key_head_gradient, value_head_gradient = lax.map(
        head_backward,
        (query_head_rows, key_head_rows, value_head_rows, log_totals, mixed_head_gradient),
    )
    query_grad = query_heads_grad.transpose(1, 3, 0, 2, 4).reshape(
        token_count, QUERY_HEADS, HEAD_SIZE
    )
    key_complete_gradient = key_head_gradient.transpose(1, 2, 0, 3).reshape(
        sequence_count, sequence_length, KEY_VALUE_HEADS * HEAD_SIZE
    )
    value_complete_gradient = value_head_gradient.transpose(1, 2, 0, 3).reshape(
        sequence_count, sequence_length, KEY_VALUE_HEADS * HEAD_SIZE
    )
    key_portion, value_portion = (
        lax.psum_scatter(
            key_complete_gradient.astype(jnp.bfloat16), "ctx", scatter_dimension=1, tiled=True
        ).astype(jnp.float32),
        lax.psum_scatter(
            value_complete_gradient.astype(jnp.bfloat16), "ctx", scatter_dimension=1, tiled=True
        ).astype(jnp.float32),
    )

    def query_shape(unnormalized_rows, gain_scale_apply):
        return reshape_to_heads(unnormalized_rows, gain_scale_apply, token_positions, QUERY_HEADS)

    def key_shape(unnormalized_rows, gain_scale_apply):
        return reshape_to_heads(
            unnormalized_rows, gain_scale_apply, token_positions, KEY_VALUE_HEADS
        )

    q_raw_grad, q_gain_part = jax.vjp(query_shape, q_raw, gain_query)[1](query_grad)
    k_raw_grad, k_gain_part = jax.vjp(key_shape, key_unrotated, key_gain_name)[1](
        key_portion.reshape(token_count, KEY_VALUE_HEADS, HEAD_SIZE)
    )
    q_raw_low = q_raw_grad.astype(jnp.bfloat16)
    k_raw_low = k_raw_grad.astype(jnp.bfloat16)
    value_reduced_precision = value_portion.reshape(
        token_count, KEY_VALUE_HEADS * HEAD_SIZE
    ).astype(jnp.bfloat16)
    hidden_grad = jnp.einsum("tc,dc->td", q_raw_low, full_query, preferred_element_type=jnp.float32)
    hidden_grad = hidden_grad + jnp.einsum(
        "tc,dc->td", k_raw_low, full_key, preferred_element_type=jnp.float32
    )
    hidden_grad = hidden_grad + jnp.einsum(
        "tc,dc->td", value_reduced_precision, full_value, preferred_element_type=jnp.float32
    )
    input_part, attn_gain_part = jax.vjp(normalized_rows, resid_in, gain_attn)[1](hidden_grad)
    input_grad = (
        (resid_grad + input_part)
        .astype(jnp.bfloat16)
        .reshape(sequence_count, span_length, MODEL_WIDTH)
    )
    router_grad = jnp.einsum("td,te->de", normed, logit_grad, preferred_element_type=jnp.float32)
    out_proj_grad = jnp.einsum("tc,td->cd", mixed, attn_grad, preferred_element_type=jnp.float32)
    query_w_grad = jnp.einsum("td,tc->dc", hidden, q_raw_low, preferred_element_type=jnp.float32)
    key_w_grad = jnp.einsum("td,tc->dc", hidden, k_raw_low, preferred_element_type=jnp.float32)
    value_w_grad = jnp.einsum(
        "td,tc->dc", hidden, value_reduced_precision, preferred_element_type=jnp.float32
    )
    owned = (
        lax.psum_scatter(
            attn_gain_part.astype(jnp.bfloat16), "fsdp", scatter_dimension=0, tiled=True
        ).astype(jnp.float32),
        lax.psum_scatter(
            query_w_grad.astype(jnp.bfloat16), "fsdp", scatter_dimension=0, tiled=True
        ).astype(jnp.float32),
        lax.psum_scatter(
            key_w_grad.astype(jnp.bfloat16), "fsdp", scatter_dimension=0, tiled=True
        ).astype(jnp.float32),
        lax.psum_scatter(
            value_w_grad.astype(jnp.bfloat16), "fsdp", scatter_dimension=0, tiled=True
        ).astype(jnp.float32),
        lax.psum_scatter(
            q_gain_part.astype(jnp.bfloat16), "fsdp", scatter_dimension=0, tiled=True
        ).astype(jnp.float32),
        lax.psum_scatter(
            k_gain_part.astype(jnp.bfloat16), "fsdp", scatter_dimension=0, tiled=True
        ).astype(jnp.float32),
        lax.psum_scatter(
            out_proj_grad.astype(jnp.bfloat16), "fsdp", scatter_dimension=0, tiled=True
        ).astype(jnp.float32),
        lax.psum_scatter(
            ffn_gain_part.astype(jnp.bfloat16), "fsdp", scatter_dimension=0, tiled=True
        ).astype(jnp.float32),
        lax.psum_scatter(
            router_grad.astype(jnp.bfloat16), "fsdp", scatter_dimension=0, tiled=True
        ).astype(jnp.float32),
    )
    shares = (
        lax.psum(owned[0].astype(jnp.bfloat16), "ctx").astype(jnp.float32),
        lax.psum(owned[1].astype(jnp.bfloat16), "ctx").astype(jnp.float32),
        lax.psum(owned[2].astype(jnp.bfloat16), "ctx").astype(jnp.float32),
        lax.psum(owned[3].astype(jnp.bfloat16), "ctx").astype(jnp.float32),
        lax.psum(owned[4].astype(jnp.bfloat16), "ctx").astype(jnp.float32),
        lax.psum(owned[5].astype(jnp.bfloat16), "ctx").astype(jnp.float32),
        lax.psum(owned[6].astype(jnp.bfloat16), "ctx").astype(jnp.float32),
        lax.psum(owned[7].astype(jnp.bfloat16), "ctx").astype(jnp.float32),
        lax.psum(owned[8].astype(jnp.bfloat16), "ctx").astype(jnp.float32),
    )
    return (
        output,
        input_grad,
        shares[0],
        shares[1],
        shares[2],
        shares[3],
        shares[4],
        shares[5],
        shares[6],
        shares[7],
        shares[8],
        egate_grad[None],
        expert_up_gradient[None],
        down_grad[None],
    )


def solution(mesh):
    in_specs = (
        P("fsdp", "ctx", None),
        P("fsdp", None),
        P("fsdp", "ctx", None),
        P("fsdp", "ctx", None),
        P("fsdp"),
        P("fsdp", None),
        P("fsdp", None),
        P("fsdp", None),
        P("fsdp"),
        P("fsdp"),
        P("fsdp", None),
        P("fsdp"),
        P("fsdp", None),
        P(("ctx", "fsdp"), None, None),
        P(("ctx", "fsdp"), None, None),
        P(("ctx", "fsdp"), None, None),
        P("fsdp", "ctx", None),
    )
    out_specs = (
        P("fsdp", "ctx", None),
        P("fsdp", "ctx", None),
        P("fsdp"),
        P("fsdp", None),
        P("fsdp", None),
        P("fsdp", None),
        P("fsdp"),
        P("fsdp"),
        P("fsdp", None),
        P("fsdp"),
        P("fsdp", None),
        P(("ctx", "fsdp"), None, None),
        P(("ctx", "fsdp"), None, None),
        P(("ctx", "fsdp"), None, None),
    )
    return jax.shard_map(
        on_device, mesh=mesh, in_specs=in_specs, out_specs=out_specs, check_vma=False
    )
```

profile of v0, /device:TPU:0, one launch (start us, length us, event | category | flops | bytes accessed | tf_op | source)
XLA Modules:
  0.0 2077.9 jit_solution(5957704319187998278)
XLA Ops:
  12.4 15.2 all-reduce.11
  28.3 7.9 all-gather.1
  44.4 26.0 %all-gather.12.cloned.1.call-done = bf16[2048,512]{1,0:T(8,128)(2,1)} async-done(((bf16[256,512]{1,0:T(8,128)(2,1)}), bf16[2048,512]{1,0:T(8,128)(2,1)}) %all-gather.12.cloned.1.call-update) | async-done | bytes 2097168 | tf_op jit(solution)/shard_map/all_gather | solution.py:85
  80.6 8.8 all-gather.2
  94.8 14.6 scatter_custom_fusion.1
  110.8 8.4 scatter_custom_fusion
  123.8 8.4 all-gather.14.cloned.1.call-done
  134.5 87.7 %all-gather.10.cloned.1.call-done = bf16[2048,4096]{1,0:T(8,128)(2,1)} async-done(((bf16[256,4096]{1,0:T(8,128)(2,1)}), bf16[2048,4096]{1,0:T(8,128)(2,1)}) %all-gather.10.cloned.1.call-update) | async-done | bytes 16777232 | tf_op jit(solution)/shard_map/all_gather | solution.py:84
  222.2 22.1 %copy.83 = bf16[4096,2048]{1,0:T(8,128)(2,1)} copy(bf16[4096,2048]{0,1:T(8,128)(2,1)} %bitcast.347) | data formatting | bytes 33554432 | tf_op jit(solution)/shard_map/dot_general | solution.py:113
  244.3 8.9 multiply_reduce_fusion.3
  267.8 54.8 %while.28 = (s32[]{:T(128)}, bf16[4,1,8,256,128]{3,4,2,0,1:T(8,128)(2,1)}, f32[4,1,8,256,1]{3,2,4,1,0:T(8,128)}, bf16[4,1,8,256,128]{4,3,2,1,0:T(8,128)(2,1)}, b...) while((s32[]{:T(128)}, ...), condition=%wide.region_6.7_spmd.clone, body=%wide.region_3.6_spmd.clone.sunk | while | flops 1097332736 | bytes 29956208 | solution.py:161
  322.7 11.2 multiply_reduce_fusion.6
  336.5 21.5 %gather_fusion = bf16[2560,2048]{1,0:T(8,128)(2,1)} fusion(bf16[256,2048]{1,0:T(8,128)(2,1)} %multiply_convert_fusion.5, s32[3072]{0:T(1024)S(1)} %pad_clamp_fusion), kind=kCustom, calls=%fused_computation | custom fusion | bytes 20981760 | tf_op jit(solution)/shard_map/gather | solution.py:187
  358.0 10.1 broadcast_multiply_fusion
  377.0 21.3 %gather_fusion.2 = f32[2560,2048]{1,0:T(8,128)} fusion(f32[256,2048]{1,0:T(8,128)} %bitcast_convert_fusion, s32[3072]{0:T(1024)S(1)} %pad_clamp_fusion), kind=kCustom, calls=%fused_computation.2 | custom fusion | bytes 41953280 | tf_op jit(solution)/shard_map/gather | solution.py:210
  398.3 49.9 %all_gather.43 = bf16[2048,32]{0,1:T(8,128)(2,1)S(1)} all-gather(bf16[256,32]{0,1:T(8,128)(2,1)S(1)} %copy-done.57), channel_id=1, replica_groups=mesh['ctx'=4,'fsdp'=8] {'fsdp'}, dimensions={0}, use_global_device_ids=true | all-gather | bytes 147456 | tf_op jit(solution)/shard_map/all_gather | solution.py:91
  450.5 16.8 gather_fusion.4
  469.1 8.2 scatter_custom_fusion.2
  477.4 12.2 multiply_convert_fusion.1
  489.6 115.6 %all-to-all-done = bf16[32,80,2048]{2,1,0:T(8,128)(2,1)} async-done(((bf16[32,80,2048]{2,1,0:T(8,128)(2,1)}), bf16[32,80,2048]{2,1,0:T(8,128)(2,1)}, u32[]{:S(2)}, u32[]{:S(2)}) %all-to-all-start) | async-done | bytes 10485792 | tf_op jit(solution)/shard_map/all_to_all | solution.py:50
  609.2 14.0 fusion.68
  623.2 13.0 fusion.72
  636.2 205.5 %all-to-all-done.2 = bf16[32,80,2048]{2,1,0:T(8,128)(2,1)} async-done(((bf16[32,80,2048]{2,1,0:T(8,128)(2,1)}), bf16[32,80,2048]{2,1,0:T(8,128)(2,1)}, u32[]{:S(2)}, u32[]{:S(2)}) %all-to-all-start.2) | async-done | bytes 10485792 | tf_op jit(solution)/shard_map/all_to_all | solution.py:50
  841.7 19.9 multiply_convert_fusion.2
  861.5 13.3 convolution_convert_fusion.2
  878.9 13.5 fusion.70
  892.4 16.6 add_convert_fusion
  909.0 202.3 %all-to-all-done.1 = bf16[32,80,2048]{2,1,0:T(8,128)(2,1)} async-done(((bf16[32,80,2048]{2,1,0:T(8,128)(2,1)}), bf16[32,80,2048]{2,1,0:T(8,128)(2,1)}, u32[]{:S(2)}, u32[]{:S(2)}) %all-to-all-start.1) | async-done | bytes 10485792 | tf_op jit(solution)/shard_map/all_to_all | solution.py:50
  1115.5 22.1 %gather_fusion.1 = bf16[2048,2048]{1,0:T(8,128)(2,1)} fusion(bf16[2560,2048]{1,0:T(8,128)(2,1)} %bitcast.32, s32[2048]{0:T(1024)S(1)} %broadcast_clamp_fusion), kind=kCustom, calls=%fused_computation.1 | custom fusion | bytes 16785408 | tf_op jit(solution)/shard_map/gather | solution.py:199
  1137.7 8.7 fusion.61
  1154.1 193.5 %all-to-all-done.3 = bf16[32,80,2048]{2,1,0:T(8,128)(2,1)} async-done(((bf16[32,80,2048]{2,1,0:T(8,128)(2,1)}), bf16[32,80,2048]{2,1,0:T(8,128)(2,1)}, u32[]{:S(2)}, u32[]{:S(2)}) %all-to-all-start.3) | async-done | bytes 10485792 | tf_op jit(solution)/shard_map/all_to_all | solution.py:50
  1347.6 21.8 %gather_fusion.3 = bf16[2048,2048]{1,0:T(8,128)(2,1)} fusion(bf16[2560,2048]{1,0:T(8,128)(2,1)} %bitcast.42, s32[2048]{0:T(1024)S(1)} %broadcast_clamp_fusion), kind=kCustom, calls=%fused_computation.3 | custom fusion | bytes 16785408 | tf_op jit(solution)/shard_map/gather | solution.py:239
  1380.8 12.3 fusion.92
  1397.4 71.0 %while.29 = (s32[]{:T(128)}, f32[4,1,8,256,128]{4,3,2,1,0:T(8,128)}, bf16[4,1,1024,128]{2,3,0,1:T(8,128)(2,1)}, bf16[4,1,1024,128]{2,3,0,1:T(8,128)(2,1)}, bf16[...) while((s32[]{:T(128)}, ...), condition=%wide.region_20.21_spmd.clone, body=%wide.region_18.20_spmd.clone.sunk | while | flops 2716596224 | bytes 86574304 | solution.py:280
  1469.3 22.3 %reduce-scatter.10.cloned.1.call-done = bf16[1,256,512]{1,2,0:T(8,128)(2,1)} async-done(((bf16[1,1024,512]{1,2,0:T(8,128)(2,1)}), bf16[1,256,512]{1,2,0:T(8,128)(2,1)}) %reduce-scatter.10.cloned.1.call-update) | async-done | bytes 262160 | tf_op jit(solution)/shard_map/reduce_scatter | solution.py:297
  1494.9 24.9 %reduce-scatter.8.cloned.1.call-done = bf16[1,256,512]{1,2,0:T(8,128)(2,1)} async-done(((bf16[1,1024,512]{1,2,0:T(8,128)(2,1)}), bf16[1,256,512]{1,2,0:T(8,128)(2,1)}) %reduce-scatter.8.cloned.1.call-update) | async-done | bytes 262160 | tf_op jit(solution)/shard_map/reduce_scatter | solution.py:294
  1523.5 12.9 convolution_convert_fusion
  1550.2 10.1 convolution_convert_fusion.1
  1561.6 14.3 convolution_bitcast_fusion.2
  1577.2 14.4 convolution_bitcast_fusion.3
  1591.6 16.1 reduce-scatter.14.cloned.1.call-done
  1607.7 119.6 %reduce-scatter.18.cloned.1.call-done = bf16[512,2048]{1,0:T(8,128)(2,1)} async-done(((bf16[4096,2048]{1,0:T(8,128)(2,1)}), bf16[512,2048]{1,0:T(8,128)(2,1)}) %reduce-scatter.18.cloned.1.call-update) | async-done | bytes 2097168 | tf_op jit(solution)/shard_map/reduce_scatter | solution.py:358
  1727.3 119.4 %reduce-scatter.12.cloned.1.call-done = bf16[256,4096]{1,0:T(8,128)(2,1)} async-done(((bf16[2048,4096]{1,0:T(8,128)(2,1)}), bf16[256,4096]{1,0:T(8,128)(2,1)}) %reduce-scatter.12.cloned.1.call-update) | async-done | bytes 2097168 | tf_op jit(solution)/shard_map/reduce_scatter | solution.py:343
  1846.7 14.2 convolution_bitcast_fusion.1
  1860.9 12.3 fusion.143
  1878.9 13.3 all-reduce.10
  1892.5 20.0 all-reduce.12
  1919.2 141.1 %all-reduce.16.cloned.1.call-done = (bf16[256,4096]{1,0:T(8,128)(2,1)}, bf16[256,512]{1,0:T(8,128)(2,1)}, bf16[256,512]{1,0:T(8,128)(2,1)}, bf16[512,2048]{1,0:T(8,128)(2,1)}) async-done(((bf16[256,4096]{1,0:T(8,128)(2,1)}, bf16[256,512]{1,0:T(8,128)(2,1)}, bf16[256,512]{1,0:T(8,128)(2,1)}, bf16[512,2048]{1,0:T(8,128)(2,1)}), (bf16[256,4096]{1,0:T(8,128)(2,1)}, bf16[256,512]{1,0:T(8,128)(2,1)}, ...) | async-done | bytes 4718608 | tf_op jit(solution)/shard_map/psum | solution.py:370
  (396 shorter events, 273.1 us)
Async XLA Ops:
  7.2 834.5 %copy-start = (bf16[1,768,2048]{2,1,0:T(8,128)(2,1)S(1)}, bf16[1,768,2048]{2,1,0:T(8,128)(2,1)}, u32[]{:S(2)}) copy-start(bf16[1,768,2048]{2,1,0:T(8,128)(2,1)} %param.36) | copy-start | bytes 9437188
  7.2 33.4 %all-gather.16.cloned.1.call-start = ((), (), s32[]{:S(2)}) async-start(), calls=%async_computation.14 | async-start | bytes 2359296 | tf_op jit(solution)/shard_map/all_gather | solution.py:86
  7.9 62.5 %all-gather.12.cloned.1.call-start = ((), (), s32[]{:S(2)}) async-start(), calls=%async_computation.12 | async-start | bytes 2359296 | tf_op jit(solution)/shard_map/all_gather | solution.py:85
  8.7 110.6 %all-gather.20.cloned.1.call-start = ((), (), s32[]{:S(2)}) async-start(), calls=%async_computation.23 | async-start | bytes 1310720 | tf_op jit(solution)/shard_map/all_gather | solution.py:129
  27.7 50.0 %copy-start.68 = (f32[128]{0:T(128)}, f32[128]{0:T(128)S(1)}, u32[]{:S(2)}) copy-start(f32[128]{0:T(128)S(1)} %convert_element_type.283) | copy-start | bytes 1540
  36.2 38.1 %copy-start.31 = (f32[8,1,256]{2,1,0:T(1,128)}, f32[8,1,256]{2,1,0:T(1,128)S(1)}, u32[]{:S(2)}) copy-start(f32[8,1,256]{2,1,0:T(1,128)S(1)} %convert_element_type.334) | copy-start | bytes 24580
  37.7 36.6 %copy-start.63 = (f32[256]{0:T(256)}, f32[256]{0:T(256)S(1)}, u32[]{:S(2)}) copy-start(f32[256]{0:T(256)S(1)} %fusion.83) | copy-start | bytes 3076
  37.8 206.5 %copy-start.49 = (f32[256]{0:T(256)}, f32[256]{0:T(256)S(1)}, u32[]{:S(2)}) copy-start(f32[256]{0:T(256)S(1)} %fusion.133) | copy-start | bytes 3076
  44.0 88.2 %all-gather.14.cloned.1.call-start = ((), (), s32[]{:S(2)}) async-start(), calls=%async_computation.13 | async-start | bytes 1310720 | tf_op jit(solution)/shard_map/all_gather | solution.py:128
  44.4 209.5 %copy-start.16 = (f32[256,64]{0,1:T(8,128)}, f32[256,64]{0,1:T(8,128)S(1)}, u32[]{:S(2)}) copy-start(f32[256,64]{0,1:T(8,128)S(1)} %get-tuple-element.300) | copy-start | bytes 196612
  44.4 209.5 %copy-start.18 = (f32[256,64]{0,1:T(8,128)}, f32[256,64]{0,1:T(8,128)S(1)}, u32[]{:S(2)}) copy-start(f32[256,64]{0,1:T(8,128)S(1)} %get-tuple-element.301) | copy-start | bytes 196612
  77.1 13.0 copy-start.74
  77.9 41.3 %copy-start.29 = (s32[1,1024]{1,0:T(1,128)S(1)}, s32[1,1024]{1,0:T(1,128)}, u32[]{:S(2)}) copy-start(s32[1,1024]{1,0:T(1,128)} %param.22) | copy-start | bytes 12292
  78.8 143.3 %all-gather.10.cloned.1.call-start = ((), (), s32[]{:S(2)}) async-start(), calls=%async_computation.11 | async-start | bytes 18874368 | tf_op jit(solution)/shard_map/all_gather | solution.py:84
  79.4 243.3 %all-gather.18.cloned.1.call-start = ((), (), s32[]{:S(2)}) async-start(), calls=%async_computation.15 | async-start | bytes 18874368 | tf_op jit(solution)/shard_map/all_gather | solution.py:89
  94.8 14.6 copy-start.67
  222.2 22.1 %copy-start.32 = (f32[8,1,256]{2,1,0:T(1,128)S(1)}, f32[8,1,256]{2,1,0:T(1,128)}, u32[]{:S(2)}) copy-start(f32[8,1,256]{2,1,0:T(1,128)} %copy-done.31) | copy-start | bytes 24580
  333.9 24.1 %copy-start.65 = (f32[256]{0:T(256)}, f32[256]{0:T(256)S(1)}, u32[]{:S(2)}) copy-start(f32[256]{0:T(256)S(1)} %get-tuple-element.308) | copy-start | bytes 3076
  334.0 24.0 %copy-start.61 = (f32[256]{0:T(256)}, f32[256]{0:T(256)S(1)}, u32[]{:S(2)}) copy-start(f32[256]{0:T(256)S(1)} %fusion.134) | copy-start | bytes 3076
  336.5 21.5 %copy-start.53 = (bf16[32,80]{1,0:T(8,128)(2,1)S(1)}, bf16[32,80]{1,0:T(8,128)(2,1)}, u32[]{:S(2)}) copy-start(bf16[32,80]{1,0:T(8,128)(2,1)} %mul.564) | copy-start | bytes 15364
  368.1 237.2 %all-to-all-start = ((bf16[32,80,2048]{2,1,0:T(8,128)(2,1)}), bf16[32,80,2048]{2,1,0:T(8,128)(2,1)}, u32[]{:S(2)}, u32[]{:S(2)}) async-start(bf16[32,80,2048]{2,1,0:T(8,128)(2,1)} %broadcast_multiply_fusion), calls=%async_computation | async-start | bytes 20971520 | tf_op jit(solution)/shard_map/all_to_all | solution.py:50
  377.0 21.3 %copy-start.57 = (bf16[256,32]{0,1:T(8,128)(2,1)S(1)}, bf16[256,32]{0,1:T(8,128)(2,1)}, u32[]{:S(2)}) copy-start(bf16[256,32]{0,1:T(8,128)(2,1)} %param.33) | copy-start | bytes 49156
  605.3 236.4 %all-to-all-start.2 = ((bf16[32,80,2048]{2,1,0:T(8,128)(2,1)}), bf16[32,80,2048]{2,1,0:T(8,128)(2,1)}, u32[]{:S(2)}, u32[]{:S(2)}) async-start(bf16[32,80,2048]{2,1,0:T(8,128)(2,1)} %multiply_convert_fusion.1), calls=%async_computation.2 | async-start | bytes 20971520 | tf_op jit(solution)/shard_map/all_to_all | solution.py:50
  609.2 14.0 copy-start.72
  874.8 236.5 %all-to-all-start.1 = ((bf16[32,80,2048]{2,1,0:T(8,128)(2,1)}), bf16[32,80,2048]{2,1,0:T(8,128)(2,1)}, u32[]{:S(2)}, u32[]{:S(2)}) async-start(bf16[32,80,2048]{2,1,0:T(8,128)(2,1)} %bitcast.354), calls=%async_computation.1 | async-start | bytes 20971520 | tf_op jit(solution)/shard_map/all_to_all | solution.py:50
  1111.3 236.3 %all-to-all-start.3 = ((bf16[32,80,2048]{2,1,0:T(8,128)(2,1)}), bf16[32,80,2048]{2,1,0:T(8,128)(2,1)}, u32[]{:S(2)}, u32[]{:S(2)}) async-start(bf16[32,80,2048]{2,1,0:T(8,128)(2,1)} %bitcast.353), calls=%async_computation.3 | async-start | bytes 20971520 | tf_op jit(solution)/shard_map/all_to_all | solution.py:50
  1115.2 376.4 %reduce-scatter.10.cloned.1.call-start = ((), (), s32[]{:S(2)}) async-start(), calls=%async_computation.17 | async-start | bytes 1310720 | tf_op jit(solution)/shard_map/reduce_scatter | solution.py:297
  1115.5 22.2 %copy-start.13 = (bf16[1,256,2048]{2,1,0:T(8,128)(2,1)S(1)}, bf16[1,256,2048]{2,1,0:T(8,128)(2,1)}, u32[]{:S(2)}) copy-start(bf16[1,256,2048]{2,1,0:T(8,128)(2,1)} %param.37) | copy-start | bytes 3145732
  1147.1 228.3 %copy-start.36 = (bf16[256,32]{0,1:T(8,128)(2,1)}, bf16[256,32]{0,1:T(8,128)(2,1)S(1)}, u32[]{:S(2)}) copy-start(bf16[256,32]{0,1:T(8,128)(2,1)S(1)} %select_reduce_fusion) | copy-start | bytes 49156
  1397.4 94.2 %copy-start.3 = (bf16[1,256,2048]{2,1,0:T(8,128)(2,1)S(1)}, bf16[1,256,2048]{2,1,0:T(8,128)(2,1)}, u32[]{:S(2)}) copy-start(bf16[1,256,2048]{2,1,0:T(8,128)(2,1)} %param.21) | copy-start | bytes 3145732
  1397.4 94.2 %copy-start.33 = (f32[8,1,256]{2,1,0:T(1,128)S(1)}, f32[8,1,256]{2,1,0:T(1,128)}, u32[]{:S(2)}) copy-start(f32[8,1,256]{2,1,0:T(1,128)} %copy-done.31) | copy-start | bytes 24580
  1397.4 94.1 %copy-start.50 = (f32[256]{0:T(256)S(1)}, f32[256]{0:T(256)}, u32[]{:S(2)}) copy-start(f32[256]{0:T(256)} %copy-done.49) | copy-start | bytes 3076
  1468.4 52.4 %copy-start.17 = (f32[256,64]{0,1:T(8,128)S(1)}, f32[256,64]{0,1:T(8,128)}, u32[]{:S(2)}) copy-start(f32[256,64]{0,1:T(8,128)} %copy-done.16) | copy-start | bytes 196612
  1468.4 52.4 %copy-start.19 = (f32[256,64]{0,1:T(8,128)S(1)}, f32[256,64]{0,1:T(8,128)}, u32[]{:S(2)}) copy-start(f32[256,64]{0,1:T(8,128)} %copy-done.18) | copy-start | bytes 196612
  1468.4 51.4 %reduce-scatter.8.cloned.1.call-start = ((), (), s32[]{:S(2)}) async-start(), calls=%async_computation.16 | async-start | bytes 1310720 | tf_op jit(solution)/shard_map/reduce_scatter | solution.py:294
  1469.2 51.7 %copy-start.12 = (f32[256,4,128]{0,2,1:T(8,128)S(1)}, f32[256,4,128]{0,2,1:T(8,128)}, u32[]{:S(2)}) copy-start(f32[256,4,128]{0,2,1:T(8,128)} %copy-done.11) | copy-start | bytes 1572868
  1469.2 51.7 %copy-start.48 = (f32[256,4]{0,1:T(4,128)S(1)}, f32[256,4]{0,1:T(4,128)}, u32[]{:S(2)}) copy-start(f32[256,4]{0,1:T(4,128)} %copy-done.47) | copy-start | bytes 12292
  1469.2 51.7 %copy-start.69 = (f32[128]{0:T(128)S(1)}, f32[128]{0:T(128)}, u32[]{:S(2)}) copy-start(f32[128]{0:T(128)} %copy-done.68) | copy-start | bytes 1540
  1469.2 51.9 %copy-start.59 = (f32[256,4]{0,1:T(4,128)S(1)}, f32[256,4]{0,1:T(4,128)}, u32[]{:S(2)}) copy-start(f32[256,4]{0,1:T(4,128)} %copy-done.58) | copy-start | bytes 12292
  1469.2 122.3 %reduce-scatter.16.cloned.1.call-start = ((), (), s32[]{:S(2)}) async-start(), calls=%async_computation.20 | async-start | bytes 2359296 | tf_op jit(solution)/shard_map/reduce_scatter | solution.py:349
  1494.9 112.8 %reduce-scatter.14.cloned.1.call-start = ((), (), s32[]{:S(2)}) async-start(), calls=%async_computation.19 | async-start | bytes 2359296 | tf_op jit(solution)/shard_map/reduce_scatter | solution.py:346
  1523.4 203.9 %reduce-scatter.18.cloned.1.call-start = ((), (), s32[]{:S(2)}) async-start(), calls=%async_computation.21 | async-start | bytes 18874368 | tf_op jit(solution)/shard_map/reduce_scatter | solution.py:358
  1536.4 310.4 %reduce-scatter.12.cloned.1.call-start = ((), (), s32[]{:S(2)}) async-start(), calls=%async_computation.18 | async-start | bytes 18874368 | tf_op jit(solution)/shard_map/reduce_scatter | solution.py:343
  1560.3 332.2 %reduce-scatter.20.cloned.1.call-start = ((), (), s32[]{:S(2)}) async-start(), calls=%async_computation.22 | async-start | bytes 147456 | tf_op jit(solution)/shard_map/reduce_scatter | solution.py:364
  1561.6 14.3 copy-start.2
  1561.6 14.3 copy-start.37
  1576.9 483.4 %all-reduce.16.cloned.1.call-start = ((), (), s32[]{:S(2)}) async-start(), calls=%async_computation.24 | async-start | bytes 9437184 | tf_op jit(solution)/shard_map/psum | solution.py:370
  1876.4 38.9 %copy-start.64 = (f32[256]{0:T(256)S(1)}, f32[256]{0:T(256)}, u32[]{:S(2)}) copy-start(f32[256]{0:T(256)} %copy-done.63) | copy-start | bytes 3076
  (55 other events, 244.5 us)
Sparse Core Ops, SparseCore 0:
  9.9 30.6 all-gather.15
  42.5 27.8 all-gather.11
  72.6 27.9 all-gather.19
  102.5 29.6 all-gather.13
  134.0 88.1 all-gather.9
  223.9 89.8 all-gather.17
  1468.5 22.9 reduce-scatter.9
  1494.0 25.7 reduce-scatter.7
  1523.1 39.8 reduce-scatter.15
  1566.5 41.2 reduce-scatter.13
  1611.3 115.9 reduce-scatter.17
  1730.7 115.9 reduce-scatter.11
  1850.3 33.3 reduce-scatter.19
  1886.3 173.9 all-reduce.15
where the time goes:
time: 2090 us; the launch traced here: 2080 us
  waiting for transfers between devices  1290 us (62%)
  matrix products  325 us (16%)
  local copies, waits for them, and re-layouts  220 us (11%)
  blocking collectives  115 us (6%)
  other arithmetic  92.7 us (4%)
    all_to_all x4, waiting for transfers between devices, route_rows(): lax.all_to_all(buffer, ('ctx', 'fsdp'), split_axis=0, concat_axis=0, tile...  717 us
    psum x1, waiting for transfers between devices, on_device(): lax.psum(owned[1].astype(jnp.bfloat16), 'ctx').astype(jnp.float32)  141 us
    reduce_scatter x1, waiting for transfers between devices, on_device(): lax.psum_scatter(out_proj_grad.astype(jnp.bfloat16), 'fsdp', scatter_dime...  120 us
    reduce_scatter x1, waiting for transfers between devices, on_device(): lax.psum_scatter(query_w_grad.astype(jnp.bfloat16), 'fsdp', scatter_dimen...  119 us
    all_gather x1, waiting for transfers between devices, on_device(): lax.all_gather(w_query, 'fsdp', axis=0, tiled=True)  87.7 us
    all_gather x1, blocking collectives, on_device(): lax.all_gather(w_router, 'fsdp', axis=0, tiled=True)  49.9 us
  transfers between devices with their start and end apart: 18, of which 14 were waited for; matrix products, arithmetic and copies ran while one was open for 20% of the time, Pallas kernels for 0%

commit v1 on v0

v1 whole, which is shorter than its diff:
```python
import functools

import jax
import jax.numpy as jnp
from jax import lax
from jax.experimental import pallas as pl
from jax.experimental.pallas import tpu as pltpu
from jax.sharding import PartitionSpec as P

QUERY_HEADS = 32
KEY_VALUE_HEADS = 4
HEAD_SIZE = 128
TOP = 8

EPSILON = 1e-06
ROPE_BASE = 1000000.0
MASKED = -1000000000.0
SCALE = HEAD_SIZE ** (-0.5)
HALF = HEAD_SIZE // 2
BF = jnp.bfloat16
F32 = jnp.float32


def nt(a, b):
    return lax.dot_general(a, b, (((1,), (1,)), ((), ())), preferred_element_type=F32)


def nn(a, b):
    return lax.dot_general(a, b, (((1,), (0,)), ((), ())), preferred_element_type=F32)


def tn(a, b):
    return lax.dot_general(a, b, (((0,), (0,)), ((), ())), preferred_element_type=F32)


def inverse_rms(values):
    return lax.rsqrt(jnp.mean(values * values, axis=-1, keepdims=True) + EPSILON)


def norm_rope(raw, gain, cosine, sine):
    z = raw * inverse_rms(raw) * gain
    return z * cosine + pltpu.roll(z, HALF, 1) * sine


def norm_rope_back(raw, gain, cosine, sine, grad):
    dz = grad * cosine - pltpu.roll(grad, HALF, 1) * sine
    r = inverse_rms(raw)
    n = dz * gain
    d_raw = r * n - raw * (r * r * r) * jnp.mean(n * raw, axis=-1, keepdims=True)
    return d_raw, jnp.sum(dz * raw * r, axis=0, keepdims=True)


def attention_forward(
    q_ref, k_ref, v_ref, cos_ref, sin_ref, gains_ref, own_ref, key_ref, mixed_ref, total_ref, keys, values_t
):
    cosine, sine = cos_ref[...], sin_ref[...]

    @pl.when(pl.program_id(0) == 0)
    def _():
        keys[...] = norm_rope(k_ref[...], gains_ref[1:2, :], cosine, sine).astype(BF)
        values_t[...] = v_ref[...].T.astype(BF)

    queries = norm_rope(q_ref[...], gains_ref[0:1, :], cosine, sine).astype(BF)
    length = queries.shape[0]
    chunk = 256
    for start in range(0, length, chunk):
        scores = nt(keys[...], queries[start : start + chunk]) * SCALE
        seen = key_ref[...] <= own_ref[0:1, start : start + chunk]
        scores = jnp.where(seen, scores, MASKED)
        top = jnp.max(scores, axis=0, keepdims=True)
        weights = jnp.exp(scores - top)
        total = jnp.sum(weights, axis=0, keepdims=True)
        out = nn(values_t[...], weights.astype(BF)) / total
        mixed_ref[start : start + chunk, :] = out.T.astype(BF)
        total_ref[0, :, start : start + chunk] = jnp.broadcast_to(top + jnp.log(total), (8, chunk))


def attention_backward(
    heads,
    q_ref,
    k_ref,
    v_ref,
    grad_ref,
    total_ref,
    cos_ref,
    sin_ref,
    gains_ref,
    own_ref,
    key_ref,
    dq_ref,
    dkv_ref,
    dgain_ref,
    keys,
    keys_t,
    values,
    dk,
    dv,
):
    cosine, sine = cos_ref[...], sin_ref[...]
    head = pl.program_id(0)

    @pl.when(head == 0)
    def _():
        rotated = norm_rope(k_ref[...], gains_ref[1:2, :], cosine, sine)
        keys[...] = rotated.astype(BF)
        keys_t[...] = rotated.T.astype(BF)
        values[...] = v_ref[...].astype(BF)
        dk[...] = jnp.zeros_like(dk)
        dv[...] = jnp.zeros_like(dv)
        dgain_ref[...] = jnp.zeros_like(dgain_ref)

    queries = norm_rope(q_ref[...], gains_ref[0:1, :], cosine, sine).astype(BF)
    length = queries.shape[0]
    chunk = 256
    for start in range(0, length, chunk):
        rows = slice(start, start + chunk)
        q_part = queries[rows]
        grad = grad_ref[rows, :]
        scores = nt(keys[...], q_part) * SCALE
        seen = key_ref[...] <= own_ref[0:1, rows]
        scores = jnp.where(seen, scores, MASKED)
        weights = jnp.exp(scores - total_ref[0, 0:1, rows])
        d_weights = nt(values[...], grad)
        row_dot = jnp.sum(weights * d_weights, axis=0, keepdims=True)
        d_scores = (weights * (d_weights - row_dot)).astype(BF)
        dv[...] += nn(weights.astype(BF), grad)
        dk[...] += nn(d_scores, q_part)
        d_queries = nn(keys_t[...], d_scores).T * SCALE
        d_raw, d_gain = norm_rope_back(
            q_ref[rows, :], gains_ref[0:1, :], cos_ref[rows, :], sin_ref[rows, :], d_queries
        )
        dq_ref[rows, :] = d_raw.astype(BF)
        dgain_ref[0:1, :] += d_gain

    @pl.when(head == heads - 1)
    def _():
        d_raw, d_gain = norm_rope_back(
            k_ref[...], gains_ref[1:2, :], cosine, sine, dk[...] * SCALE
        )
        dkv_ref[:, :HEAD_SIZE] = d_raw.astype(BF)
        dkv_ref[:, HEAD_SIZE:] = dv[...].astype(BF)
        dgain_ref[1:2, :] = d_gain


def attention_specs(heads, length):
    whole = lambda shape: pl.BlockSpec(shape, lambda h: (0,) * len(shape))
    column = lambda at: pl.BlockSpec((length, HEAD_SIZE), lambda h: (0, at))
    head_column = pl.BlockSpec((length, HEAD_SIZE), lambda h: (0, h))
    totals = pl.BlockSpec((1, 8, length), lambda h: (h, 0, 0))
    shared = [
        whole((length, HEAD_SIZE)),
        whole((length, HEAD_SIZE)),
        whole((8, HEAD_SIZE)),
        whole((8, length)),
        whole((length, 1)),
    ]
    return whole, column, head_column, totals, shared


def run_attention(qkv, heads, cosine, sine, gains, own, key_blocks):
    length = qkv.shape[0]
    whole, column, head_column, totals, shared = attention_specs(heads, length)
    return pl.pallas_call(
        attention_forward,
        grid=(heads,),
        in_specs=[head_column, column(heads), column(heads + 1)] + shared,
        out_specs=[head_column, totals],
        out_shape=[
            jax.ShapeDtypeStruct((length, heads * HEAD_SIZE), BF),
            jax.ShapeDtypeStruct((heads, 8, length), F32),
        ],
        scratch_shapes=[
            pltpu.VMEM((length, HEAD_SIZE), BF),
            pltpu.VMEM((HEAD_SIZE, length), BF),
        ],
        compiler_params=pltpu.CompilerParams(vmem_limit_bytes=48 * 2**20),
        cost_estimate=pl.CostEstimate(
            flops=4 * heads * length * length * HEAD_SIZE,
            bytes_accessed=8 * heads * length * HEAD_SIZE,
            transcendentals=heads * length * length,
        ),
    )(qkv, qkv, qkv, cosine, sine, gains, own, key_blocks)


def run_attention_back(qkv, grad, totals_in, heads, cosine, sine, gains, own, key_blocks):
    length = qkv.shape[0]
    whole, column, head_column, totals, shared = attention_specs(heads, length)
    return pl.pallas_call(
        functools.partial(attention_backward, heads),
        grid=(heads,),
        in_specs=[head_column, column(heads), column(heads + 1), head_column, totals] + shared,
        out_specs=[head_column, whole((length, 2 * HEAD_SIZE)), whole((8, HEAD_SIZE))],
        out_shape=[
            jax.ShapeDtypeStruct((length, heads * HEAD_SIZE), BF),
            jax.ShapeDtypeStruct((length, 2 * HEAD_SIZE), BF),
            jax.ShapeDtypeStruct((8, HEAD_SIZE), F32),
        ],
        scratch_shapes=[
            pltpu.VMEM((length, HEAD_SIZE), BF),
            pltpu.VMEM((HEAD_SIZE, length), BF),
            pltpu.VMEM((length, HEAD_SIZE), BF),
            pltpu.VMEM((length, HEAD_SIZE), F32),
            pltpu.VMEM((length, HEAD_SIZE), F32),
        ],
        compiler_params=pltpu.CompilerParams(vmem_limit_bytes=48 * 2**20),
        cost_estimate=pl.CostEstimate(
            flops=10 * heads * length * length * HEAD_SIZE,
            bytes_accessed=10 * heads * length * HEAD_SIZE,
            transcendentals=heads * length * length,
        ),
    )(qkv, qkv, qkv, grad, totals_in, cosine, sine, gains, own, key_blocks)


def push(source, target, sends, recvs, device):
    copy = pltpu.make_async_remote_copy(
        src_ref=source,
        dst_ref=target,
        send_sem=sends,
        recv_sem=recvs,
        device_id=device,
        device_id_type=pl.DeviceIdType.MESH,
    )
    return copy


def greet(devices):
    barrier = pltpu.get_barrier_semaphore()
    for device in devices:
        pl.semaphore_signal(barrier, 1, device_id=device, device_id_type=pl.DeviceIdType.MESH)
    pl.semaphore_wait(barrier, len(devices))


def line_gather(n_ctx, ctx, fsdp, own_ref, all_ref, up, down, arrived):
    def hop(block, step, sems, to):
        def start(source):
            push(source, all_ref.at[block], sems.at[step], arrived.at[block], (to, fsdp)).start()

        if step == 0:
            start(own_ref)
        else:
            push(
                all_ref.at[block], all_ref.at[block], sems.at[step], arrived.at[block], (to, fsdp)
            ).wait_recv()
            start(all_ref.at[block])

    for step in range(n_ctx - 1):

        @pl.when((ctx - step >= 0) & (ctx < n_ctx - 1))
        def _():
            hop(ctx - step, step, up, ctx + 1)

        @pl.when((ctx + step < n_ctx) & (ctx > 0))
        def _():
            hop(ctx + step, step, down, ctx - 1)

    def finish(block):
        push(own_ref, all_ref.at[block], up.at[0], arrived.at[block], (ctx, fsdp)).wait_recv()

    for other in range(1, n_ctx):

        @pl.when(ctx == n_ctx - 1)
        def _():
            finish(n_ctx - 1 - other)

        @pl.when(ctx == 0)
        def _():
            finish(other)

    for step in range(n_ctx - 1):

        @pl.when((ctx - step >= 0) & (ctx < n_ctx - 1))
        def _():
            push(own_ref, all_ref.at[0], up.at[step], arrived.at[0], (ctx, fsdp)).wait_send()

        @pl.when((ctx + step < n_ctx) & (ctx > 0))
        def _():
            push(own_ref, all_ref.at[0], down.at[step], arrived.at[0], (ctx, fsdp)).wait_send()


def first_gather(
    n_ctx,
    n_fsdp,
    x_ref,
    table_ref,
    packed_ref,
    x_all,
    table_all,
    packed_all,
    local,
    up,
    down,
    arrived,
    table_send,
    table_arrived,
    packed_send,
    passed_send,
    packed_arrived,
):
    ctx, fsdp = lax.axis_index("ctx"), lax.axis_index("fsdp")
    sibling = lax.rem(fsdp + 1, 2) + (fsdp // 2) * 2
    chips = n_fsdp // 2

    def same_core(offset):
        return lax.rem(fsdp + 2 * offset, n_fsdp)

    def along(offset):
        return lax.rem(ctx + offset, n_ctx)

    greet(
        [(along(i), fsdp) for i in range(1, n_ctx)]
        + [(ctx, same_core(i)) for i in range(1, chips)]
        + [(ctx, sibling)]
    )
    kept = [
        pltpu.make_async_copy(x_ref, x_all.at[ctx], local.at[0]),
        pltpu.make_async_copy(table_ref, table_all.at[ctx], local.at[1]),
        pltpu.make_async_copy(packed_ref, packed_all.at[fsdp], local.at[2]),
    ]
    for copy in kept:
        copy.start()

    def packed_copy(source, owner, sems, to):
        return push(source, packed_all.at[owner], sems, packed_arrived.at[owner], (ctx, to))

    for i in range(1, chips):
        packed_copy(packed_ref, fsdp, packed_send.at[i], same_core(i)).start()
    packed_copy(packed_ref, fsdp, packed_send.at[0], sibling).start()
    for i in range(1, n_ctx):
        push(
            table_ref, table_all.at[ctx], table_send.at[i], table_arrived.at[ctx], (along(i), fsdp)
        ).start()
    line_gather(n_ctx, ctx, fsdp, x_ref, x_all, up, down, arrived)
    for i in range(1, chips):
        owner = same_core(chips - i)
        packed_copy(packed_ref, owner, packed_send.at[i], sibling).wait_recv()
        packed_copy(packed_all.at[owner], owner, passed_send.at[i], sibling).start()
    for i in range(chips):
        owner = lax.rem(sibling + 2 * i, n_fsdp)
        packed_copy(packed_ref, owner, packed_send.at[0], sibling).wait_recv()
    for i in range(1, n_ctx):
        owner = along(i)
        push(
            table_ref, table_all.at[owner], table_send.at[i], table_arrived.at[owner], (owner, fsdp)
        ).wait()
    for i in range(chips):
        packed_copy(packed_ref, fsdp, packed_send.at[i], sibling).wait_send()
    for i in range(1, chips):
        packed_copy(packed_ref, fsdp, passed_send.at[i], sibling).wait_send()
    for copy in kept:
        copy.wait()


def run_first_gather(n_ctx, n_fsdp, x, table, packed):
    anywhere = pl.BlockSpec(memory_space=pl.ANY)
    dma = pltpu.SemaphoreType.DMA
    return pl.pallas_call(
        functools.partial(first_gather, n_ctx, n_fsdp),
        in_specs=[anywhere] * 3,
        out_specs=[anywhere] * 3,
        out_shape=[
            jax.ShapeDtypeStruct((n_ctx,) + x.shape, x.dtype),
            jax.ShapeDtypeStruct((n_ctx,) + table.shape, table.dtype),
            jax.ShapeDtypeStruct((n_fsdp,) + packed.shape, packed.dtype),
        ],
        scratch_shapes=[
            dma((3,)),
            dma((n_ctx,)),
            dma((n_ctx,)),
            dma((n_ctx,)),
            dma((n_ctx,)),
            dma((n_ctx,)),
            dma((n_fsdp // 2,)),
            dma((n_fsdp // 2,)),
            dma((n_fsdp,)),
        ],
        compiler_params=pltpu.CompilerParams(collective_id=1, has_side_effects=True),
        cost_estimate=pl.CostEstimate(
            flops=0, bytes_accessed=200 * 2**20, transcendentals=0
        ),
    )(x, table, packed)


def on_device(
    inputs,
    block_ids,
    expert_ids,
    drop_order,
    attn_gain,
    w_query,
    key_projection_weight,
    value_projection_weight,
    q_gain,
    key_norm_gain,
    w_out,
    ffn_gain,
    w_router,
    expert_gate,
    expert_up,
    expert_down,
    cotangent,
):
    n_ctx, n_fsdp = lax.axis_size("ctx"), lax.axis_size("fsdp")
    ctx = lax.axis_index("ctx")
    span, width = inputs.shape[1], inputs.shape[2]
    length = block_ids.shape[1]
    experts = n_ctx * n_fsdp
    capacity = 5 * span * TOP // (4 * experts)
    slots = experts * capacity
    heads = QUERY_HEADS // n_ctx
    share = n_ctx // KEY_VALUE_HEADS
    own_rows = w_query.shape[0]
    q_width = heads * HEAD_SIZE
    qkv_width = q_width + 2 * HEAD_SIZE
    extra_width = -(-(experts + 4) // 128) * 128

    def gather_ctx(array):
        return lax.all_gather(array, "ctx", axis=0, tiled=True)

    def scatter_ctx(array):
        return lax.psum_scatter(array.astype(BF), "ctx", scatter_dimension=0, tiled=True)

    def scatter_fsdp(array):
        parts = route(array.astype(BF).reshape((n_fsdp, -1) + array.shape[1:]))
        return jnp.sum(parts.astype(F32), axis=0).astype(BF)

    def route(rows):
        return lax.all_to_all(rows, "fsdp", split_axis=0, concat_axis=0, tiled=True)

    def columns(weight, index, count):
        return lax.dynamic_slice_in_dim(weight, index * count, count, axis=1)

    def as_column(vector):
        return jnp.pad(vector, (0, own_rows - vector.shape[0]))[:, None]

    packed = jnp.concatenate(
        [
            columns(w_query, ctx, q_width),
            columns(key_projection_weight, ctx // share, HEAD_SIZE),
            columns(value_projection_weight, ctx // share, HEAD_SIZE),
            w_router,
            as_column(attn_gain),
            as_column(ffn_gain),
            as_column(q_gain),
            as_column(key_norm_gain),
            jnp.zeros((own_rows, extra_width - experts - 4), BF),
        ],
        axis=1,
    )
    table = jnp.concatenate(
        [expert_ids[0].T, drop_order[0], jnp.zeros((7, span), jnp.int32)], axis=0
    )
    inputs_all, tables, packed_all = run_first_gather(n_ctx, n_fsdp, inputs[0], table, packed)
    inputs_all = inputs_all.reshape(length, width)
    packed_all = packed_all.reshape(width, qkv_width + extra_width)
    w_qkv = packed_all[:, :qkv_width]
    extra = packed_all[:, qkv_width:].T
    router_t = extra[:experts]
    gain_attn = extra[experts : experts + 1].astype(F32)
    gain_ffn = extra[experts + 1 : experts + 2].astype(F32)

    def head_gain(at):
        return extra[at].reshape(n_fsdp, own_rows)[:, : HEAD_SIZE // n_fsdp].reshape(1, HEAD_SIZE)

    gains = jnp.concatenate(
        [head_gain(experts + 2), head_gain(experts + 3), jnp.zeros((6, HEAD_SIZE), BF)], axis=0
    ).astype(F32)

    named = tables[:, :TOP, :]
    ranks = tables[:, TOP, :]
    here = ctx * n_fsdp + jnp.arange(n_fsdp, dtype=jnp.int32)
    member = jnp.any(named[:, :, None, :] == here[None, None, :, None], axis=1)
    before = (ranks[:, :, None] < ranks[:, None, :]).astype(BF)
    place = jnp.einsum(
        "gjs,gst->gjt", member.astype(BF), before, preferred_element_type=F32
    ).astype(jnp.int32)
    place = jnp.where(member, place, capacity)
    select = (
        place[:, :, None, :] == jnp.arange(capacity, dtype=jnp.int32)[None, None, :, None]
    ).astype(BF)
    chosen = jnp.any(
        named[:, :, :, None] == jnp.arange(experts, dtype=jnp.int32), axis=1
    ).reshape(length, experts)

    def dispatch(rows):
        picked = jnp.einsum(
            "gjkt,gtd->jgkd", select, rows.reshape(n_ctx, span, width), preferred_element_type=F32
        ).astype(BF)
        return route(picked).reshape(slots, width)

    def combine(rows):
        back = route(rows.reshape(n_fsdp, n_ctx, capacity, width))
        return jnp.einsum("gjkt,jgkd->gtd", select, back, preferred_element_type=F32).reshape(
            length, width
        )

    fsdp = lax.axis_index("fsdp")
    chips = n_fsdp // 2
    half = jnp.where(fsdp // 2 == ctx, w_out, jnp.zeros_like(w_out))
    for offset in range(1, chips):
        pairs = [
            (c * n_fsdp + 2 * c + core, c * n_fsdp + 2 * (c ^ offset) + core)
            for c in range(n_ctx)
            for core in range(2)
        ]
        half = half + lax.ppermute(w_out, ("ctx", "fsdp"), pairs)
    other = lax.ppermute(half, "fsdp", [(f, f ^ 1) for f in range(n_fsdp)])
    first = fsdp % 2 == 0
    out_here = jnp.concatenate(
        [jnp.where(first, half, other), jnp.where(first, other, half)], axis=0
    )

    x_all = inputs_all.astype(F32)
    r_all = inverse_rms(x_all)
    hidden = (x_all * r_all * gain_attn).astype(BF)
    qkv = nn(hidden, w_qkv)
    exponent = jnp.arange(HALF, dtype=F32) * (2.0 / HEAD_SIZE)
    angles = jnp.arange(length, dtype=F32)[:, None] * (ROPE_BASE ** (-exponent))[None, :]
    cosine = jnp.tile(jnp.cos(angles), (1, 2))
    sine = jnp.concatenate([-jnp.sin(angles), jnp.sin(angles)], axis=1)
    own_blocks = jnp.broadcast_to(block_ids, (8, length))
    key_blocks = block_ids.reshape(length, 1)
    mixed, totals = run_attention(qkv, heads, cosine, sine, gains, own_blocks, key_blocks)
    grad_own, qkv = lax.optimization_barrier((cotangent[0], qkv))
    grad_all = gather_ctx(grad_own)
    grad_rows = dispatch(grad_all)

    mixed, grad_all = lax.optimization_barrier((mixed, grad_all))
    attn_out = scatter_ctx(nn(mixed, out_here))

    x = inputs[0].astype(F32)
    resid = x + attn_out.astype(F32)
    r_ffn = inverse_rms(resid)
    normed = gather_ctx((resid * r_ffn * gain_ffn).astype(BF))
    normed, grad_rows = lax.optimization_barrier((normed, grad_rows))
    grad_inner = nt(grad_rows, expert_down[0])
    logits = nt(normed, router_t)
    gates = jax.nn.softmax(jnp.where(chosen, logits, -jnp.inf), axis=-1)
    gates_here = lax.dynamic_slice_in_dim(gates, ctx * n_fsdp, n_fsdp, axis=1)
    gates_here = gates_here.reshape(n_ctx, span, n_fsdp).transpose(0, 2, 1)
    slot_gates = jnp.sum(select.astype(F32) * gates_here[:, :, None, :], axis=-1)
    slot_gates = route(slot_gates.transpose(1, 0, 2)).reshape(slots, 1)
    rows = dispatch(normed)

    piece = QUERY_HEADS * HEAD_SIZE // experts
    groups = n_fsdp // n_ctx
    dealt = mixed.reshape(length, groups, n_ctx, piece).transpose(2, 0, 1, 3)
    dealt = lax.all_to_all(
        dealt.reshape(n_ctx, length, groups * piece), "ctx", split_axis=0, concat_axis=0, tiled=True
    )
    rows, dealt = lax.optimization_barrier((rows, dealt))

    g = nn(rows, expert_gate[0])
    u = nn(rows, expert_up[0])
    s = jax.nn.sigmoid(g)
    inner = g * s * u
    inner_low = inner.astype(BF)
    slot_dgates = jnp.sum(inner * grad_inner, axis=-1).reshape(n_fsdp, n_ctx, capacity)
    d_inner = grad_inner * slot_gates
    dg = (d_inner * u * s * (1.0 + g * (1.0 - s))).astype(BF)
    du = (d_inner * g * s).astype(BF)
    d_rows = (nt(dg, expert_gate[0]) + nt(du, expert_up[0])).astype(BF)
    y = (nn(inner_low, expert_down[0]) * slot_gates).astype(BF)
    gate_grad = tn(rows, dg)
    up_grad = tn(rows, du)
    down_grad = tn((inner * slot_gates).astype(BF), grad_rows)

    d_gates = jnp.einsum(
        "gjkt,jgk->gjt", select.astype(F32), route(slot_dgates), precision=lax.Precision.HIGHEST
    )
    weighted = (d_gates * gates_here).transpose(0, 2, 1).reshape(length, n_fsdp)
    d_logits = lax.dynamic_update_slice_in_dim(
        jnp.zeros((length, experts), F32), weighted, ctx * n_fsdp, axis=1
    ) - gates * jnp.sum(weighted, axis=1, keepdims=True)
    d_logits = d_logits.astype(BF)
    d_normed = scatter_ctx(combine(d_rows) + nn(d_logits, router_t)).astype(F32)
    router_grad = tn(normed, d_logits)

    grad = cotangent[0].astype(F32)
    n = d_normed * gain_ffn
    d_resid = grad + r_ffn * n - resid * r_ffn**3 * jnp.mean(n * resid, axis=-1, keepdims=True)
    ffn_gain_grad = jnp.sum(d_normed * resid * r_ffn, axis=0)
    d_attn = gather_ctx(d_resid.astype(BF))
    y_all = combine(y).astype(BF)
    d_attn, y_all = lax.optimization_barrier((d_attn, y_all))
    d_mixed = nt(d_attn, out_here).astype(BF)

    moe = scatter_ctx(y_all).astype(F32)
    output = (resid + moe).astype(BF)[None]

    out_grad = jnp.einsum("ntk,td->nkd", dealt, d_attn, preferred_element_type=F32).astype(BF)
    out_grad = scatter_fsdp(out_grad.reshape(n_fsdp * piece, width))
    out_grad = gather_ctx(out_grad).astype(F32)

    dq, dkv, dgains = run_attention_back(
        qkv, d_mixed, totals, heads, cosine, sine, gains, own_blocks, key_blocks
    )
    dq, moe = lax.optimization_barrier((dq, moe))
    d_qkv = jnp.concatenate([dq, dkv], axis=1)
    d_hidden = nt(d_qkv, w_qkv)
    attn_gain_grad = jnp.sum(d_hidden * x_all * r_all, axis=0)
    d_hidden = scatter_ctx(d_hidden).astype(F32)
    r_attn = inverse_rms(x)
    n = d_hidden * gain_attn
    input_grad = d_resid + r_attn * n - x * r_attn**3 * jnp.mean(n * x, axis=-1, keepdims=True)
    input_grad = input_grad.astype(BF)[None]

    def spread(vector):
        parts = vector.reshape(n_fsdp, HEAD_SIZE // n_fsdp)
        return jnp.pad(parts, ((0, 0), (0, own_rows - parts.shape[1]))).reshape(width)

    small = jnp.stack(
        [attn_gain_grad, ffn_gain_grad, spread(dgains[0]), spread(dgains[1])], axis=1
    )
    extra_grad = jnp.concatenate(
        [
            router_grad.astype(BF),
            small.astype(BF),
            jnp.zeros((width, extra_width - experts - 4), BF),
        ],
        axis=1,
    )
    shared_grad = jnp.concatenate(
        [scatter_fsdp(tn(hidden, d_qkv)), scatter_fsdp(extra_grad)], axis=1
    )
    shared_grad = lax.all_gather(shared_grad, "ctx", axis=0, tiled=False)
    query_grad = (
        shared_grad[:, :, :q_width].transpose(1, 0, 2).reshape(own_rows, n_ctx * q_width).astype(F32)
    )

    def kv_grad(at):
        parts = shared_grad[:, :, at : at + HEAD_SIZE].astype(F32)
        parts = parts.reshape(KEY_VALUE_HEADS, share, own_rows, HEAD_SIZE).sum(axis=1)
        return parts.transpose(1, 0, 2).reshape(own_rows, KEY_VALUE_HEADS * HEAD_SIZE)

    key_grad, value_grad = kv_grad(q_width), kv_grad(q_width + HEAD_SIZE)
    rest = shared_grad[:, :, qkv_width:].astype(F32).sum(axis=0)
    head_rows = HEAD_SIZE // n_fsdp
    return (
        output,
        input_grad,
        rest[:, experts],
        query_grad,
        key_grad,
        value_grad,
        rest[:head_rows, experts + 2],
        rest[:head_rows, experts + 3],
        out_grad,
        rest[:, experts + 1],
        rest[:, :experts],
        gate_grad[None],
        up_grad[None],
        down_grad[None],
    )


def solution(mesh):
    rows, tokens = P("fsdp", None), P("fsdp", "ctx", None)
    vector, expert = P("fsdp"), P(("ctx", "fsdp"), None, None)
    in_specs = (
        tokens,
        rows,
        tokens,
        tokens,
        vector,
        rows,
        rows,
        rows,
        vector,
        vector,
        rows,
        vector,
        rows,
        expert,
        expert,
        expert,
        tokens,
    )
    out_specs = (
        tokens,
        tokens,
        vector,
        rows,
        rows,
        rows,
        vector,
        vector,
        rows,
        vector,
        rows,
        expert,
        expert,
        expert,
    )
    return jax.shard_map(
        on_device, mesh=mesh, in_specs=in_specs, out_specs=out_specs, check_vma=False
    )
```

time: 2090 us -> 1380 us (0.66)
  waiting for transfers between devices: 1290 us -> 701 us
  Pallas kernels: 0 us -> 149 us
  local copies, waits for them, and re-layouts: 220 us -> 83.5 us
  matrix products: 325 us -> 243 us
  blocking collectives: 115 us -> 52.7 us
  starting transfers between devices: 17.7 us -> 66.8 us
  other arithmetic: 92.7 us -> 61.3 us
    all_to_all x4 -> x9, waiting for transfers between devices: 717 us -> 427 us  [the longest x8 401 us: route(): return lax.all_to_all(rows, 'fsdp', split_axis=0, concat_axis=0, tiled=True)]
    reduce_scatter x7 -> x4, waiting for transfers between devices: 302 us -> 108 us  [scatter_ctx(): lax.psum_scatter(array.astype(BF), 'ctx', scatter_dimension=0, tiled=True)]
    pallas_call x0 -> x3, Pallas kernels: none -> 149 us  [the longest x1 82.1 us: run_first_gather(): pl.pallas_call(functools.partial(first_gather, n_ctx, n_fsdp), in_specs=[...]
    psum x1 -> x0, waiting for transfers between devices: 141 us -> none  [on_device(): lax.psum(owned[1].astype(jnp.bfloat16), 'ctx').astype(jnp.float32)]
    gather x9 -> x0, local copies, waits for them, and re-layouts: 104 us -> none  [the longest x1 22.1 us: on_device(): picked = returned[clipped].astype(jnp.float32)]
    ppermute x0 -> x4, waiting for transfers between devices: none -> 83.5 us  [the longest x3 83.5 us: on_device(): half = half + lax.ppermute(w_out, ('ctx', 'fsdp'), pairs)]
    dot_general x56 -> x24, matrix products: 325 us -> 243 us  [the longest x6 72.2 us: nn(): lax.dot_general(a, b, (((1,), (0,)), ((), ())), preferred_element_type=F32)]
    all_gather x3 -> x0, blocking collectives: 66.6 us -> none  [the longest x1 49.9 us: on_device(): lax.all_gather(w_router, 'fsdp', axis=0, tiled=True)]
  transfers between devices with their start and end apart: 18 -> 22, of which waited for: 14 -> 14; matrix products, arithmetic and copies ran while one was open for 20% -> 18% of each run, Pallas kernels for 0% -> 5%
where the time goes in v1:
time: 1380 us; the launch traced here: 1370 us
  waiting for transfers between devices  701 us (51%)
  matrix products  243 us (18%)
  Pallas kernels  149 us (11%)
  local copies, waits for them, and re-layouts  83.5 us (6%)
  starting transfers between devices  66.8 us (5%)
  other arithmetic  61.3 us (4%)
  blocking collectives  52.7 us (4%)
  between operations  14.9 us (1%)
    all_to_all x8, waiting for transfers between devices, route(): return lax.all_to_all(rows, 'fsdp', split_axis=0, concat_axis=0, tiled=True)  401 us
    reduce_scatter x4, waiting for transfers between devices, scatter_ctx(): lax.psum_scatter(array.astype(BF), 'ctx', scatter_dimension=0, tiled=True)  108 us
    ppermute x3, waiting for transfers between devices, on_device(): half = half + lax.ppermute(w_out, ('ctx', 'fsdp'), pairs)  83.5 us
    pallas_call x1, Pallas kernels, run_first_gather(): pl.pallas_call(functools.partial(first_gather, n_ctx, n_fsdp), in_specs=[...  82.1 us
    dot_general x6, matrix products, nn(): lax.dot_general(a, b, (((1,), (0,)), ((), ())), preferred_element_type=F32)  72.2 us
    dot_general x6, matrix products, nt(): lax.dot_general(a, b, (((1,), (1,)), ((), ())), preferred_element_type=F32)  71.7 us
    dot_general x5, matrix products, tn(): lax.dot_general(a, b, (((0,), (0,)), ((), ())), preferred_element_type=F32)  58.8 us
    all_gather x1, waiting for transfers between devices, on_device(): shared_grad = lax.all_gather(shared_grad, 'ctx', axis=0, tiled=False)  57.1 us
  transfers between devices with their start and end apart: 22, of which 14 were waited for; matrix products, arithmetic and copies ran while one was open for 18% of the time, Pallas kernels for 5%

profile of v1, /device:TPU:0, one launch (start us, length us, event | category | flops | bytes accessed | tf_op | source)
XLA Modules:
  0.0 1372.4 jit_solution(8317379205190842585)
XLA Ops:
  18.2 82.1 %shard_map.272 = (bf16[4,256,2048]{2,1,0:T(8,128)(2,1)}, s32[4,16,256]{2,1,0:T(8,128)}, bf16[8,256,1408]{2,1,0:T(8,128)(2,1)}) custom-call(bf16[256,2048]{1,0:T(8,128)(2,1)} %bitcast.174, s32[16,256]{1,0:T(8,128)} %add_add_fusion.1.table_ref, bf16[256,1408]{1,0:T(8,128)(2,1)} %concatenate.26.packed_ref), custom_call_target="tpu_custom_call" | custom-call | bytes 209715200 | tf_op jit(solution)/shard_map/pallas_call | solution.py:356
  111.6 11.3 fusion.12.q_ref.k_ref.v_ref
  133.0 39.0 %collective-permute-done = bf16[512,2048]{1,0:T(8,128)(2,1)} collective-permute-done((bf16[512,2048]{1,0:T(8,128)(2,1)}, bf16[512,2048]{1,0:T(8,128)(2,1)}, u32[]{:S(2)}, u32[]{:S(2)}) %collective-permute-start) | collective-permute-done | bytes 2097184 | tf_op jit(solution)/shard_map/ppermute | solution.py:505
  172.0 44.5 %collective-permute-done.2 = bf16[512,2048]{1,0:T(8,128)(2,1)} collective-permute-done((bf16[512,2048]{1,0:T(8,128)(2,1)}, bf16[512,2048]{1,0:T(8,128)(2,1)}, u32[]{:S(2)}, u32[]{:S(2)}) %collective-permute-start.2) | collective-permute-done | bytes 2097184 | tf_op jit(solution)/shard_map/ppermute | solution.py:505
  216.5 5.2 add_add_fusion
  233.7 28.9 %shard_map.273 = (bf16[1024,1024]{1,0:T(8,128)(2,1)S(1)}, f32[8,8,1024]{2,1,0:T(8,128)S(1)}) custom-call(f32[1024,1280]{1,0:T(8,128)} %fusion.12.q_ref.k_ref.v_ref, f32[1024,1280]{1,0:T(8,128)} %fusion.12.q_ref.k_ref.v_ref, f32[1024,1280]{1,0:T(8,128)} %fusion.12.q_ref.k_ref.v_ref, f32[1024,128]{1,0:T(8,128)S(1)} %copy-done.6, ...), custom_call_target="tpu_custom_call" | custom-call | flops 4294967296 | bytes 8388608 | tf_op jit(solution)/shard_map/pallas_call | solution.py:163
  264.0 4.5 broadcast_select_fusion.1
  268.5 9.4 convolution_convert_fusion.1
  279.8 7.6 convert_bitcast_fusion.1
  287.4 10.2 copy.213
  297.6 19.0 %all-to-all-start = ((bf16[8,4,80,2048]{3,2,1,0:T(8,128)(2,1)}), bf16[8,4,80,2048]{3,2,1,0:T(8,128)(2,1)}, u32[]{:S(2)}, u32[]{:S(2)}) async-start(bf16[8,4,80,2048]{3,2,1,0:T(8,128)(2,1)} %copy.213), calls=%async_computation.1 | async-start | bytes 20971520 | tf_op jit(solution)/shard_map/all_to_all | solution.py:427
  316.7 37.3 %reduce-scatter.5.cloned.1.call-done = bf16[256,2048]{1,0:T(8,128)(2,1)} async-done(((bf16[1024,2048]{1,0:T(8,128)(2,1)}), bf16[256,2048]{1,0:T(8,128)(2,1)}) %reduce-scatter.5.cloned.1.call-update) | async-done | bytes 1048592 | tf_op jit(solution)/shard_map/reduce_scatter | solution.py:420
  368.8 64.6 %all-to-all-done = bf16[8,4,80,2048]{3,2,1,0:T(8,128)(2,1)} async-done(((bf16[8,4,80,2048]{3,2,1,0:T(8,128)(2,1)}), bf16[8,4,80,2048]{3,2,1,0:T(8,128)(2,1)}, u32[]{:S(2)}, u32[]{:S(2)}) %all-to-all-start) | async-done | bytes 10485792 | tf_op jit(solution)/shard_map/all_to_all | solution.py:427
  438.7 15.2 %all-gather.9.cloned.1.call-done = bf16[1024,2048]{1,0:T(8,128)(2,1)} async-done(((bf16[256,2048]{1,0:T(8,128)(2,1)}), bf16[1024,2048]{1,0:T(8,128)(2,1)}) %all-gather.9.cloned.1.call-update) | async-done | bytes 4194320 | tf_op jit(solution)/shard_map/all_gather | solution.py:417
  460.2 25.9 %all-to-all-done.3 = bf16[4,1024,256]{1,2,0:T(8,128)(2,1)} async-done(((bf16[4,1024,256]{1,2,0:T(8,128)(2,1)}), bf16[4,1024,256]{1,2,0:T(8,128)(2,1)}, u32[]{:S(2)}, u32[]{:S(2)}) %all-to-all-start.3) | async-done | bytes 2097184 | tf_op jit(solution)/shard_map/all_to_all | solution.py:547
  490.1 7.7 convert_bitcast_fusion
  497.7 10.2 copy.216
  507.9 5.1 all-to-all-start.2
  514.5 115.1 %all-to-all-done.2 = bf16[8,4,80,2048]{3,2,1,0:T(8,128)(2,1)} async-done(((bf16[8,4,80,2048]{3,2,1,0:T(8,128)(2,1)}), bf16[8,4,80,2048]{3,2,1,0:T(8,128)(2,1)}, u32[]{:S(2)}, u32[]{:S(2)}) %all-to-all-start.2) | async-done | bytes 10485792 | tf_op jit(solution)/shard_map/all_to_all | solution.py:427
  629.6 13.0 fusion.27
  642.7 16.1 %fusion.30 = f32[2560,768]{0,1:T(8,128)} fusion(bf16[2560,2048]{1,0:T(8,128)(2,1)} %bitcast.26, bf16[1,2048,768]{2,1,0:T(8,128)(2,1)S(1)} %copy-done.39), kind=kOutput, calls=%fused_computation.51 | convolution fusion | flops 8053063680 | bytes 21495808 | tf_op jit(solution)/shard_map/dot_general | solution.py:29
  658.8 19.5 %multiply_reduce_fusion = (f32[2560]{0:T(1024)}, bf16[2560,768]{0,1:T(8,128)(2,1)}, bf16[2560,768]{0,1:T(8,128)(2,1)}) fusion(f32[2560,768]{0,1:T(8,128)} %fusion.30, f32[2560,768]{0,1:T(8,128)S(1)} %fusion.27, f32[2560]{0:T(1024)S(1)} %copy-done.36, bf16[2560,2048]{1,0:T(8,128)(2,1)} %bitcast.17, bf16[1,768,2048]{2,1,0:T(8,128)(2,1)S(1)} %copy-done), kind=kOutput, calls=%fused_computation.20 | convolution fusion | flops 8088450560 | bytes 37244928 | tf_op jit(solution)/shard_map/dot_general | solution.py:25
  684.0 15.1 %fusion.25 = f32[2560,2048]{1,0:T(8,128)} fusion(bf16[2560,768]{0,1:T(8,128)(2,1)} %get-tuple-element.148, bf16[1,2048,768]{2,1,0:T(8,128)(2,1)} %param.30), kind=kOutput, calls=%fused_computation.46 | convolution fusion | flops 8053063680 | bytes 28049408 | tf_op jit(solution)/shard_map/dot_general | solution.py:25
  699.1 16.6 %add_convert_fusion = bf16[2560,2048]{1,0:T(8,128)(2,1)} fusion(f32[2560,2048]{1,0:T(8,128)} %fusion.25, bf16[2560,768]{0,1:T(8,128)(2,1)} %get-tuple-element.149, bf16[1,2048,768]{2,1,0:T(8,128)(2,1)} %param.31), kind=kOutput, calls=%fused_computation.1 | convolution fusion | flops 8063549440 | bytes 38535168 | tf_op jit(solution)/shard_map/dot_general | solution.py:25
  715.7 5.1 all-to-all-start.4
  724.1 113.3 %all-to-all-done.4 = bf16[8,4,80,2048]{3,2,1,0:T(8,128)(2,1)} async-done(((bf16[8,4,80,2048]{3,2,1,0:T(8,128)(2,1)}), bf16[8,4,80,2048]{3,2,1,0:T(8,128)(2,1)}, u32[]{:S(2)}, u32[]{:S(2)}) %all-to-all-start.4) | async-done | bytes 10485792 | tf_op jit(solution)/shard_map/all_to_all | solution.py:427
  837.4 6.4 fusion.2
  848.7 18.3 %multiply_convert_fusion = bf16[2560,2048]{1,0:T(8,128)(2,1)} fusion(f32[2560]{0:T(1024)S(1)} %copy-done.37, bf16[1,768,2048]{2,1,0:T(8,128)(2,1)S(1)} %copy-done, f32[2560,768]{0,1:T(8,128)} %fusion.30, f32[2560,768]{0,1:T(8,128)} %copy-done.40), kind=kOutput, calls=%fused_computation | convolution fusion | flops 8075345920 | bytes 29370368 | tf_op jit(solution)/shard_map/dot_general | solution.py:29
  867.1 5.4 all-to-all-start.6
  872.6 48.8 %reduce-scatter.7.cloned.1.call-done = bf16[256,2048]{1,0:T(8,128)(2,1)} async-done(((bf16[1024,2048]{1,0:T(8,128)(2,1)}), bf16[256,2048]{1,0:T(8,128)(2,1)}) %reduce-scatter.7.cloned.1.call-update) | async-done | bytes 1048592 | tf_op jit(solution)/shard_map/reduce_scatter | solution.py:420
  926.9 62.2 %all-to-all-done.6 = bf16[8,4,80,2048]{3,2,1,0:T(8,128)(2,1)} async-done(((bf16[8,4,80,2048]{3,2,1,0:T(8,128)(2,1)}), bf16[8,4,80,2048]{3,2,1,0:T(8,128)(2,1)}, u32[]{:S(2)}, u32[]{:S(2)}) %all-to-all-start.6) | async-done | bytes 10485792 | tf_op jit(solution)/shard_map/all_to_all | solution.py:427
  989.1 9.4 bitcast_convert_fusion
  998.4 9.6 all-gather.11.cloned.1.call-done
  1008.0 7.3 fusion.22
  1015.3 52.7 %all_to_all.50 = bf16[8,128,2048]{2,1,0:T(8,128)(2,1)} all-to-all(bf16[8,128,2048]{2,1,0:T(8,128)(2,1)S(1)} %bitcast.184), channel_id=1, replica_groups=mesh['ctx'=4,'fsdp'=8] {'fsdp'}, dimensions={0} | all-to-all | bytes 8388608 | tf_op jit(solution)/shard_map/all_to_all | solution.py:427
  1072.4 9.6 fusion.50.grad_ref
  1082.1 37.7 %shard_map.274 = (bf16[1024,1024]{1,0:T(8,128)(2,1)S(1)}, bf16[1024,256]{1,0:T(8,128)(2,1)S(1)}, f32[8,128]{1,0:T(8,128)S(1)}) custom-call(f32[1024,1280]{1,0:T(8,128)} %fusion.12.q_ref.k_ref.v_ref, f32[1024,1280]{1,0:T(8,128)} %fusion.12.q_ref.k_ref.v_ref, f32[1024,1280]{1,0:T(8,128)} %fusion.12.q_ref.k_ref.v_ref, bf16[1024,1024]{1,0:T(8,128)(2,1)} %fusion.50.grad_ref, ...), custom_call_target="tpu_custom_call" | custom-call | flops 10737418240 | bytes 10485760 | tf_op jit(solution)/shard_map/pallas_call | solution.py:188
  1122.0 7.3 fusion.9
  1143.6 9.8 convolution_convert_fusion
  1153.4 4.7 all-to-all-start.7
  1158.1 14.0 %convolution_bitcast_fusion.1 = f32[1,2048,768]{2,1,0:T(8,128)} fusion(bf16[2560,2048]{1,0:T(8,128)(2,1)} %bitcast.26, bf16[2560,768]{0,1:T(8,128)(2,1)} %get-tuple-element.148), kind=kOutput, calls=%fused_computation.39 | convolution fusion | flops 8053063680 | bytes 20709376 | tf_op jit(solution)/shard_map/dot_general | solution.py:33
  1172.1 46.2 %all-to-all-done.7 = bf16[8,256,1280]{2,1,0:T(8,128)(2,1)} async-done(((bf16[8,256,1280]{2,1,0:T(8,128)(2,1)}), bf16[8,256,1280]{2,1,0:T(8,128)(2,1)}, u32[]{:S(2)}, u32[]{:S(2)}) %all-to-all-start.7) | async-done | bytes 5242912 | tf_op jit(solution)/shard_map/all_to_all | solution.py:427
  1222.9 13.9 %convolution_bitcast_fusion = f32[1,2048,768]{2,1,0:T(8,128)} fusion(bf16[2560,2048]{1,0:T(8,128)(2,1)} %bitcast.26, bf16[2560,768]{0,1:T(8,128)(2,1)} %get-tuple-element.149), kind=kOutput, calls=%fused_computation.38 | convolution fusion | flops 8053063680 | bytes 20709376 | tf_op jit(solution)/shard_map/dot_general | solution.py:33
  1236.8 17.7 %fusion.21 = f32[1,768,2048]{2,1,0:T(8,128)} fusion(bf16[2560,2048]{1,0:T(8,128)(2,1)} %bitcast.17, f32[2560]{0:T(1024)S(1)} %copy-done.37, f32[2560,768]{0,1:T(8,128)} %fusion.30, f32[2560,768]{0,1:T(8,128)} %copy-done.40), kind=kOutput, calls=%fused_computation.37 | convolution fusion | flops 8066826240 | bytes 32516096 | tf_op jit(solution)/shard_map/dot_general | solution.py:33
  1260.6 21.8 %reduce-scatter.9.cloned.1.call-done = bf16[256,2048]{1,0:T(8,128)(2,1)} async-done(((bf16[1024,2048]{1,0:T(8,128)(2,1)}), bf16[256,2048]{1,0:T(8,128)(2,1)}) %reduce-scatter.9.cloned.1.call-update) | async-done | bytes 1048592 | tf_op jit(solution)/shard_map/reduce_scatter | solution.py:420
  1286.6 57.1 %all-gather.15.cloned.1.call-done = bf16[1024,1408]{1,0:T(8,128)(2,1)} async-done(((bf16[256,1408]{1,0:T(8,128)(2,1)}), bf16[1024,1408]{1,0:T(8,128)(2,1)}) %all-gather.15.cloned.1.call-update) | async-done | bytes 2883600 | tf_op jit(solution)/shard_map/all_gather | solution.py:625
  1354.5 5.4 copy.227
  1359.8 5.7 copy.230
  (227 shorter events, 145.0 us)
Async XLA Ops:
  7.2 651.6 %copy-start = (bf16[1,768,2048]{2,1,0:T(8,128)(2,1)S(1)}, bf16[1,768,2048]{2,1,0:T(8,128)(2,1)}, u32[]{:S(2)}) copy-start(bf16[1,768,2048]{2,1,0:T(8,128)(2,1)} %param.32) | copy-start | bytes 9437188
  7.2 261.3 %all-gather.7.cloned.1.call-start = ((), (), s32[]{:S(2)}) async-start(), calls=%async_computation.14 | async-start | bytes 5242880 | tf_op jit(solution)/shard_map/all_gather | solution.py:417
  108.3 248.2 %copy-start.24 = (f32[1,2048]{1,0:T(1,128)}, f32[1,2048]{1,0:T(1,128)S(1)}, u32[]{:S(2)}) copy-start(f32[1,2048]{1,0:T(1,128)S(1)} %get-tuple-element.158) | copy-start | bytes 24580
  111.6 11.3 copy-start.20
  122.9 231.1 %reduce-scatter.5.cloned.1.call-start = ((), (), s32[]{:S(2)}) async-start(), calls=%async_computation.15 | async-start | bytes 5242880 | tf_op jit(solution)/shard_map/reduce_scatter | solution.py:420
  122.9 49.0 %collective-permute-start = (bf16[512,2048]{1,0:T(8,128)(2,1)}, bf16[512,2048]{1,0:T(8,128)(2,1)}, u32[]{:S(2)}, u32[]{:S(2)}) collective-permute-start(bf16[512,2048]{1,0:T(8,128)(2,1)} %param.27), channel_id=1, source_target_pairs={{0,2},{1,3},{10,8},{11,9},{20,22},{21,23},{30,28},{31,29}} | collective-permute-start | bytes 6291464 | tf_op jit(solution)/shard_map/ppermute | solution.py:505
  127.1 89.3 %collective-permute-start.2 = (bf16[512,2048]{1,0:T(8,128)(2,1)}, bf16[512,2048]{1,0:T(8,128)(2,1)}, u32[]{:S(2)}, u32[]{:S(2)}) collective-permute-start(bf16[512,2048]{1,0:T(8,128)(2,1)} %param.27), channel_id=1, source_target_pairs={{0,6},{1,7},{10,12},{11,13},{20,18},{21,19},{30,24},{31,25}} | collective-permute-start | bytes 6291464 | tf_op jit(solution)/shard_map/ppermute | solution.py:505
  130.1 86.4 %collective-permute-start.1 = (bf16[512,2048]{1,0:T(8,128)(2,1)}, bf16[512,2048]{1,0:T(8,128)(2,1)}, u32[]{:S(2)}, u32[]{:S(2)}) collective-permute-start(bf16[512,2048]{1,0:T(8,128)(2,1)} %param.27), channel_id=1, source_target_pairs={{0,4},{1,5},{10,14},{11,15},{20,16},{21,17},{30,26},{31,27}} | collective-permute-start | bytes 6291464 | tf_op jit(solution)/shard_map/ppermute | solution.py:505
  133.0 88.6 %copy-start.33 = (s32[1,1024]{1,0:T(1,128)S(1)}, s32[1,1024]{1,0:T(1,128)}, u32[]{:S(2)}) copy-start(s32[1,1024]{1,0:T(1,128)} %param.18) | copy-start | bytes 12292
  221.6 42.3 %collective-permute-start.3 = (bf16[512,2048]{1,0:T(8,128)(2,1)}, bf16[512,2048]{1,0:T(8,128)(2,1)}, u32[]{:S(2)}, u32[]{:S(2)}) collective-permute-start(bf16[512,2048]{1,0:T(8,128)(2,1)} %add_add_fusion), channel_id=1, source_target_pairs={{0,1},{1,0},{2,3},{3,2},{4,5},{5,4},{6,7},{7,6},{8,9},{9,8},{10,11... | collective-permute-start | bytes 6291464 | tf_op jit(solution)/shard_map/ppermute | solution.py:506
  231.4 31.2 %copy-start.2 = (f32[1024,128]{1,0:T(8,128)}, f32[1024,128]{1,0:T(8,128)S(1)}, u32[]{:S(2)}) copy-start(f32[1024,128]{1,0:T(8,128)S(1)} %pad_maximum_fusion.6.sin_ref) | copy-start | bytes 1572868
  231.5 31.1 %copy-start.11 = (f32[8,128]{1,0:T(8,128)}, f32[8,128]{1,0:T(8,128)S(1)}, u32[]{:S(2)}) copy-start(f32[8,128]{1,0:T(8,128)S(1)} %maximum_convert_fusion.gains_ref) | copy-start | bytes 12292
  233.7 28.9 %copy-start.9 = (s32[8,1024]{1,0:T(8,128)}, s32[8,1024]{1,0:T(8,128)S(1)}, u32[]{:S(2)}) copy-start(s32[8,1024]{1,0:T(8,128)S(1)} %broadcast_in_dim.85.own_ref) | copy-start | bytes 98308
  297.6 135.8 %all-to-all-start = ((bf16[8,4,80,2048]{3,2,1,0:T(8,128)(2,1)}), bf16[8,4,80,2048]{3,2,1,0:T(8,128)(2,1)}, u32[]{:S(2)}, u32[]{:S(2)}) async-start(bf16[8,4,80,2048]{3,2,1,0:T(8,128)(2,1)} %copy.213), calls=%async_computation.1 | async-start | bytes 20971520 | tf_op jit(solution)/shard_map/all_to_all | solution.py:427
  316.6 137.3 %all-gather.9.cloned.1.call-start = ((), (), s32[]{:S(2)}) async-start(), calls=%async_computation.16 | async-start | bytes 5242880 | tf_op jit(solution)/shard_map/all_gather | solution.py:417
  433.4 52.8 %all-to-all-start.3 = ((bf16[4,1024,256]{1,2,0:T(8,128)(2,1)}), bf16[4,1024,256]{1,2,0:T(8,128)(2,1)}, u32[]{:S(2)}, u32[]{:S(2)}) async-start(bf16[4,1024,256]{1,2,0:T(8,128)(2,1)} %bitcast.180), calls=%async_computation.4 | async-start | bytes 4194304 | tf_op jit(solution)/shard_map/all_to_all | solution.py:547
  486.2 21.8 %all-to-all-start.1 = ((f32[8,4,80]{2,1,0:T(4,128)}), f32[8,4,80]{2,1,0:T(4,128)}, u32[]{:S(2)}, u32[]{:S(2)}) async-start(f32[8,4,80]{2,1,0:T(4,128)} %copy.215), calls=%async_computation.2 | async-start | bytes 32768 | tf_op jit(solution)/shard_map/all_to_all | solution.py:427
  507.9 121.7 %all-to-all-start.2 = ((bf16[8,4,80,2048]{3,2,1,0:T(8,128)(2,1)}), bf16[8,4,80,2048]{3,2,1,0:T(8,128)(2,1)}, u32[]{:S(2)}, u32[]{:S(2)}) async-start(bf16[8,4,80,2048]{3,2,1,0:T(8,128)(2,1)} %copy.216), calls=%async_computation.3 | async-start | bytes 20971520 | tf_op jit(solution)/shard_map/all_to_all | solution.py:427
  629.6 13.0 copy-start.39
  642.7 16.1 %copy-start.40 = (f32[2560,768]{0,1:T(8,128)}, f32[2560,768]{0,1:T(8,128)S(1)}, u32[]{:S(2)}) copy-start(f32[2560,768]{0,1:T(8,128)S(1)} %fusion.27) | copy-start | bytes 23592964
  642.7 16.1 %copy-start.36 = (f32[2560]{0:T(1024)S(1)}, f32[2560]{0:T(1024)}, u32[]{:S(2)}) copy-start(f32[2560]{0:T(1024)} %mul.296) | copy-start | bytes 30724
  679.6 36.1 %all-to-all-start.5 = ((f32[8,4,80]{2,1,0:T(4,128)}), f32[8,4,80]{2,1,0:T(4,128)}, u32[]{:S(2)}, u32[]{:S(2)}) async-start(f32[8,4,80]{2,1,0:T(4,128)} %reshape.224), calls=%async_computation.6 | async-start | bytes 32768 | tf_op jit(solution)/shard_map/all_to_all | solution.py:427
  715.7 121.7 %all-to-all-start.4 = ((bf16[8,4,80,2048]{3,2,1,0:T(8,128)(2,1)}), bf16[8,4,80,2048]{3,2,1,0:T(8,128)(2,1)}, u32[]{:S(2)}, u32[]{:S(2)}) async-start(bf16[8,4,80,2048]{3,2,1,0:T(8,128)(2,1)} %bitcast.177), calls=%async_computation.5 | async-start | bytes 20971520 | tf_op jit(solution)/shard_map/all_to_all | solution.py:427
  720.9 200.5 %reduce-scatter.7.cloned.1.call-start = ((), (), s32[]{:S(2)}) async-start(), calls=%async_computation.17 | async-start | bytes 5242880 | tf_op jit(solution)/shard_map/reduce_scatter | solution.py:420
  724.1 119.7 %copy-start.22 = (bf16[1024,32]{0,1:T(8,128)(2,1)S(1)}, bf16[1024,32]{0,1:T(8,128)(2,1)}, u32[]{:S(2)}) copy-start(bf16[1024,32]{0,1:T(8,128)(2,1)} %subtract_convert_fusion) | copy-start | bytes 196612
  867.0 54.3 %copy-start.13 = (bf16[1,256,2048]{2,1,0:T(8,128)(2,1)S(1)}, bf16[1,256,2048]{2,1,0:T(8,128)(2,1)}, u32[]{:S(2)}) copy-start(bf16[1,256,2048]{2,1,0:T(8,128)(2,1)} %param.17) | copy-start | bytes 3145732
  867.0 54.3 %copy-start.15 = (bf16[256,2048]{1,0:T(8,128)(2,1)S(1)}, bf16[256,2048]{1,0:T(8,128)(2,1)}, u32[]{:S(2)}) copy-start(bf16[256,2048]{1,0:T(8,128)(2,1)} %reduce-scatter.5.cloned.1.call-done) | copy-start | bytes 3145732
  867.1 54.3 %copy-start.25 = (f32[1,2048]{1,0:T(1,128)S(1)}, f32[1,2048]{1,0:T(1,128)}, u32[]{:S(2)}) copy-start(f32[1,2048]{1,0:T(1,128)} %copy-done.24) | copy-start | bytes 24580
  867.1 54.3 %copy-start.31 = (f32[256]{0:T(256)S(1)}, f32[256]{0:T(256)}, u32[]{:S(2)}) copy-start(f32[256]{0:T(256)} %copy-done.30) | copy-start | bytes 3076
  867.1 56.5 %copy-start.18 = (bf16[1,256,2048]{2,1,0:T(8,128)(2,1)S(1)}, bf16[1,256,2048]{2,1,0:T(8,128)(2,1)}, u32[]{:S(2)}) copy-start(bf16[1,256,2048]{2,1,0:T(8,128)(2,1)} %param.33) | copy-start | bytes 3145732
  867.1 56.5 %copy-start.38 = (f32[256]{0:T(256)S(1)}, f32[256]{0:T(256)}, u32[]{:S(2)}) copy-start(f32[256]{0:T(256)} %get-tuple-element.162) | copy-start | bytes 3076
  867.1 122.0 %all-to-all-start.6 = ((bf16[8,4,80,2048]{3,2,1,0:T(8,128)(2,1)}), bf16[8,4,80,2048]{3,2,1,0:T(8,128)(2,1)}, u32[]{:S(2)}, u32[]{:S(2)}) async-start(bf16[8,4,80,2048]{3,2,1,0:T(8,128)(2,1)} %bitcast.178), calls=%async_computation.8 | async-start | bytes 20971520 | tf_op jit(solution)/shard_map/all_to_all | solution.py:427
  872.5 116.5 %copy-start.29 = (s32[4,8,256]{2,1,0:T(8,128)S(1)}, s32[4,8,256]{2,1,0:T(8,128)}, u32[]{:S(2)}) copy-start(s32[4,8,256]{2,1,0:T(8,128)} %copy-done.28) | copy-start | bytes 98308
  872.5 135.5 %all-gather.11.cloned.1.call-start = ((), (), s32[]{:S(2)}) async-start(), calls=%async_computation.18 | async-start | bytes 5242880 | tf_op jit(solution)/shard_map/all_gather | solution.py:417
  926.6 328.0 %all-gather.13.cloned.1.call-start = ((), (), s32[]{:S(2)}) async-start(), calls=%async_computation.21 | async-start | bytes 2621440 | tf_op jit(solution)/shard_map/all_gather | solution.py:417
  1071.9 10.1 copy-start.3
  1071.9 10.1 copy-start.5
  1071.9 10.1 copy-start.7
  1071.9 10.1 copy-start.10
  1071.9 187.0 %reduce-scatter.11.cloned.1.call-start = ((), (), s32[]{:S(2)}) async-start(), calls=%async_computation.20 | async-start | bytes 5242880 | tf_op jit(solution)/shard_map/reduce_scatter | solution.py:420
  1072.4 47.7 %slice-start = ((s8[5767168]{0:T(1024)(128)(4,1)}), s8[4194304]{0:T(1024)(128)(4,1)S(1)}, s32[]{:S(2)}) async-start(s8[5767168]{0:T(1024)(128)(4,1)} %bitcast.212), calls=%async_computation.23 | async-start | bytes 8388608
  1082.1 38.0 %slice-start.1 = ((s8[5767168]{0:T(1024)(128)(4,1)}), s8[1572864]{0:T(1024)(128)(4,1)S(1)}, s32[]{:S(2)}) async-start(s8[5767168]{0:T(1024)(128)(4,1)} %bitcast.212), calls=%async_computation.24 | async-start | bytes 3145728
  1129.3 153.1 %reduce-scatter.9.cloned.1.call-start = ((), (), s32[]{:S(2)}) async-start(), calls=%async_computation.19 | async-start | bytes 5242880 | tf_op jit(solution)/shard_map/reduce_scatter | solution.py:420
  1140.1 13.3 all-to-all-start.8
  1153.4 65.0 %all-to-all-start.7 = ((bf16[8,256,1280]{2,1,0:T(8,128)(2,1)}), bf16[8,256,1280]{2,1,0:T(8,128)(2,1)}, u32[]{:S(2)}, u32[]{:S(2)}) async-start(bf16[8,256,1280]{2,1,0:T(8,128)(2,1)} %bitcast.182), calls=%async_computation.11 | async-start | bytes 10485760 | tf_op jit(solution)/shard_map/all_to_all | solution.py:427
  1158.0 185.7 %all-gather.15.cloned.1.call-start = ((), (), s32[]{:S(2)}) async-start(), calls=%async_computation.22 | async-start | bytes 3604480 | tf_op jit(solution)/shard_map/all_gather | solution.py:625
  1254.6 27.8 %copy-start.16 = (bf16[256,2048]{1,0:T(8,128)(2,1)S(1)}, bf16[256,2048]{1,0:T(8,128)(2,1)}, u32[]{:S(2)}) copy-start(bf16[256,2048]{1,0:T(8,128)(2,1)} %reduce-scatter.5.cloned.1.call-done) | copy-start | bytes 3145732
  1254.6 27.8 %copy-start.19 = (bf16[1,256,2048]{2,1,0:T(8,128)(2,1)S(1)}, bf16[1,256,2048]{2,1,0:T(8,128)(2,1)}, u32[]{:S(2)}) copy-start(bf16[1,256,2048]{2,1,0:T(8,128)(2,1)} %param.33) | copy-start | bytes 3145732
  (17 other events, 54.5 us)
Sparse Core Ops, SparseCore 0:
  123.0 79.8 all-gather.6
  278.0 75.9 reduce-scatter.4
  360.1 93.7 all-gather.8
  848.2 73.1 reduce-scatter.6
  926.7 81.2 all-gather.10
  1072.0 42.7 all-gather.12
  1129.4 73.2 reduce-scatter.10
  1205.1 77.2 reduce-scatter.8
  1284.0 59.6 all-gather.14

commit v2 on v1

--- a/solution.py
+++ b/solution.py
@@ -51,7 +51,7 @@
 
 
 def attention_forward(
-    q_ref, k_ref, v_ref, cos_ref, sin_ref, gains_ref, own_ref, key_ref, mixed_ref, total_ref, keys, values_t
+    q_ref, k_ref, v_ref, cos_ref, sin_ref, gains_ref, own_ref, key_ref, mixed_ref, total_ref, dealt_ref, keys, values_t
 ):
     cosine, sine = cos_ref[...], sin_ref[...]
 
@@ -72,6 +72,7 @@
         total = jnp.sum(weights, axis=0, keepdims=True)
         out = nn(values_t[...], weights.astype(BF)) / total
         mixed_ref[start : start + chunk, :] = out.T.astype(BF)
+        dealt_ref[0, start : start + chunk, :] = out.T.astype(BF)
         total_ref[0, :, start : start + chunk] = jnp.broadcast_to(top + jnp.log(total), (8, chunk))
 
 
@@ -157,17 +158,23 @@
     return whole, column, head_column, totals, shared
 
 
-def run_attention(qkv, heads, cosine, sine, gains, own, key_blocks):
+def run_attention(qkv, heads, n_ctx, cosine, sine, gains, own, key_blocks):
     length = qkv.shape[0]
     whole, column, head_column, totals, shared = attention_specs(heads, length)
+    deals = min(n_ctx, heads)
     return pl.pallas_call(
         attention_forward,
         grid=(heads,),
         in_specs=[head_column, column(heads), column(heads + 1)] + shared,
-        out_specs=[head_column, totals],
+        out_specs=[
+            head_column,
+            totals,
+            pl.BlockSpec((1, length, HEAD_SIZE), lambda h: (h % deals, 0, h // deals)),
+        ],
         out_shape=[
             jax.ShapeDtypeStruct((length, heads * HEAD_SIZE), BF),
             jax.ShapeDtypeStruct((heads, 8, length), F32),
+            jax.ShapeDtypeStruct((deals, length, heads // deals * HEAD_SIZE), BF),
         ],
         scratch_shapes=[
             pltpu.VMEM((length, HEAD_SIZE), BF),
@@ -230,51 +237,59 @@
     pl.semaphore_wait(barrier, len(devices))
 
 
-def line_gather(n_ctx, ctx, fsdp, own_ref, all_ref, up, down, arrived):
-    def hop(block, step, sems, to):
-        def start(source):
-            push(source, all_ref.at[block], sems.at[step], arrived.at[block], (to, fsdp)).start()
-
+class LineGather:
+    def __init__(self, n_ctx, ctx, fsdp, own_ref, all_ref, up, down, arrived):
+        self.n_ctx, self.ctx, self.fsdp = n_ctx, ctx, fsdp
+        self.own_ref, self.all_ref = own_ref, all_ref
+        self.up, self.down, self.arrived = up, down, arrived
+
+    def copy(self, source, block, sems, step, to):
+        return push(
+            source, self.all_ref.at[block], sems.at[step], self.arrived.at[block], (to, self.fsdp)
+        )
+
+    def going_up(self, step):
+        return (self.ctx - step >= 0) & (self.ctx < self.n_ctx - 1)
+
+    def going_down(self, step):
+        return (self.ctx + step < self.n_ctx) & (self.ctx > 0)
+
+    def hop(self, block, step, sems, to):
         if step == 0:
-            start(own_ref)
+            self.copy(self.own_ref, block, sems, step, to).start()
         else:
-            push(
-                all_ref.at[block], all_ref.at[block], sems.at[step], arrived.at[block], (to, fsdp)
-            ).wait_recv()
-            start(all_ref.at[block])
-
-    for step in range(n_ctx - 1):
-
-        @pl.when((ctx - step >= 0) & (ctx < n_ctx - 1))
-        def _():
-            hop(ctx - step, step, up, ctx + 1)
-
-        @pl.when((ctx + step < n_ctx) & (ctx > 0))
-        def _():
-            hop(ctx + step, step, down, ctx - 1)
-
-    def finish(block):
-        push(own_ref, all_ref.at[block], up.at[0], arrived.at[block], (ctx, fsdp)).wait_recv()
-
-    for other in range(1, n_ctx):
-
-        @pl.when(ctx == n_ctx - 1)
-        def _():
-            finish(n_ctx - 1 - other)
-
-        @pl.when(ctx == 0)
-        def _():
-            finish(other)
-
-    for step in range(n_ctx - 1):
-
-        @pl.when((ctx - step >= 0) & (ctx < n_ctx - 1))
-        def _():
-            push(own_ref, all_ref.at[0], up.at[step], arrived.at[0], (ctx, fsdp)).wait_send()
-
-        @pl.when((ctx + step < n_ctx) & (ctx > 0))
-        def _():
-            push(own_ref, all_ref.at[0], down.at[step], arrived.at[0], (ctx, fsdp)).wait_send()
+            self.copy(self.own_ref, block, sems, step, to).wait_recv()
+            self.copy(self.all_ref.at[block], block, sems, step, to).start()
+
+    def step(self, step):
+        @pl.when(self.going_up(step))
+        def _():
+            self.hop(self.ctx - step, step, self.up, self.ctx + 1)
+
+        @pl.when(self.going_down(step))
+        def _():
+            self.hop(self.ctx + step, step, self.down, self.ctx - 1)
+
+    def finish(self):
+        for other in range(1, self.n_ctx):
+
+            @pl.when(self.ctx == self.n_ctx - 1)
+            def _():
+                self.copy(self.own_ref, self.n_ctx - 1 - other, self.up, 0, self.ctx).wait_recv()
+
+            @pl.when(self.ctx == 0)
+            def _():
+                self.copy(self.own_ref, other, self.up, 0, self.ctx).wait_recv()
+
+        for step in range(self.n_ctx - 1):
+
+            @pl.when(self.going_up(step))
+            def _():
+                self.copy(self.own_ref, 0, self.up, step, self.ctx).wait_send()
+
+            @pl.when(self.going_down(step))
+            def _():
+                self.copy(self.own_ref, 0, self.down, step, self.ctx).wait_send()
 
 
 def first_gather(
@@ -329,7 +344,9 @@
         push(
             table_ref, table_all.at[ctx], table_send.at[i], table_arrived.at[ctx], (along(i), fsdp)
         ).start()
-    line_gather(n_ctx, ctx, fsdp, x_ref, x_all, up, down, arrived)
+    line = LineGather(n_ctx, ctx, fsdp, x_ref, x_all, up, down, arrived)
+    for step in range(n_ctx - 1):
+        line.step(step)
     for i in range(1, chips):
         owner = same_core(chips - i)
         packed_copy(packed_ref, owner, packed_send.at[i], sibling).wait_recv()
@@ -342,6 +359,7 @@
         push(
             table_ref, table_all.at[owner], table_send.at[i], table_arrived.at[owner], (owner, fsdp)
         ).wait()
+    line.finish()
     for i in range(chips):
         packed_copy(packed_ref, fsdp, packed_send.at[i], sibling).wait_send()
     for i in range(1, chips):
@@ -378,6 +396,616 @@
             flops=0, bytes_accessed=200 * 2**20, transcendentals=0
         ),
     )(x, table, packed)
+
+
+TILE = 512
+AUX = 128
+
+
+def expert_exchange(
+    n_ctx,
+    n_fsdp,
+    x_ref,
+    sel_ref,
+    selt_ref,
+    gate_ref,
+    up_ref,
+    down_ref,
+    grad_ref,
+    dealt_ref,
+    rows_ref,
+    back_ref,
+    part_ref,
+    inner_ref,
+    dg_ref,
+    du_ref,
+    y_ref,
+    dealt_all,
+    w_gate,
+    w_up,
+    w_down,
+    held,
+    staged,
+    rows_in,
+    grad_in,
+    inner_out,
+    dg_out,
+    du_out,
+    y_out,
+    back_in,
+    w_sems,
+    local,
+    held_send,
+    held_arrived,
+    rows_send,
+    rows_arrived,
+    back_send,
+    back_arrived,
+    part_send,
+    part_arrived,
+    dealt_send,
+    dealt_arrived,
+    out_sems,
+):
+    ctx, fsdp = lax.axis_index("ctx"), lax.axis_index("fsdp")
+    experts = n_ctx * n_fsdp
+    expert = ctx * n_fsdp + fsdp
+    width, hidden = w_gate.shape
+    wide = held.shape[2]
+    capacity = staged.shape[2]
+    half = n_fsdp // 2
+    tiles = [(at, min(TILE, wide - at)) for at in range(0, wide, TILE)]
+
+    def along(offset):
+        return lax.rem(ctx + offset, n_ctx)
+
+    def around(offset):
+        return lax.rem(fsdp + offset, n_fsdp)
+
+    greet(
+        [(along(i), fsdp) for i in range(1, n_ctx)] + [(ctx, around(i)) for i in range(1, n_fsdp)]
+    )
+    weights = [
+        pltpu.make_async_copy(gate_ref, w_gate, w_sems.at[0]),
+        pltpu.make_async_copy(up_ref, w_up, w_sems.at[1]),
+        pltpu.make_async_copy(down_ref, w_down, w_sems.at[2]),
+    ]
+    own = pltpu.make_async_copy(x_ref, held.at[ctx], local.at[0])
+    own.start()
+    for copy in weights:
+        copy.start()
+
+    def held_copy(step):
+        to = lax.rem(ctx + n_ctx - step, n_ctx)
+        return push(x_ref, held.at[ctx], held_send.at[step], held_arrived.at[ctx], (to, fsdp))
+
+    def rows_copy(step, group, offset):
+        to = around(offset)
+        return push(
+            staged.at[step, to],
+            rows_ref.at[fsdp, group],
+            rows_send.at[step, offset],
+            rows_arrived.at[group, fsdp],
+            (ctx, to),
+        )
+
+    def rows_kept(step, group):
+        return pltpu.make_async_copy(
+            staged.at[step, fsdp], rows_ref.at[fsdp, group], rows_arrived.at[group, fsdp]
+        )
+
+    def back_copy(step, group, offset):
+        to = around(offset)
+        return push(
+            staged.at[step, to],
+            back_ref.at[group, fsdp],
+            back_send.at[step, offset],
+            back_arrived.at[group, fsdp],
+            (ctx, to),
+        )
+
+    def back_kept(step, group):
+        return pltpu.make_async_copy(
+            staged.at[step, fsdp], back_ref.at[group, fsdp], back_arrived.at[group, fsdp]
+        )
+
+    def outputs(group):
+        return [
+            pltpu.make_async_copy(inner_out, inner_ref.at[:, group], out_sems.at[0]),
+            pltpu.make_async_copy(dg_out, dg_ref.at[:, group], out_sems.at[1]),
+            pltpu.make_async_copy(du_out, du_ref.at[:, group], out_sems.at[2]),
+            pltpu.make_async_copy(y_out, y_ref.at[:, group], out_sems.at[3]),
+        ]
+
+    def dispatch(step):
+        group = along(step)
+
+        @pl.when(step == 0)
+        def _():
+            own.wait()
+
+        @pl.when(step > 0)
+        def _():
+            push(
+                x_ref, held.at[group], held_send.at[step], held_arrived.at[group], (group, fsdp)
+            ).wait_recv()
+
+        @pl.when(step + 1 < n_ctx)
+        def _():
+            held_copy(step + 1).start()
+
+        for at, size in tiles:
+            picked = nn(sel_ref[group], held[group, :, at : at + size])
+            staged[step, :, :, at : at + size] = picked.astype(BF).reshape(n_fsdp, capacity, size)
+        rows_kept(step, group).start()
+        for offset in range(1, n_fsdp):
+            rows_copy(step, group, offset).start()
+
+    def compute(step):
+        group = along(step)
+        rows_kept(step, group).wait()
+        for offset in range(1, n_fsdp):
+            source = around(offset)
+            push(
+                staged.at[step, source],
+                rows_ref.at[source, group],
+                rows_send.at[step, offset],
+                rows_arrived.at[group, source],
+                (ctx, source),
+            ).wait_recv()
+        load_rows = pltpu.make_async_copy(rows_ref.at[:, group], rows_in, local.at[1])
+        load_inner = pltpu.make_async_copy(grad_ref.at[:, group], grad_in, local.at[2])
+        load_rows.start()
+        load_inner.start()
+
+        @pl.when(step == 0)
+        def _():
+            for copy in weights:
+                copy.wait()
+
+        @pl.when(step > 0)
+        def _():
+            for copy in outputs(group):
+                copy.wait()
+
+        for offset in range(1, n_fsdp):
+            rows_copy(step, group, offset).wait_send()
+        load_rows.wait()
+        load_inner.wait()
+        count = half * capacity
+        lane = lax.broadcasted_iota(jnp.int32, (count, AUX), 1)
+        high, low = lane == expert, lane == experts + expert
+
+        @pl.loop(0, 2)
+        def _(part):
+            sources = pl.ds(part * half, half)
+            rows = rows_in[sources, :, :width].reshape(count, width)
+            aux = rows_in[sources, :, width:].reshape(count, AUX).astype(F32)
+            gate = jnp.sum(jnp.where(high | low, aux, 0.0), axis=1, keepdims=True)
+            g = nn(rows, w_gate[...])
+            u = nn(rows, w_up[...])
+            s = jax.nn.sigmoid(g)
+            inner = g * s * u
+            d_inner = nt(grad_in[sources].reshape(count, width), w_down[...])
+            d_gate = jnp.sum(inner * d_inner, axis=1, keepdims=True)
+            d_inner = d_inner * gate
+            dg = (d_inner * u * s * (1.0 + g * (1.0 - s))).astype(BF)
+            du = (d_inner * g * s).astype(BF)
+            inner_out[sources] = (inner * gate).astype(BF).reshape(half, capacity, hidden)
+            dg_out[sources] = dg.reshape(half, capacity, hidden)
+            du_out[sources] = du.reshape(half, capacity, hidden)
+            rest = d_gate - d_gate.astype(BF).astype(F32)
+            staged[step, sources, :, width:] = (
+                jnp.where(high, d_gate, jnp.where(low, rest, 0.0))
+                .astype(BF)
+                .reshape(half, capacity, AUX)
+            )
+            for at in range(0, width, TILE):
+                grad = nt(dg, w_gate[at : at + TILE, :]) + nt(du, w_up[at : at + TILE, :])
+                staged[step, sources, :, at : at + TILE] = grad.astype(BF).reshape(
+                    half, capacity, TILE
+                )
+            low_inner = inner.astype(BF)
+            for at in range(0, width, TILE):
+                y = nn(low_inner, w_down[:, at : at + TILE]) * gate
+                y_out[sources, :, at : at + TILE] = y.astype(BF).reshape(half, capacity, TILE)
+
+        back_kept(step, group).start()
+        for offset in range(1, n_fsdp):
+            back_copy(step, group, offset).start()
+        for copy in outputs(group):
+            copy.start()
+
+    def combine(step):
+        group = along(step)
+        back_kept(step, group).wait()
+        for offset in range(1, n_fsdp):
+            source = around(offset)
+            push(
+                staged.at[step, source],
+                back_ref.at[group, source],
+                back_send.at[step, offset],
+                back_arrived.at[group, source],
+                (ctx, source),
+            ).wait_recv()
+        load = pltpu.make_async_copy(back_ref.at[group], back_in, local.at[1])
+        load.start()
+        load.wait()
+        for at, size in tiles:
+            back = back_in[:, :, at : at + size].reshape(n_fsdp * capacity, size)
+            held[group, :, at : at + size] = nn(selt_ref[group], back).astype(BF)
+
+        @pl.when(step == 0)
+        def _():
+            pltpu.make_async_copy(
+                held.at[group], part_ref.at[ctx], part_arrived.at[ctx]
+            ).start()
+
+        @pl.when(step > 0)
+        def _():
+            push(
+                held.at[group],
+                part_ref.at[ctx],
+                part_send.at[step],
+                part_arrived.at[ctx],
+                (group, fsdp),
+            ).start()
+
+    def dealt_copy(offset):
+        to = along(offset)
+        return push(
+            dealt_ref.at[to],
+            dealt_all.at[ctx],
+            dealt_send.at[offset],
+            dealt_arrived.at[ctx],
+            (to, fsdp),
+        )
+
+    dealt_kept = pltpu.make_async_copy(
+        dealt_ref.at[ctx], dealt_all.at[ctx], dealt_arrived.at[ctx]
+    )
+
+    @pl.loop(0, n_ctx + 3)
+    def _(tick):
+        @pl.when(tick < n_ctx)
+        def _():
+            dispatch(tick)
+
+        @pl.when(tick == n_ctx - 1)
+        def _():
+            dealt_kept.start()
+            for offset in range(1, n_ctx):
+                dealt_copy(offset).start()
+
+        @pl.when((tick >= 1) & (tick <= n_ctx))
+        def _():
+            compute(tick - 1)
+
+        @pl.when(tick >= 3)
+        def _():
+            combine(tick - 3)
+
+    pltpu.make_async_copy(held.at[ctx], part_ref.at[ctx], part_arrived.at[ctx]).wait()
+    for step in range(1, n_ctx):
+        other = along(step)
+        copy = push(
+            held.at[other], part_ref.at[other], part_send.at[step], part_arrived.at[other], (other, fsdp)
+        )
+        copy.wait()
+        held_copy(step).wait_send()
+    dealt_kept.wait()
+    for offset in range(1, n_ctx):
+        other = along(offset)
+        push(
+            dealt_ref.at[other],
+            dealt_all.at[other],
+            dealt_send.at[offset],
+            dealt_arrived.at[other],
+            (other, fsdp),
+        ).wait()
+    for step in range(n_ctx):
+        for offset in range(1, n_fsdp):
+            back_copy(step, along(step), offset).wait_send()
+    for copy in outputs(along(n_ctx - 1)):
+        copy.wait()
+
+
+def run_expert_exchange(n_ctx, n_fsdp, x, select, select_t, gate, up, down, grads, dealt):
+    anywhere, inside = pl.BlockSpec(memory_space=pl.ANY), pl.BlockSpec(memory_space=pltpu.VMEM)
+    span, wide = x.shape
+    width, hidden = gate.shape
+    capacity = grads.shape[2]
+    slots = (n_fsdp, n_ctx, capacity)
+    one = (n_fsdp, capacity)
+    dma, vmem, shape = pltpu.SemaphoreType.DMA, pltpu.VMEM, jax.ShapeDtypeStruct
+    return pl.pallas_call(
+        functools.partial(expert_exchange, n_ctx, n_fsdp),
+        in_specs=[anywhere, inside, inside] + [anywhere] * 5,
+        out_specs=[anywhere] * 8,
+        out_shape=[
+            shape(slots + (wide,), BF),
+            shape((n_ctx, n_fsdp, capacity, wide), BF),
+            shape((n_ctx, span, wide), BF),
+            shape(slots + (hidden,), BF),
+            shape(slots + (hidden,), BF),
+            shape(slots + (hidden,), BF),
+            shape(slots + (width,), BF),
+            shape(dealt.shape, BF),
+        ],
+        scratch_shapes=[
+            vmem((width, hidden), BF),
+            vmem((width, hidden), BF),
+            vmem((hidden, width), BF),
+            vmem((n_ctx, span, wide), BF),
+            vmem((n_ctx,) + one + (wide,), BF),
+            vmem(one + (wide,), BF),
+            vmem(one + (width,), BF),
+            vmem(one + (hidden,), BF),
+            vmem(one + (hidden,), BF),
+            vmem(one + (hidden,), BF),
+            vmem(one + (width,), BF),
+            vmem(one + (wide,), BF),
+            dma((3,)),
+            dma((3,)),
+            dma((n_ctx,)),
+            dma((n_ctx,)),
+            dma((n_ctx, n_fsdp)),
+            dma((n_ctx, n_fsdp)),
+            dma((n_ctx, n_fsdp)),
+            dma((n_ctx, n_fsdp)),
+            dma((n_ctx,)),
+            dma((n_ctx,)),
+            dma((n_ctx,)),
+            dma((n_ctx,)),
+            dma((4,)),
+        ],
+        compiler_params=pltpu.CompilerParams(
+            collective_id=2, has_side_effects=True, vmem_limit_bytes=60 * 2**20
+        ),
+        cost_estimate=pl.CostEstimate(
+            flops=12 * n_fsdp * n_ctx * capacity * width * hidden,
+            bytes_accessed=600 * 2**20,
+            transcendentals=0,
+        ),
+    )(x, select, select_t, gate, up, down, grads, dealt)
+
+
+def last_reduce(n_ctx, n_fsdp, chunks, dh_ref, *refs):
+    ctx, fsdp = lax.axis_index("ctx"), lax.axis_index("fsdp")
+    count = (len(refs) - 9) // 11
+    ins, refs = refs[:count], refs[count:]
+    total_ref, refs = refs[0], refs[1:]
+    alls, refs = refs[:count], refs[count:]
+    held, low, high, local, up_send, low_arrived, down_send, refs = refs[:7] + (refs[7:],)
+    high_arrived, refs = refs[0], refs[1:]
+    items = [refs[9 * i : 9 * i + 9] for i in range(count)]
+    chips, chip, core = n_fsdp // 2, fsdp // 2, lax.rem(fsdp, 2)
+    sibling = chip * 2 + 1 - core
+
+    def along(offset):
+        return lax.rem(ctx + offset, n_ctx)
+
+    def other_chip(offset):
+        return lax.rem(chip + offset, chips)
+
+    greet(
+        [(along(i), fsdp) for i in range(1, n_ctx)]
+        + [(ctx, other_chip(i) * 2 + core) for i in range(1, chips)]
+        + [(ctx, sibling)]
+    )
+    load = pltpu.make_async_copy(dh_ref, held, local.at[0])
+    load.start()
+    crossing, loads, lines = [], [], []
+    for at, (in_ref, all_ref, item) in enumerate(zip(ins, alls, items)):
+        mine, beside, landed, own, cross, sends, arrived, line_sems, line_arrived = item
+        crossing.append(
+            push(in_ref.at[:, 1 - core], beside, cross.at[0], cross.at[1], (ctx, sibling))
+        )
+        crossing[-1].start()
+        loads.append(pltpu.make_async_copy(in_ref.at[:, core], mine, local.at[1 + at]))
+        loads[-1].start()
+        lines.append(
+            LineGather(
+                n_ctx, ctx, fsdp, own, all_ref, line_sems.at[0], line_sems.at[1], line_arrived
+            )
+        )
+    load.wait()
+    size = held.shape[1] // chunks
+
+    def travel(landing, block, chunk, sends, arrived, to):
+        rows = pl.ds(chunk * size, size)
+        return push(
+            held.at[block, rows],
+            landing.at[block, rows],
+            sends.at[block, chunk],
+            arrived.at[block, chunk],
+            (to, fsdp),
+        )
+
+    def up(block, chunk, to):
+        return travel(low, block, chunk, up_send, low_arrived, to)
+
+    def down(block, chunk, to):
+        return travel(high, block, chunk, down_send, high_arrived, to)
+
+    def scatter(chunk):
+        rows = slice(chunk * size, (chunk + 1) * size)
+
+        def add(block, landing):
+            held[block, rows, :] = (
+                held[block, rows, :].astype(F32) + landing[block, rows, :].astype(F32)
+            ).astype(BF)
+
+        for step in range(n_ctx - 1):
+            above, below = n_ctx - 1 - step, step
+
+            @pl.when(ctx < above)
+            def _():
+                @pl.when(ctx > 0)
+                def _():
+                    up(above, chunk, ctx).wait_recv()
+                    add(above, low)
+
+                up(above, chunk, ctx + 1).start()
+
+            @pl.when(ctx > below)
+            def _():
+                @pl.when(ctx < n_ctx - 1)
+                def _():
+                    down(below, chunk, ctx).wait_recv()
+                    add(below, high)
+
+                down(below, chunk, ctx - 1).start()
+
+    def settle(chunk):
+        rows = slice(chunk * size, (chunk + 1) * size)
+        total_ref[rows, :] = held[ctx, rows, :].astype(F32)
+
+        @pl.when(ctx > 0)
+        def _():
+            up(ctx, chunk, ctx).wait_recv()
+            total_ref[rows, :] += low[ctx, rows, :].astype(F32)
+
+        @pl.when(ctx < n_ctx - 1)
+        def _():
+            down(ctx, chunk, ctx).wait_recv()
+            total_ref[rows, :] += high[ctx, rows, :].astype(F32)
+
+    def chip_copy(item, offset):
+        mine, beside, landed, own, cross, sends, arrived, line_sems, line_arrived = item
+        to = other_chip(offset)
+        return push(
+            mine.at[to], landed.at[chip], sends.at[offset], arrived.at[chip], (ctx, to * 2 + core)
+        )
+
+    scatter(0)
+    scatter(1)
+    for crossed, loaded, item in zip(crossing, loads, items):
+        mine, beside = item[:2]
+        loaded.wait()
+        crossed.wait_recv()
+        for offset in range(1, chips + 1):
+            to = other_chip(offset)
+            mine[to] = (mine[to].astype(F32) + beside[to].astype(F32)).astype(BF)
+            if offset < chips:
+                chip_copy(item, offset).start()
+    for chunk in range(2, chunks):
+        scatter(chunk)
+    keeps = []
+    for at, (item, line, all_ref) in enumerate(zip(items, lines, alls)):
+        mine, beside, landed, own, cross, sends, arrived, line_sems, line_arrived = item
+        total = mine[chip].astype(F32)
+        for offset in range(1, chips):
+            source = other_chip(offset)
+            push(
+                mine.at[source], landed.at[source], sends.at[offset], arrived.at[source], (ctx, sibling)
+            ).wait_recv()
+            total = total + landed[source].astype(F32)
+        own[...] = total.astype(BF)
+        line.step(0)
+        keeps.append(pltpu.make_async_copy(own, all_ref.at[ctx], local.at[1 + at]))
+        keeps[-1].start()
+    for step in range(1, n_ctx - 1):
+        for line in lines:
+            line.step(step)
+    for chunk in range(chunks):
+        settle(chunk)
+    for crossed, keep, line, item in zip(crossing, keeps, lines, items):
+        crossed.wait_send()
+        keep.wait()
+        line.finish()
+        for offset in range(1, chips):
+            chip_copy(item, offset).wait_send()
+    for chunk in range(chunks):
+        for step in range(n_ctx - 1):
+            above, below = n_ctx - 1 - step, step
+
+            @pl.when(ctx < above)
+            def _():
+                up(above, chunk, ctx).wait_send()
+
+            @pl.when(ctx > below)
+            def _():
+                down(below, chunk, ctx).wait_send()
+
+
+def run_last_reduce(n_ctx, n_fsdp, d_hidden, grads):
+    anywhere = pl.BlockSpec(memory_space=pl.ANY)
+    dma, vmem, shape = pltpu.SemaphoreType.DMA, pltpu.VMEM, jax.ShapeDtypeStruct
+    chunks, chips = 4, n_fsdp // 2
+    _, span, width = d_hidden.shape
+    grads = [grad.reshape((chips, 2, -1) + grad.shape[-1:]) for grad in grads]
+    blocks = [grad.shape[2:] for grad in grads]
+    scratch = [
+        vmem(d_hidden.shape, BF),
+        vmem(d_hidden.shape, BF),
+        vmem(d_hidden.shape, BF),
+        dma((1 + len(grads),)),
+        dma((n_ctx, chunks)),
+        dma((n_ctx, chunks)),
+        dma((n_ctx, chunks)),
+        dma((n_ctx, chunks)),
+    ]
+    for block in blocks:
+        scratch += [
+            vmem((chips,) + block, BF),
+            vmem((chips,) + block, BF),
+            vmem((chips,) + block, BF),
+            vmem(block, BF),
+            dma((2,)),
+            dma((chips,)),
+            dma((chips,)),
+            dma((2, n_ctx)),
+            dma((n_ctx,)),
+        ]
+    return pl.pallas_call(
+        functools.partial(last_reduce, n_ctx, n_fsdp, chunks),
+        in_specs=[anywhere] * (1 + len(grads)),
+        out_specs=[pl.BlockSpec(memory_space=pltpu.VMEM)] + [anywhere] * len(grads),
+        out_shape=[shape((span, width), F32)] + [shape((n_ctx,) + block, BF) for block in blocks],
+        scratch_shapes=scratch,
+        compiler_params=pltpu.CompilerParams(
+            collective_id=3, has_side_effects=True, vmem_limit_bytes=60 * 2**20
+        ),
+        cost_estimate=pl.CostEstimate(flops=0, bytes_accessed=300 * 2**20, transcendentals=0),
+    )(d_hidden, *grads)
+
+
+def widen_columns(in_ref, out_ref):
+    out_ref[...] = in_ref[0].astype(F32)
+
+
+def run_widen_columns(blocks, columns):
+    n, rows, _ = blocks.shape
+    return pl.pallas_call(
+        widen_columns,
+        grid=(n,),
+        in_specs=[pl.BlockSpec((1, rows, columns), lambda i: (i, 0, 0))],
+        out_specs=pl.BlockSpec((rows, columns), lambda i: (0, i)),
+        out_shape=jax.ShapeDtypeStruct((rows, n * columns), F32),
+    )(blocks)
+
+
+def pick_rows(select_ref, rows_ref, out_ref):
+    shape = out_ref.shape
+    for at in range(0, shape[3], TILE):
+        picked = nn(select_ref[0], rows_ref[0, :, at : at + TILE])
+        out_ref[:, 0, :, at : at + TILE] = picked.astype(BF).reshape(shape[0], shape[2], TILE)
+
+
+def run_pick_rows(select, rows, n_fsdp):
+    n_ctx, count, span = select.shape
+    capacity, width = count // n_fsdp, rows.shape[2]
+    return pl.pallas_call(
+        pick_rows,
+        grid=(n_ctx,),
+        in_specs=[
+            pl.BlockSpec((1, count, span), lambda g: (g, 0, 0)),
+            pl.BlockSpec((1, span, width), lambda g: (g, 0, 0)),
+        ],
+        out_specs=pl.BlockSpec((n_fsdp, 1, capacity, width), lambda g: (0, g, 0, 0)),
+        out_shape=jax.ShapeDtypeStruct((n_fsdp, n_ctx, capacity, width), BF),
+    )(select, rows)
 
 
 def on_device(
@@ -419,10 +1047,6 @@
     def scatter_ctx(array):
         return lax.psum_scatter(array.astype(BF), "ctx", scatter_dimension=0, tiled=True)
 
-    def scatter_fsdp(array):
-        parts = route(array.astype(BF).reshape((n_fsdp, -1) + array.shape[1:]))
-        return jnp.sum(parts.astype(F32), axis=0).astype(BF)
-
     def route(rows):
         return lax.all_to_all(rows, "fsdp", split_axis=0, concat_axis=0, tiled=True)
 
@@ -449,7 +1073,11 @@
     table = jnp.concatenate(
         [expert_ids[0].T, drop_order[0], jnp.zeros((7, span), jnp.int32)], axis=0
     )
+    grad_all = gather_ctx(cotangent[0])
     inputs_all, tables, packed_all = run_first_gather(n_ctx, n_fsdp, inputs[0], table, packed)
+    w_out, grad_all = lax.optimization_barrier((w_out, grad_all))
+    out_all = lax.all_gather(w_out, "fsdp", axis=0, tiled=True)
+    out_here = lax.dynamic_slice_in_dim(out_all, ctx * q_width, q_width, axis=0)
     inputs_all = inputs_all.reshape(length, width)
     packed_all = packed_all.reshape(width, qkv_width + extra_width)
     w_qkv = packed_all[:, :qkv_width]
@@ -477,11 +1105,15 @@
     select = (
         place[:, :, None, :] == jnp.arange(capacity, dtype=jnp.int32)[None, None, :, None]
     ).astype(BF)
-    chosen = jnp.any(
-        named[:, :, :, None] == jnp.arange(experts, dtype=jnp.int32), axis=1
-    ).reshape(length, experts)
+
+    fused = capacity % 16 == 0 and 2 * experts <= AUX
+    select_rows = select.reshape(n_ctx, n_fsdp * capacity, span)
 
     def dispatch(rows):
+        if fused:
+            return route(
+                run_pick_rows(select_rows, rows.reshape(n_ctx, span, width), n_fsdp)
+            ).reshape(slots, width)
         picked = jnp.einsum(
             "gjkt,gtd->jgkd", select, rows.reshape(n_ctx, span, width), preferred_element_type=F32
         ).astype(BF)
@@ -492,22 +1124,6 @@
         return jnp.einsum("gjkt,jgkd->gtd", select, back, preferred_element_type=F32).reshape(
             length, width
         )
-
-    fsdp = lax.axis_index("fsdp")
-    chips = n_fsdp // 2
-    half = jnp.where(fsdp // 2 == ctx, w_out, jnp.zeros_like(w_out))
-    for offset in range(1, chips):
-        pairs = [
-            (c * n_fsdp + 2 * c + core, c * n_fsdp + 2 * (c ^ offset) + core)
-            for c in range(n_ctx)
-            for core in range(2)
-        ]
-        half = half + lax.ppermute(w_out, ("ctx", "fsdp"), pairs)
-    other = lax.ppermute(half, "fsdp", [(f, f ^ 1) for f in range(n_fsdp)])
-    first = fsdp % 2 == 0
-    out_here = jnp.concatenate(
-        [jnp.where(first, half, other), jnp.where(first, other, half)], axis=0
-    )
 
     x_all = inputs_all.astype(F32)
     r_all = inverse_rms(x_all)
@@ -519,60 +1135,96 @@
     sine = jnp.concatenate([-jnp.sin(angles), jnp.sin(angles)], axis=1)
     own_blocks = jnp.broadcast_to(block_ids, (8, length))
     key_blocks = block_ids.reshape(length, 1)
-    mixed, totals = run_attention(qkv, heads, cosine, sine, gains, own_blocks, key_blocks)
-    grad_own, qkv = lax.optimization_barrier((cotangent[0], qkv))
-    grad_all = gather_ctx(grad_own)
+    mixed, totals, dealt = run_attention(
+        qkv, heads, n_ctx, cosine, sine, gains, own_blocks, key_blocks
+    )
+    piece = QUERY_HEADS * HEAD_SIZE // experts
+    groups = n_fsdp // n_ctx
+    if piece != HEAD_SIZE:
+        dealt = mixed.reshape(length, groups, n_ctx, piece).transpose(2, 0, 1, 3)
+        dealt = dealt.reshape(n_ctx, length, groups * piece)
     grad_rows = dispatch(grad_all)
-
-    mixed, grad_all = lax.optimization_barrier((mixed, grad_all))
     attn_out = scatter_ctx(nn(mixed, out_here))
 
     x = inputs[0].astype(F32)
     resid = x + attn_out.astype(F32)
     r_ffn = inverse_rms(resid)
-    normed = gather_ctx((resid * r_ffn * gain_ffn).astype(BF))
-    normed, grad_rows = lax.optimization_barrier((normed, grad_rows))
-    grad_inner = nt(grad_rows, expert_down[0])
-    logits = nt(normed, router_t)
-    gates = jax.nn.softmax(jnp.where(chosen, logits, -jnp.inf), axis=-1)
-    gates_here = lax.dynamic_slice_in_dim(gates, ctx * n_fsdp, n_fsdp, axis=1)
-    gates_here = gates_here.reshape(n_ctx, span, n_fsdp).transpose(0, 2, 1)
-    slot_gates = jnp.sum(select.astype(F32) * gates_here[:, :, None, :], axis=-1)
-    slot_gates = route(slot_gates.transpose(1, 0, 2)).reshape(slots, 1)
-    rows = dispatch(normed)
-
-    piece = QUERY_HEADS * HEAD_SIZE // experts
-    groups = n_fsdp // n_ctx
-    dealt = mixed.reshape(length, groups, n_ctx, piece).transpose(2, 0, 1, 3)
-    dealt = lax.all_to_all(
-        dealt.reshape(n_ctx, length, groups * piece), "ctx", split_axis=0, concat_axis=0, tiled=True
-    )
-    rows, dealt = lax.optimization_barrier((rows, dealt))
-
-    g = nn(rows, expert_gate[0])
-    u = nn(rows, expert_up[0])
-    s = jax.nn.sigmoid(g)
-    inner = g * s * u
-    inner_low = inner.astype(BF)
-    slot_dgates = jnp.sum(inner * grad_inner, axis=-1).reshape(n_fsdp, n_ctx, capacity)
-    d_inner = grad_inner * slot_gates
-    dg = (d_inner * u * s * (1.0 + g * (1.0 - s))).astype(BF)
-    du = (d_inner * g * s).astype(BF)
-    d_rows = (nt(dg, expert_gate[0]) + nt(du, expert_up[0])).astype(BF)
-    y = (nn(inner_low, expert_down[0]) * slot_gates).astype(BF)
+    normed = (resid * r_ffn * gain_ffn).astype(BF)
+    if fused:
+        chosen = jnp.any(
+            expert_ids[0][:, :, None] == jnp.arange(experts, dtype=jnp.int32), axis=1
+        )
+        logits = nt(normed, router_t)
+        gates = jax.nn.softmax(jnp.where(chosen, logits, -jnp.inf), axis=-1)
+        high = lax.reduce_precision(gates, 8, 7)
+        payload = jnp.concatenate(
+            [
+                normed,
+                high.astype(BF),
+                (gates - high).astype(BF),
+                jnp.zeros((span, AUX - 2 * experts), BF),
+            ],
+            axis=1,
+        )
+        rows, _, parts, inner_low, dg, du, y, dealt = run_expert_exchange(
+            n_ctx,
+            n_fsdp,
+            payload,
+            select_rows,
+            select_rows.swapaxes(1, 2),
+            expert_gate[0],
+            expert_up[0],
+            expert_down[0],
+            grad_rows.reshape(n_fsdp, n_ctx, capacity, width),
+            dealt,
+        )
+        rows = rows.reshape(slots, width + AUX)[:, :width]
+        inner_low, dg, du = (array.reshape(slots, -1) for array in (inner_low, dg, du))
+        y = y.reshape(slots, width)
+        parts = jnp.sum(parts.astype(F32), axis=0)
+        d_gates = parts[:, width : width + experts] + parts[:, width + experts : width + 2 * experts]
+        d_logits = gates * (d_gates - jnp.sum(gates * d_gates, axis=-1, keepdims=True))
+        d_logits = d_logits.astype(BF)
+        d_normed = parts[:, :width] + nn(d_logits, router_t)
+    else:
+        dealt = lax.all_to_all(dealt, "ctx", split_axis=0, concat_axis=0, tiled=True)
+        chosen = jnp.any(
+            named[:, :, :, None] == jnp.arange(experts, dtype=jnp.int32), axis=1
+        ).reshape(length, experts)
+        normed = gather_ctx(normed)
+        normed, grad_rows = lax.optimization_barrier((normed, grad_rows))
+        grad_inner = nt(grad_rows, expert_down[0])
+        logits = nt(normed, router_t)
+        gates = jax.nn.softmax(jnp.where(chosen, logits, -jnp.inf), axis=-1)
+        gates_here = lax.dynamic_slice_in_dim(gates, ctx * n_fsdp, n_fsdp, axis=1)
+        gates_here = gates_here.reshape(n_ctx, span, n_fsdp).transpose(0, 2, 1)
+        slot_gates = jnp.sum(select.astype(F32) * gates_here[:, :, None, :], axis=-1)
+        slot_gates = route(slot_gates.transpose(1, 0, 2)).reshape(slots, 1)
+        rows = dispatch(normed)
+        g = nn(rows, expert_gate[0])
+        u = nn(rows, expert_up[0])
+        s = jax.nn.sigmoid(g)
+        inner = g * s * u
+        slot_dgates = jnp.sum(inner * grad_inner, axis=-1).reshape(n_fsdp, n_ctx, capacity)
+        d_inner = grad_inner * slot_gates
+        dg = (d_inner * u * s * (1.0 + g * (1.0 - s))).astype(BF)
+        du = (d_inner * g * s).astype(BF)
+        d_rows = (nt(dg, expert_gate[0]) + nt(du, expert_up[0])).astype(BF)
+        y = (nn(inner.astype(BF), expert_down[0]) * slot_gates).astype(BF)
+        inner_low = (inner * slot_gates).astype(BF)
+        d_gates = jnp.einsum(
+            "gjkt,jgk->gjt", select.astype(F32), route(slot_dgates), precision=lax.Precision.HIGHEST
+        )
+        weighted = (d_gates * gates_here).transpose(0, 2, 1).reshape(length, n_fsdp)
+        d_logits = lax.dynamic_update_slice_in_dim(
+            jnp.zeros((length, experts), F32), weighted, ctx * n_fsdp, axis=1
+        ) - gates * jnp.sum(weighted, axis=1, keepdims=True)
+        d_logits = d_logits.astype(BF)
+        d_normed = scatter_ctx(combine(d_rows) + nn(d_logits, router_t)).astype(F32)
+
     gate_grad = tn(rows, dg)
     up_grad = tn(rows, du)
-    down_grad = tn((inner * slot_gates).astype(BF), grad_rows)
-
-    d_gates = jnp.einsum(
-        "gjkt,jgk->gjt", select.astype(F32), route(slot_dgates), precision=lax.Precision.HIGHEST
-    )
-    weighted = (d_gates * gates_here).transpose(0, 2, 1).reshape(length, n_fsdp)
-    d_logits = lax.dynamic_update_slice_in_dim(
-        jnp.zeros((length, experts), F32), weighted, ctx * n_fsdp, axis=1
-    ) - gates * jnp.sum(weighted, axis=1, keepdims=True)
-    d_logits = d_logits.astype(BF)
-    d_normed = scatter_ctx(combine(d_rows) + nn(d_logits, router_t)).astype(F32)
+    down_grad = tn(inner_low, grad_rows)
     router_grad = tn(normed, d_logits)
 
     grad = cotangent[0].astype(F32)
@@ -588,8 +1240,6 @@
     output = (resid + moe).astype(BF)[None]
 
     out_grad = jnp.einsum("ntk,td->nkd", dealt, d_attn, preferred_element_type=F32).astype(BF)
-    out_grad = scatter_fsdp(out_grad.reshape(n_fsdp * piece, width))
-    out_grad = gather_ctx(out_grad).astype(F32)
 
     dq, dkv, dgains = run_attention_back(
         qkv, d_mixed, totals, heads, cosine, sine, gains, own_blocks, key_blocks
@@ -598,11 +1248,6 @@
     d_qkv = jnp.concatenate([dq, dkv], axis=1)
     d_hidden = nt(d_qkv, w_qkv)
     attn_gain_grad = jnp.sum(d_hidden * x_all * r_all, axis=0)
-    d_hidden = scatter_ctx(d_hidden).astype(F32)
-    r_attn = inverse_rms(x)
-    n = d_hidden * gain_attn
-    input_grad = d_resid + r_attn * n - x * r_attn**3 * jnp.mean(n * x, axis=-1, keepdims=True)
-    input_grad = input_grad.astype(BF)[None]
 
     def spread(vector):
         parts = vector.reshape(n_fsdp, HEAD_SIZE // n_fsdp)
@@ -619,13 +1264,20 @@
         ],
         axis=1,
     )
-    shared_grad = jnp.concatenate(
-        [scatter_fsdp(tn(hidden, d_qkv)), scatter_fsdp(extra_grad)], axis=1
-    )
-    shared_grad = lax.all_gather(shared_grad, "ctx", axis=0, tiled=False)
-    query_grad = (
-        shared_grad[:, :, :q_width].transpose(1, 0, 2).reshape(own_rows, n_ctx * q_width).astype(F32)
-    )
+    d_hidden, shared_grad, rest, out_grad = run_last_reduce(
+        n_ctx,
+        n_fsdp,
+        d_hidden.astype(BF).reshape(n_ctx, span, width),
+        [tn(hidden, d_qkv).astype(BF), extra_grad, out_grad.reshape(n_fsdp * piece, width)],
+    )
+    out_grad = out_grad.reshape(n_ctx * piece, width).astype(F32)
+    rest = rest.astype(F32).sum(axis=0)
+    r_attn = inverse_rms(x)
+    n = d_hidden * gain_attn
+    input_grad = d_resid + r_attn * n - x * r_attn**3 * jnp.mean(n * x, axis=-1, keepdims=True)
+    input_grad = input_grad.astype(BF)[None]
+
+    query_grad = run_widen_columns(shared_grad, q_width)
 
     def kv_grad(at):
         parts = shared_grad[:, :, at : at + HEAD_SIZE].astype(F32)
@@ -633,7 +1285,6 @@
         return parts.transpose(1, 0, 2).reshape(own_rows, KEY_VALUE_HEADS * HEAD_SIZE)
 
     key_grad, value_grad = kv_grad(q_width), kv_grad(q_width + HEAD_SIZE)
-    rest = shared_grad[:, :, qkv_width:].astype(F32).sum(axis=0)
     head_rows = HEAD_SIZE // n_fsdp
     return (
         output,

time: 1380 us -> 1120 us (0.81)
  Pallas kernels: 149 us -> 612 us
  waiting for transfers between devices: 701 us -> 266 us
  matrix products: 243 us -> 114 us
  blocking collectives: 52.7 us -> 0 us
  starting transfers between devices: 66.8 us -> 15.9 us
  local copies, waits for them, and re-layouts: 83.5 us -> 40.4 us
  other arithmetic: 61.3 us -> 37.2 us
    pallas_call x0 -> x4, Pallas kernels: none -> 471 us  [the longest x1 290 us: run_expert_exchange(): pl.pallas_call(functools.partial(expert_exchange, n_ctx, n_fsdp), in_spec...]
    all_to_all x8 -> x2, waiting for transfers between devices: 401 us -> 132 us  [route(): return lax.all_to_all(rows, 'fsdp', split_axis=0, concat_axis=0, tiled=True)]
    ppermute x4 -> x0, waiting for transfers between devices: 83.5 us -> none  [the longest x3 83.5 us: on_device(): half = half + lax.ppermute(w_out, ('ctx', 'fsdp'), pairs)]
    all_gather x4 -> x2, waiting for transfers between devices: 24.8 us -> 85.1 us  [gather_ctx(): return lax.all_gather(array, 'ctx', axis=0, tiled=True)]
    reduce_scatter x4 -> x2, waiting for transfers between devices: 108 us -> 48.3 us  [scatter_ctx(): lax.psum_scatter(array.astype(BF), 'ctx', scatter_dimension=0, tiled=True)]
    all_gather x1, waiting for transfers between devices: 57.1 us -> 0.01 us  [on_device(): out_all = lax.all_gather(w_out, 'fsdp', axis=0, tiled=True)]
    all_to_all x1 -> x0, blocking collectives: 52.7 us -> none  [route(): return lax.all_to_all(rows, 'fsdp', split_axis=0, concat_axis=0, tiled=True)]
    dot_general x6 -> x3, matrix products: 71.7 us -> 21.5 us  [nt(): lax.dot_general(a, b, (((1,), (1,)), ((), ())), preferred_element_type=F32)]
  transfers between devices with their start and end apart: 22 -> 7, of which waited for: 14 -> 4; matrix products, arithmetic and copies ran while one was open for 18% -> 16% of each run, Pallas kernels for 5% -> 29%
where the time goes in v2:
time: 1120 us; the launch traced here: 1100 us
  Pallas kernels  612 us (55%)
  waiting for transfers between devices  266 us (24%)
  matrix products  114 us (10%)
  local copies, waits for them, and re-layouts  40.4 us (4%)
  other arithmetic  37.2 us (3%)
  starting transfers between devices  15.9 us (1%)
  between operations  14.9 us (1%)
    pallas_call x1, Pallas kernels, run_expert_exchange(): pl.pallas_call(functools.partial(expert_exchange, n_ctx, n_fsdp), in_spec...  290 us
    pallas_call x1, Pallas kernels, run_last_reduce(): pl.pallas_call(functools.partial(last_reduce, n_ctx, n_fsdp, chunks), in_...  169 us
    all_to_all x2, waiting for transfers between devices, route(): return lax.all_to_all(rows, 'fsdp', split_axis=0, concat_axis=0, tiled=True)  132 us
    all_gather x2, waiting for transfers between devices, gather_ctx(): return lax.all_gather(array, 'ctx', axis=0, tiled=True)  85.1 us
    pallas_call x1, Pallas kernels, run_first_gather(): pl.pallas_call(functools.partial(first_gather, n_ctx, n_fsdp), in_specs=[...  74.4 us
    dot_general x5, matrix products, tn(): lax.dot_general(a, b, (((0,), (0,)), ((), ())), preferred_element_type=F32)  49.6 us
    reduce_scatter x2, waiting for transfers between devices, scatter_ctx(): lax.psum_scatter(array.astype(BF), 'ctx', scatter_dimension=0, tiled=True)  48.3 us
    pallas_call x1, Pallas kernels, run_attention_back(): pl.pallas_call(functools.partial(attention_backward, heads), grid=(heads,...  37.3 us
  transfers between devices with their start and end apart: 7, of which 4 were waited for; matrix products, arithmetic and copies ran while one was open for 16% of the time, Pallas kernels for 29%

profile of v2, /device:TPU:0, one launch (start us, length us, event | category | flops | bytes accessed | tf_op | source)
XLA Modules:
  0.0 1100.6 jit_solution(15987236842454130567)
XLA Ops:
  8.0 85.1 %all-gather.9.cloned.1.call-done = bf16[1,1024,2048]{2,1,0:T(8,128)(2,1)} async-done(((bf16[1,256,2048]{2,1,0:T(8,128)(2,1)}), bf16[1,1024,2048]{2,1,0:T(8,128)(2,1)}) %all-gather.9.cloned.1.call-update) | async-done | bytes 4194320 | tf_op jit(solution)/shard_map/all_gather | solution.py:1045
  94.9 1.1 concatenate.23.packed_ref
  96.7 74.4 %shard_map.272 = (bf16[4,256,2048]{2,1,0:T(8,128)(2,1)}, s32[4,16,256]{2,1,0:T(8,128)}, bf16[8,256,1408]{2,1,0:T(8,128)(2,1)}) custom-call(bf16[256,2048]{1,0:T(8,128)(2,1)} %bitcast.123, s32[16,256]{1,0:T(8,128)} %add_add_fusion.table_ref, bf16[256,1408]{1,0:T(8,128)(2,1)} %concatenate.23.packed_ref), custom_call_target="tpu_custom_call" | custom-call | bytes 209715200 | tf_op jit(solution)/shard_map/pallas_call | solution.py:374
  172.4 3.3 fusion.6
  176.0 2.0 fusion.50
  179.0 3.3 fusion.8
  182.4 11.3 %fusion.13.q_ref.k_ref.v_ref = f32[1024,1280]{1,0:T(8,128)} fusion(bf16[1024,2048]{1,0:T(8,128)(2,1)S(1)} %fusion.8, bf16[2048,1408]{1,0:T(8,128)(2,1)} %bitcast.148), kind=kOutput, calls=%fused_computation.19 | convolution fusion | flops 5368709120 | bytes 14680064 | tf_op jit(solution)/shard_map/dot_general | solution.py:29
  193.7 29.4 %shard_map.273 = (bf16[1024,1024]{1,0:T(8,128)(2,1)S(1)}, f32[8,8,1024]{2,1,0:T(8,128)S(1)}, bf16[4,1024,256]{2,1,0:T(8,128)(2,1)S(1)}) custom-call(f32[1024,1280]{1,0:T(8,128)} %fusion.13.q_ref.k_ref.v_ref, f32[1024,1280]{1,0:T(8,128)} %fusion.13.q_ref.k_ref.v_ref, f32[1024,1280]{1,0:T(8,128)} %fusion.13.q_ref.k_ref.v_ref, f32[1024,128]{1,0:T(8,128)S(1)} %copy.161.cos_ref, ...), custom_call_target="tpu_custom_call" | custom-call | flops 4294967296 | bytes 8388608 | tf_op jit(solution)/shard_map/pallas_call | solution.py:165
  223.7 1.3 copy-done.8
  225.0 8.5 convolution_convert_fusion.1
  234.8 1.7 eq.56
  236.5 3.2 copy.165
  239.8 2.0 compare_convert_fusion
  241.8 1.5 copy.167.select_ref.sel_ref
  243.3 8.3 shard_map.274
  251.6 5.2 all-to-all-start
  257.6 3.2 fusion.76.selt_ref
  260.8 48.3 %reduce-scatter.3.cloned.1.call-done = bf16[256,2048]{1,0:T(8,128)(2,1)} async-done(((bf16[1024,2048]{1,0:T(8,128)(2,1)}), bf16[256,2048]{1,0:T(8,128)(2,1)}) %reduce-scatter.3.cloned.1.call-update) | async-done | bytes 1048592 | tf_op jit(solution)/shard_map/reduce_scatter | solution.py:1048
  309.1 2.4 fusion.31
  313.6 1.4 fusion.59
  317.2 3.1 concatenate.26.x_ref
  320.3 53.0 %all-to-all-done.grad_ref = bf16[8,4,80,2048]{3,2,1,0:T(8,128)(2,1)} async-done(((bf16[8,4,80,2048]{3,2,1,0:T(8,128)(2,1)}), bf16[8,4,80,2048]{3,2,1,0:T(8,128)(2,1)}, u32[]{:S(2)}, u32[]{:S(2)}) %all-to-all-start) | async-done | bytes 10485792 | tf_op jit(solution)/shard_map/all_to_all | solution.py:1051
  373.3 290.1 %shard_map.275 = (bf16[8,4,80,2176]{3,2,1,0:T(8,128)(2,1)}, bf16[4,8,80,2176]{3,2,1,0:T(8,128)(2,1)}, bf16[4,256,2176]{2,1,0:T(8,128)(2,1)}, bf16[8,4,80,768]{3,...) custom-call(bf16[256,2176]{1,0:T(8,128)(2,1)} %concatenate.26.x_ref,, ...), custom_call_target="tpu_custom_call" | custom-call | flops 48318382080 | bytes 629145600 | tf_op jit(solution)/shard_map/pallas_call | solution.py:721
  663.4 10.4 all-to-all-start.1
  673.8 3.1 convert_reduce_fusion
  677.5 3.3 multiply_reduce_fusion
  680.9 3.4 fusion.58
  684.5 14.3 %fusion.22 = f32[1,2048,768]{2,1,0:T(8,128)} fusion(bf16[2560,768]{1,0:T(8,128)(2,1)} %bitcast.166, bf16[2560,2176]{1,0:T(8,128)(2,1)} %bitcast.163), kind=kOutput, calls=%fused_computation.25 | convolution fusion | flops 8053063680 | bytes 20709376 | tf_op jit(solution)/shard_map/dot_general | solution.py:33
  698.8 13.1 %fusion.19 = f32[1,2048,768]{2,1,0:T(8,128)} fusion(bf16[2560,768]{1,0:T(8,128)(2,1)S(1)} %bitcast.165, bf16[2560,2176]{1,0:T(8,128)(2,1)} %bitcast.164), kind=kOutput, calls=%fused_computation.24 | convolution fusion | flops 8053063680 | bytes 20709376 | tf_op jit(solution)/shard_map/dot_general | solution.py:33
  711.9 79.0 %all-to-all-done.1 = bf16[8,4,80,2048]{3,2,1,0:T(8,128)(2,1)} async-done(((bf16[8,4,80,2048]{3,2,1,0:T(8,128)(2,1)}), bf16[8,4,80,2048]{3,2,1,0:T(8,128)(2,1)}, u32[]{:S(2)}, u32[]{:S(2)}) %all-to-all-start.1) | async-done | bytes 10485792 | tf_op jit(solution)/shard_map/all_to_all | solution.py:1051
  790.9 9.4 bitcast_convert_fusion
  800.4 14.3 %convolution_bitcast_fusion = f32[1,768,2048]{2,1,0:T(8,128)} fusion(bf16[8,4,80,768]{3,2,1,0:T(8,128)(2,1)} %get-tuple-element.63, bf16[8,4,80,2048]{3,2,1,0:T(8,128)(2,1)} %all-to-all-done.grad_ref), kind=kOutput, calls=%fused_computation.23 | convolution fusion | flops 8053063680 | bytes 20709376 | tf_op jit(solution)/shard_map/dot_general | solution.py:33
  816.3 9.4 fusion.37.grad_ref
  825.7 37.3 %shard_map.276 = (bf16[1024,1024]{1,0:T(8,128)(2,1)S(1)}, bf16[1024,256]{1,0:T(8,128)(2,1)S(1)}, f32[8,128]{1,0:T(8,128)S(1)}) custom-call(f32[1024,1280]{1,0:T(8,128)} %fusion.13.q_ref.k_ref.v_ref, f32[1024,1280]{1,0:T(8,128)} %fusion.13.q_ref.k_ref.v_ref, f32[1024,1280]{1,0:T(8,128)} %fusion.13.q_ref.k_ref.v_ref, bf16[1024,1024]{1,0:T(8,128)(2,1)} %fusion.37.grad_ref, ...), custom_call_target="tpu_custom_call" | custom-call | flops 10737418240 | bytes 10485760 | tf_op jit(solution)/shard_map/pallas_call | solution.py:195
  863.2 1.9 copy-done.11
  865.2 10.8 fusion.10
  878.8 4.1 concatenate.28
  882.9 9.6 fusion.25
  892.5 7.6 convolution_convert_fusion
  900.0 168.7 %shard_map.277 = (f32[256,2048]{1,0:T(8,128)}, bf16[4,256,1280]{2,1,0:T(8,128)(2,1)}, bf16[4,256,128]{2,1,0:T(8,128)(2,1)}, bf16[4,128,2048]{2,1,0:T(8,128)(2,1)}) custom-call(bf16[4,256,2048]{2,1,0:T(8,128)(2,1)} %bitcast.126, bf16[4,2,256,1280]{3,2,1,0:T(8,128)(2,1)} %bitcast.125, bf16[4,2,256,128]{3,2,1,0:T(8,128)(2,1)} %bitcast.131, ...), custom_call_target="tpu_custom_call" | custom-call | bytes 314572800 | tf_op jit(solution)/shard_map/pallas_call | solution.py:961
  1068.8 4.2 shard_map.278
  1073.0 2.1 convert_bitcast_fusion
  1075.1 2.2 copy.177
  1077.3 2.0 copy.179
  1079.3 2.0 copy.178
  1081.3 2.0 copy.180
  1086.1 2.7 bitcast_convert_fusion.1
  1088.8 5.1 fusion.43
  (193 shorter events, 20.7 us)
Async XLA Ops:
  7.2 87.6 %copy-start = (bf16[256,4096]{1,0:T(8,128)(2,1)S(1)}, bf16[256,4096]{1,0:T(8,128)(2,1)}, u32[]{:S(2)}) copy-start(bf16[256,4096]{1,0:T(8,128)(2,1)} %param.22) | copy-start | bytes 6291460
  7.2 86.0 %copy-start.50 = (bf16[16]{0:T(256)(128)(2,1)S(1)}, bf16[16]{0:T(256)(128)(2,1)}, u32[]{:S(2)}) copy-start(bf16[16]{0:T(256)(128)(2,1)} %param.25) | copy-start | bytes 100
  7.2 86.1 %copy-start.51 = (bf16[16]{0:T(256)(128)(2,1)S(1)}, bf16[16]{0:T(256)(128)(2,1)}, u32[]{:S(2)}) copy-start(bf16[16]{0:T(256)(128)(2,1)} %param.26) | copy-start | bytes 100
  7.2 86.3 %copy-start.48 = (bf16[256]{0:T(256)(128)(2,1)S(1)}, bf16[256]{0:T(256)(128)(2,1)}, u32[]{:S(2)}) copy-start(bf16[256]{0:T(256)(128)(2,1)} %param.21) | copy-start | bytes 1540
  7.2 86.4 %copy-start.49 = (bf16[256]{0:T(256)(128)(2,1)S(1)}, bf16[256]{0:T(256)(128)(2,1)}, u32[]{:S(2)}) copy-start(bf16[256]{0:T(256)(128)(2,1)} %param.28) | copy-start | bytes 1540
  7.2 86.5 %copy-start.39 = (bf16[256,32]{0,1:T(8,128)(2,1)S(1)}, bf16[256,32]{0,1:T(8,128)(2,1)}, u32[]{:S(2)}) copy-start(bf16[256,32]{0,1:T(8,128)(2,1)} %param.29) | copy-start | bytes 49156
  7.2 85.9 %all-gather.9.cloned.1.call-start = ((), (), s32[]{:S(2)}) async-start(), calls=%async_computation.8 | async-start | bytes 5242880 | tf_op jit(solution)/shard_map/all_gather | solution.py:1045
  8.0 217.0 %all-gather.5.cloned.1.call-start = ((), (), s32[]{:S(2)}) async-start(), calls=%async_computation.4 | async-start | bytes 18874368 | tf_op jit(solution)/shard_map/all_gather | solution.py:1079
  93.1 2.8 copy-start.28
  93.2 2.8 copy-start.47
  93.2 215.9 %reduce-scatter.3.cloned.1.call-start = ((), (), s32[]{:S(2)}) async-start(), calls=%async_computation.5 | async-start | bytes 5242880 | tf_op jit(solution)/shard_map/reduce_scatter | solution.py:1048
  172.3 5.6 copy-start.21
  175.6 2.8 copy-start.36
  175.7 3.4 copy-start.37
  175.7 3.3 copy-start.25
  178.9 14.7 %copy-start.2 = (f32[1024,128]{1,0:T(8,128)}, f32[1024,128]{1,0:T(8,128)S(1)}, u32[]{:S(2)}) copy-start(f32[1024,128]{1,0:T(8,128)S(1)} %pad_maximum_fusion.sin_ref) | copy-start | bytes 1572868
  179.0 14.7 %copy-start.6 = (f32[8,128]{1,0:T(8,128)}, f32[8,128]{1,0:T(8,128)S(1)}, u32[]{:S(2)}) copy-start(f32[8,128]{1,0:T(8,128)S(1)} %maximum_convert_fusion.gains_ref) | copy-start | bytes 12292
  182.3 11.3 %copy-start.16 = (bf16[1024,2048]{1,0:T(8,128)(2,1)}, bf16[1024,2048]{1,0:T(8,128)(2,1)S(1)}, u32[]{:S(2)}) copy-start(bf16[1024,2048]{1,0:T(8,128)(2,1)S(1)} %fusion.8) | copy-start | bytes 12582916
  234.8 4.9 copy-start.29
  251.6 121.7 %all-to-all-start = ((bf16[8,4,80,2048]{3,2,1,0:T(8,128)(2,1)}), bf16[8,4,80,2048]{3,2,1,0:T(8,128)(2,1)}, u32[]{:S(2)}, u32[]{:S(2)}) async-start(bf16[8,4,80,2048]{3,2,1,0:T(8,128)(2,1)} %shard_map.274), calls=%async_computation.1 | async-start | bytes 20971520 | tf_op jit(solution)/shard_map/all_to_all | solution.py:1051
  256.8 52.3 %copy-start.9 = (bf16[1,256,2048]{2,1,0:T(8,128)(2,1)S(1)}, bf16[1,256,2048]{2,1,0:T(8,128)(2,1)}, u32[]{:S(2)}) copy-start(bf16[1,256,2048]{2,1,0:T(8,128)(2,1)} %param.17) | copy-start | bytes 3145732
  309.1 3.0 copy-start.10
  309.1 4.5 copy-start.27
  312.1 368.7 %copy-start.31 = (f32[256]{0:T(256)}, f32[256]{0:T(256)S(1)}, u32[]{:S(2)}) copy-start(f32[256]{0:T(256)S(1)} %get-tuple-element.159) | copy-start | bytes 3076
  663.4 127.5 %all-to-all-start.1 = ((bf16[8,4,80,2048]{3,2,1,0:T(8,128)(2,1)}), bf16[8,4,80,2048]{3,2,1,0:T(8,128)(2,1)}, u32[]{:S(2)}, u32[]{:S(2)}) async-start(bf16[8,4,80,2048]{3,2,1,0:T(8,128)(2,1)} %get-tuple-element.47), calls=%async_computation.2 | async-start | bytes 20971520 | tf_op jit(solution)/shard_map/all_to_all | solution.py:1051
  673.8 126.6 %all-gather.7.cloned.1.call-start = ((), (), s32[]{:S(2)}) async-start(), calls=%async_computation.6 | async-start | bytes 5242880 | tf_op jit(solution)/shard_map/all_gather | solution.py:1045
  673.8 3.2 copy-start.35
  677.5 3.4 copy-start.22
  677.5 3.4 copy-start.14
  677.5 3.4 copy-start.40
  680.8 3.4 copy-start.42
  684.3 404.5 %reduce-scatter.5.cloned.1.call-start = ((), (), s32[]{:S(2)}) async-start(), calls=%async_computation.7 | async-start | bytes 5242880 | tf_op jit(solution)/shard_map/reduce_scatter | solution.py:1048
  684.5 14.3 %copy-start.52 = (bf16[8,4,80,768]{3,2,1,0:T(8,128)(2,1)S(1)}, bf16[8,4,80,768]{3,2,1,0:T(8,128)(2,1)}, u32[]{:S(2)}) copy-start(bf16[8,4,80,768]{3,2,1,0:T(8,128)(2,1)} %get-tuple-element.61) | copy-start | bytes 11796484
  698.8 92.1 %copy-start.30 = (s32[4,8,256]{2,1,0:T(8,128)S(1)}, s32[4,8,256]{2,1,0:T(8,128)}, u32[]{:S(2)}) copy-start(s32[4,8,256]{2,1,0:T(8,128)} %copy-done.29) | copy-start | bytes 98308
  800.4 14.4 %copy-start.13 = (bf16[256,2048]{1,0:T(8,128)(2,1)S(1)}, bf16[256,2048]{1,0:T(8,128)(2,1)}, u32[]{:S(2)}) copy-start(bf16[256,2048]{1,0:T(8,128)(2,1)} %copy-done.12) | copy-start | bytes 3145732
  800.4 14.4 %copy-start.23 = (bf16[256,32]{1,0:T(8,128)(2,1)S(1)}, bf16[256,32]{1,0:T(8,128)(2,1)}, u32[]{:S(2)}) copy-start(bf16[256,32]{1,0:T(8,128)(2,1)} %copy-done.22) | copy-start | bytes 49156
  800.4 15.3 %copy-start.44 = (f32[256]{0:T(256)S(1)}, f32[256]{0:T(256)}, u32[]{:S(2)}) copy-start(f32[256]{0:T(256)} %get-tuple-element.136) | copy-start | bytes 3076
  816.3 9.4 copy-start.3
  816.3 9.4 copy-start.5
  816.3 9.4 copy-start.7
  865.2 10.8 copy-start.19
  882.8 9.6 copy-start.17
  882.8 9.6 copy-start.20
  1073.0 10.4 copy-start.24
  1075.1 10.5 copy-start.15
  1075.1 10.5 copy-start.26
  1086.0 2.7 copy-start.32
  1088.8 5.1 copy-start.1
  (12 other events, 21.4 us)
Sparse Core Ops, SparseCore 0:
  9.7 83.4 all-gather.8
  95.0 111.8 all-gather.4
  233.7 75.3 reduce-scatter.2
  684.4 91.3 all-gather.6
  800.5 84.5 reduce-scatter.4

commit v3 on v2

--- a/solution.py
+++ b/solution.py
@@ -50,17 +50,16 @@
     return d_raw, jnp.sum(dz * raw * r, axis=0, keepdims=True)
 
 
-def attention_forward(
-    q_ref, k_ref, v_ref, cos_ref, sin_ref, gains_ref, own_ref, key_ref, mixed_ref, total_ref, dealt_ref, keys, values_t
+def prepare_keys(k_ref, v_ref, cos_ref, sin_ref, gains_ref, keys, values_t):
+    rotated = norm_rope(k_ref[...], gains_ref[1:2, :], cos_ref[...], sin_ref[...])
+    keys[...] = rotated.astype(BF)
+    values_t[...] = v_ref[...].T.astype(BF)
+
+
+def attend_head(
+    q_ref, cos_ref, sin_ref, gains_ref, own_ref, key_ref, total_ref, dealt_ref, keys, values_t, store
 ):
-    cosine, sine = cos_ref[...], sin_ref[...]
-
-    @pl.when(pl.program_id(0) == 0)
-    def _():
-        keys[...] = norm_rope(k_ref[...], gains_ref[1:2, :], cosine, sine).astype(BF)
-        values_t[...] = v_ref[...].T.astype(BF)
-
-    queries = norm_rope(q_ref[...], gains_ref[0:1, :], cosine, sine).astype(BF)
+    queries = norm_rope(q_ref[...], gains_ref[0:1, :], cos_ref[...], sin_ref[...]).astype(BF)
     length = queries.shape[0]
     chunk = 256
     for start in range(0, length, chunk):
@@ -70,10 +69,37 @@
         top = jnp.max(scores, axis=0, keepdims=True)
         weights = jnp.exp(scores - top)
         total = jnp.sum(weights, axis=0, keepdims=True)
-        out = nn(values_t[...], weights.astype(BF)) / total
-        mixed_ref[start : start + chunk, :] = out.T.astype(BF)
-        dealt_ref[0, start : start + chunk, :] = out.T.astype(BF)
+        out = (nn(values_t[...], weights.astype(BF)) / total).T.astype(BF)
+        store(start, chunk, out)
+        dealt_ref[0, start : start + chunk, :] = out
         total_ref[0, :, start : start + chunk] = jnp.broadcast_to(top + jnp.log(total), (8, chunk))
+
+
+def attention_forward(
+    q_ref,
+    k_ref,
+    v_ref,
+    cos_ref,
+    sin_ref,
+    gains_ref,
+    own_ref,
+    key_ref,
+    mixed_ref,
+    total_ref,
+    dealt_ref,
+    keys,
+    values_t,
+):
+    @pl.when(pl.program_id(0) == 0)
+    def _():
+        prepare_keys(k_ref, v_ref, cos_ref, sin_ref, gains_ref, keys, values_t)
+
+    def store(start, count, out):
+        mixed_ref[start : start + count, :] = out
+
+    attend_head(
+        q_ref, cos_ref, sin_ref, gains_ref, own_ref, key_ref, total_ref, dealt_ref, keys, values_t, store
+    )
 
 
 def attention_backward(
@@ -254,33 +280,25 @@
     def going_down(self, step):
         return (self.ctx + step < self.n_ctx) & (self.ctx > 0)
 
-    def hop(self, block, step, sems, to):
-        if step == 0:
-            self.copy(self.own_ref, block, sems, step, to).start()
-        else:
-            self.copy(self.own_ref, block, sems, step, to).wait_recv()
-            self.copy(self.all_ref.at[block], block, sems, step, to).start()
-
     def step(self, step):
-        @pl.when(self.going_up(step))
-        def _():
-            self.hop(self.ctx - step, step, self.up, self.ctx + 1)
-
-        @pl.when(self.going_down(step))
-        def _():
-            self.hop(self.ctx + step, step, self.down, self.ctx - 1)
+        def hop(block, sems, to, more):
+            if step > 0:
+                self.copy(self.own_ref, block, sems, 0, to).wait_recv()
+
+            @pl.when(more)
+            def _():
+                source = self.all_ref.at[block] if step > 0 else self.own_ref
+                self.copy(source, block, sems, step, to).start()
+
+        @pl.when(self.ctx - step >= 0)
+        def _():
+            hop(self.ctx - step, self.up, self.ctx + 1, self.ctx < self.n_ctx - 1)
+
+        @pl.when(self.ctx + step < self.n_ctx)
+        def _():
+            hop(self.ctx + step, self.down, self.ctx - 1, self.ctx > 0)
 
     def finish(self):
-        for other in range(1, self.n_ctx):
-
-            @pl.when(self.ctx == self.n_ctx - 1)
-            def _():
-                self.copy(self.own_ref, self.n_ctx - 1 - other, self.up, 0, self.ctx).wait_recv()
-
-            @pl.when(self.ctx == 0)
-            def _():
-                self.copy(self.own_ref, other, self.up, 0, self.ctx).wait_recv()
-
         for step in range(self.n_ctx - 1):
 
             @pl.when(self.going_up(step))
@@ -290,6 +308,76 @@
             @pl.when(self.going_down(step))
             def _():
                 self.copy(self.own_ref, 0, self.down, step, self.ctx).wait_send()
+
+
+class LineScatter:
+    def __init__(self, n_ctx, ctx, fsdp, chunks, held, low, high, up, down, low_in, high_in):
+        self.n_ctx, self.ctx, self.fsdp, self.chunks = n_ctx, ctx, fsdp, chunks
+        self.held, self.low, self.high = held, low, high
+        self.sems = {"up": (low, up, low_in), "down": (high, down, high_in)}
+        self.size = held.shape[1] // chunks
+
+    def copy(self, way, block, chunk, to):
+        landing, sends, arrived = self.sems[way]
+        rows = pl.ds(chunk * self.size, self.size)
+        return push(
+            self.held.at[block, rows],
+            landing.at[block, rows],
+            sends.at[block, chunk],
+            arrived.at[block, chunk],
+            (to, self.fsdp),
+        )
+
+    def scatter(self, chunk):
+        rows = slice(chunk * self.size, (chunk + 1) * self.size)
+        ctx, held = self.ctx, self.held
+
+        def pass_on(way, block, to, first):
+            @pl.when(jnp.logical_not(first))
+            def _():
+                self.copy(way, block, chunk, ctx).wait_recv()
+                held[block, rows, :] = (
+                    held[block, rows, :].astype(F32)
+                    + self.sems[way][0][block, rows, :].astype(F32)
+                ).astype(BF)
+
+            self.copy(way, block, chunk, to).start()
+
+        for step in range(self.n_ctx - 1):
+
+            @pl.when(ctx < self.n_ctx - 1 - step)
+            def _():
+                pass_on("up", self.n_ctx - 1 - step, ctx + 1, ctx == 0)
+
+            @pl.when(ctx > step)
+            def _():
+                pass_on("down", step, ctx - 1, ctx == self.n_ctx - 1)
+
+    def settle(self, chunk, total_ref):
+        rows = slice(chunk * self.size, (chunk + 1) * self.size)
+        total_ref[rows, :] = self.held[self.ctx, rows, :].astype(F32)
+
+        @pl.when(self.ctx > 0)
+        def _():
+            self.copy("up", self.ctx, chunk, self.ctx).wait_recv()
+            total_ref[rows, :] += self.low[self.ctx, rows, :].astype(F32)
+
+        @pl.when(self.ctx < self.n_ctx - 1)
+        def _():
+            self.copy("down", self.ctx, chunk, self.ctx).wait_recv()
+            total_ref[rows, :] += self.high[self.ctx, rows, :].astype(F32)
+
+    def finish(self):
+        for chunk in range(self.chunks):
+            for step in range(self.n_ctx - 1):
+
+                @pl.when(self.ctx < self.n_ctx - 1 - step)
+                def _():
+                    self.copy("up", self.n_ctx - 1 - step, chunk, self.ctx).wait_send()
+
+                @pl.when(self.ctx > step)
+                def _():
+                    self.copy("down", step, chunk, self.ctx).wait_send()
 
 
 def first_gather(
@@ -345,7 +433,7 @@
             table_ref, table_all.at[ctx], table_send.at[i], table_arrived.at[ctx], (along(i), fsdp)
         ).start()
     line = LineGather(n_ctx, ctx, fsdp, x_ref, x_all, up, down, arrived)
-    for step in range(n_ctx - 1):
+    for step in range(n_ctx):
         line.step(step)
     for i in range(1, chips):
         owner = same_core(chips - i)
@@ -770,14 +858,10 @@
     )(x, select, select_t, gate, up, down, grads, dealt)
 
 
-def last_reduce(n_ctx, n_fsdp, chunks, dh_ref, *refs):
+def last_reduce(n_ctx, n_fsdp, *refs):
     ctx, fsdp = lax.axis_index("ctx"), lax.axis_index("fsdp")
-    count = (len(refs) - 9) // 11
-    ins, refs = refs[:count], refs[count:]
-    total_ref, refs = refs[0], refs[1:]
-    alls, refs = refs[:count], refs[count:]
-    held, low, high, local, up_send, low_arrived, down_send, refs = refs[:7] + (refs[7:],)
-    high_arrived, refs = refs[0], refs[1:]
+    count = (len(refs) - 1) // 11
+    ins, alls, local, refs = refs[:count], refs[count : 2 * count], refs[2 * count], refs[2 * count + 1 :]
     items = [refs[9 * i : 9 * i + 9] for i in range(count)]
     chips, chip, core = n_fsdp // 2, fsdp // 2, lax.rem(fsdp, 2)
     sibling = chip * 2 + 1 - core
@@ -793,8 +877,6 @@
         + [(ctx, other_chip(i) * 2 + core) for i in range(1, chips)]
         + [(ctx, sibling)]
     )
-    load = pltpu.make_async_copy(dh_ref, held, local.at[0])
-    load.start()
     crossing, loads, lines = [], [], []
     for at, (in_ref, all_ref, item) in enumerate(zip(ins, alls, items)):
         mine, beside, landed, own, cross, sends, arrived, line_sems, line_arrived = item
@@ -802,74 +884,13 @@
             push(in_ref.at[:, 1 - core], beside, cross.at[0], cross.at[1], (ctx, sibling))
         )
         crossing[-1].start()
-        loads.append(pltpu.make_async_copy(in_ref.at[:, core], mine, local.at[1 + at]))
+        loads.append(pltpu.make_async_copy(in_ref.at[:, core], mine, local.at[at]))
         loads[-1].start()
         lines.append(
             LineGather(
                 n_ctx, ctx, fsdp, own, all_ref, line_sems.at[0], line_sems.at[1], line_arrived
             )
         )
-    load.wait()
-    size = held.shape[1] // chunks
-
-    def travel(landing, block, chunk, sends, arrived, to):
-        rows = pl.ds(chunk * size, size)
-        return push(
-            held.at[block, rows],
-            landing.at[block, rows],
-            sends.at[block, chunk],
-            arrived.at[block, chunk],
-            (to, fsdp),
-        )
-
-    def up(block, chunk, to):
-        return travel(low, block, chunk, up_send, low_arrived, to)
-
-    def down(block, chunk, to):
-        return travel(high, block, chunk, down_send, high_arrived, to)
-
-    def scatter(chunk):
-        rows = slice(chunk * size, (chunk + 1) * size)
-
-        def add(block, landing):
-            held[block, rows, :] = (
-                held[block, rows, :].astype(F32) + landing[block, rows, :].astype(F32)
-            ).astype(BF)
-
-        for step in range(n_ctx - 1):
-            above, below = n_ctx - 1 - step, step
-
-            @pl.when(ctx < above)
-            def _():
-                @pl.when(ctx > 0)
-                def _():
-                    up(above, chunk, ctx).wait_recv()
-                    add(above, low)
-
-                up(above, chunk, ctx + 1).start()
-
-            @pl.when(ctx > below)
-            def _():
-                @pl.when(ctx < n_ctx - 1)
-                def _():
-                    down(below, chunk, ctx).wait_recv()
-                    add(below, high)
-
-                down(below, chunk, ctx - 1).start()
-
-    def settle(chunk):
-        rows = slice(chunk * size, (chunk + 1) * size)
-        total_ref[rows, :] = held[ctx, rows, :].astype(F32)
-
-        @pl.when(ctx > 0)
-        def _():
-            up(ctx, chunk, ctx).wait_recv()
-            total_ref[rows, :] += low[ctx, rows, :].astype(F32)
-
-        @pl.when(ctx < n_ctx - 1)
-        def _():
-            down(ctx, chunk, ctx).wait_recv()
-            total_ref[rows, :] += high[ctx, rows, :].astype(F32)
 
     def chip_copy(item, offset):
         mine, beside, landed, own, cross, sends, arrived, line_sems, line_arrived = item
@@ -878,8 +899,6 @@
             mine.at[to], landed.at[chip], sends.at[offset], arrived.at[chip], (ctx, to * 2 + core)
         )
 
-    scatter(0)
-    scatter(1)
     for crossed, loaded, item in zip(crossing, loads, items):
         mine, beside = item[:2]
         loaded.wait()
@@ -889,8 +908,6 @@
             mine[to] = (mine[to].astype(F32) + beside[to].astype(F32)).astype(BF)
             if offset < chips:
                 chip_copy(item, offset).start()
-    for chunk in range(2, chunks):
-        scatter(chunk)
     keeps = []
     for at, (item, line, all_ref) in enumerate(zip(items, lines, alls)):
         mine, beside, landed, own, cross, sends, arrived, line_sems, line_arrived = item
@@ -903,49 +920,26 @@
             total = total + landed[source].astype(F32)
         own[...] = total.astype(BF)
         line.step(0)
-        keeps.append(pltpu.make_async_copy(own, all_ref.at[ctx], local.at[1 + at]))
+        keeps.append(pltpu.make_async_copy(own, all_ref.at[ctx], local.at[at]))
         keeps[-1].start()
-    for step in range(1, n_ctx - 1):
+    for step in range(1, n_ctx):
         for line in lines:
             line.step(step)
-    for chunk in range(chunks):
-        settle(chunk)
     for crossed, keep, line, item in zip(crossing, keeps, lines, items):
         crossed.wait_send()
         keep.wait()
         line.finish()
         for offset in range(1, chips):
             chip_copy(item, offset).wait_send()
-    for chunk in range(chunks):
-        for step in range(n_ctx - 1):
-            above, below = n_ctx - 1 - step, step
-
-            @pl.when(ctx < above)
-            def _():
-                up(above, chunk, ctx).wait_send()
-
-            @pl.when(ctx > below)
-            def _():
-                down(below, chunk, ctx).wait_send()
-
-
-def run_last_reduce(n_ctx, n_fsdp, d_hidden, grads):
+
+
+def run_last_reduce(n_ctx, n_fsdp, grads):
     anywhere = pl.BlockSpec(memory_space=pl.ANY)
     dma, vmem, shape = pltpu.SemaphoreType.DMA, pltpu.VMEM, jax.ShapeDtypeStruct
-    chunks, chips = 4, n_fsdp // 2
-    _, span, width = d_hidden.shape
+    chips = n_fsdp // 2
     grads = [grad.reshape((chips, 2, -1) + grad.shape[-1:]) for grad in grads]
     blocks = [grad.shape[2:] for grad in grads]
-    scratch = [
-        vmem(d_hidden.shape, BF),
-        vmem(d_hidden.shape, BF),
-        vmem(d_hidden.shape, BF),
-        dma((1 + len(grads),)),
-        dma((n_ctx, chunks)),
-        dma((n_ctx, chunks)),
-        dma((n_ctx, chunks)),
-        dma((n_ctx, chunks)),
-    ]
+    scratch = [dma((len(grads),))]
     for block in blocks:
         scratch += [
             vmem((chips,) + block, BF),
@@ -959,16 +953,16 @@
             dma((n_ctx,)),
         ]
     return pl.pallas_call(
-        functools.partial(last_reduce, n_ctx, n_fsdp, chunks),
-        in_specs=[anywhere] * (1 + len(grads)),
-        out_specs=[pl.BlockSpec(memory_space=pltpu.VMEM)] + [anywhere] * len(grads),
-        out_shape=[shape((span, width), F32)] + [shape((n_ctx,) + block, BF) for block in blocks],
+        functools.partial(last_reduce, n_ctx, n_fsdp),
+        in_specs=[anywhere] * len(grads),
+        out_specs=[anywhere] * len(grads),
+        out_shape=[shape((n_ctx,) + block, BF) for block in blocks],
         scratch_shapes=scratch,
         compiler_params=pltpu.CompilerParams(
             collective_id=3, has_side_effects=True, vmem_limit_bytes=60 * 2**20
         ),
-        cost_estimate=pl.CostEstimate(flops=0, bytes_accessed=300 * 2**20, transcendentals=0),
-    )(d_hidden, *grads)
+        cost_estimate=pl.CostEstimate(flops=0, bytes_accessed=400 * 2**20, transcendentals=0),
+    )(*grads)
 
 
 def widen_columns(in_ref, out_ref):
@@ -986,26 +980,236 @@
     )(blocks)
 
 
-def pick_rows(select_ref, rows_ref, out_ref):
-    shape = out_ref.shape
-    for at in range(0, shape[3], TILE):
-        picked = nn(select_ref[0], rows_ref[0, :, at : at + TILE])
-        out_ref[:, 0, :, at : at + TILE] = picked.astype(BF).reshape(shape[0], shape[2], TILE)
-
-
-def run_pick_rows(select, rows, n_fsdp):
-    n_ctx, count, span = select.shape
-    capacity, width = count // n_fsdp, rows.shape[2]
+def attention_exchange(
+    n_ctx,
+    n_fsdp,
+    heads,
+    q_ref,
+    k_ref,
+    v_ref,
+    cos_ref,
+    sin_ref,
+    gains_ref,
+    own_ref,
+    key_ref,
+    sel_ref,
+    grad_ref,
+    out_ref,
+    total_ref,
+    dealt_ref,
+    attn_ref,
+    rows_ref,
+    keys,
+    values_t,
+    mixed,
+    w_out,
+    held,
+    low,
+    high,
+    grads,
+    staged,
+    local,
+    grad_up,
+    grad_down,
+    grad_arrived,
+    rows_send,
+    rows_arrived,
+    up_send,
+    down_send,
+    low_arrived,
+    high_arrived,
+):
+    head = pl.program_id(0)
+    ctx, fsdp = lax.axis_index("ctx"), lax.axis_index("fsdp")
+    _, span, width = held.shape
+    capacity = staged.shape[2]
+    q_width = heads * HEAD_SIZE
+
+    def along(offset):
+        return lax.rem(ctx + offset, n_ctx)
+
+    def around(offset):
+        return lax.rem(fsdp + offset, n_fsdp)
+
+    line = LineGather(n_ctx, ctx, fsdp, grad_ref, grads, grad_up, grad_down, grad_arrived)
+    sums = LineScatter(
+        n_ctx, ctx, fsdp, 4, held, low, high, up_send, down_send, low_arrived, high_arrived
+    )
+    own = pltpu.make_async_copy(grad_ref, grads.at[ctx], local.at[0])
+    weights = pltpu.make_async_copy(
+        out_ref.at[pl.ds(ctx * q_width, q_width)], w_out, local.at[1]
+    )
+
+    def rows_copy(group, offset):
+        to = around(offset)
+        return push(
+            staged.at[group, to],
+            rows_ref.at[fsdp, group],
+            rows_send.at[group, offset],
+            rows_arrived.at[group, fsdp],
+            (ctx, to),
+        )
+
+    def rows_kept(group):
+        return pltpu.make_async_copy(
+            staged.at[group, fsdp], rows_ref.at[fsdp, group], rows_arrived.at[group, fsdp]
+        )
+
+    def pick(group):
+        for at in range(0, width, TILE):
+            picked = nn(sel_ref[group], grads[group, :, at : at + TILE])
+            staged[group, :, :, at : at + TILE] = picked.astype(BF).reshape(n_fsdp, capacity, TILE)
+        rows_kept(group).start()
+        for offset in range(1, n_fsdp):
+            rows_copy(group, offset).start()
+
+    def pick_from(distance):
+        @pl.when(ctx - distance >= 0)
+        def _():
+            pick(ctx - distance)
+
+        @pl.when(ctx + distance < n_ctx)
+        def _():
+            pick(ctx + distance)
+
+    @pl.when(head == 0)
+    def _():
+        own.start()
+        weights.start()
+        greet(
+            [(along(i), fsdp) for i in range(1, n_ctx)]
+            + [(ctx, around(i)) for i in range(1, n_fsdp)]
+        )
+        line.step(0)
+        own.wait()
+        pick(ctx)
+        prepare_keys(k_ref, v_ref, cos_ref, sin_ref, gains_ref, keys, values_t)
+
+    @pl.when(head < heads)
+    def _():
+        def store(start, count, out):
+            columns = pl.ds(pl.multiple_of(head * HEAD_SIZE, HEAD_SIZE), HEAD_SIZE)
+            mixed[start : start + count, columns] = out
+
+        attend_head(
+            q_ref,
+            cos_ref,
+            sin_ref,
+            gains_ref,
+            own_ref,
+            key_ref,
+            total_ref,
+            dealt_ref,
+            keys,
+            values_t,
+            store,
+        )
+
+    @pl.when(head == heads - 2)
+    def _():
+        line.step(1)
+        pick_from(1)
+
+    @pl.when(head == heads)
+    def _():
+        weights.wait()
+        for block in range(n_ctx):
+            for at in range(0, width, TILE):
+                held[block, :, at : at + TILE] = nn(
+                    mixed[block * span : (block + 1) * span, :], w_out[:, at : at + TILE]
+                ).astype(BF)
+        line.step(2)
+        sums.scatter(0)
+        pick_from(2)
+        sums.scatter(1)
+        for step in range(3, n_ctx):
+            line.step(step)
+            pick_from(step)
+        sums.scatter(2)
+        sums.scatter(3)
+        for chunk in range(4):
+            sums.settle(chunk, attn_ref)
+        sums.finish()
+        line.finish()
+        for group in range(n_ctx):
+            rows_kept(group).wait()
+            for offset in range(1, n_fsdp):
+                source = around(offset)
+                push(
+                    staged.at[group, source],
+                    rows_ref.at[source, group],
+                    rows_send.at[group, offset],
+                    rows_arrived.at[group, source],
+                    (ctx, source),
+                ).wait()
+
+
+def run_attention_exchange(
+    qkv, heads, n_ctx, n_fsdp, cosine, sine, gains, own, key_blocks, select, grad, w_out
+):
+    length = qkv.shape[0]
+    span, width = grad.shape
+    capacity = select.shape[1] // n_fsdp
+    anywhere = pl.BlockSpec(memory_space=pl.ANY)
+    dma, vmem, shape = pltpu.SemaphoreType.DMA, pltpu.VMEM, jax.ShapeDtypeStruct
+    last = heads - 1
+    whole, column, _, _, shared = attention_specs(heads, length)
+    clip = lambda h: jnp.minimum(h, last)
     return pl.pallas_call(
-        pick_rows,
-        grid=(n_ctx,),
+        functools.partial(attention_exchange, n_ctx, n_fsdp, heads),
+        grid=(heads + 1,),
         in_specs=[
-            pl.BlockSpec((1, count, span), lambda g: (g, 0, 0)),
-            pl.BlockSpec((1, span, width), lambda g: (g, 0, 0)),
+            pl.BlockSpec((length, HEAD_SIZE), lambda h: (0, clip(h))),
+            column(heads),
+            column(heads + 1),
+        ]
+        + shared
+        + [whole(select.shape), anywhere, anywhere],
+        out_specs=[
+            pl.BlockSpec((1, 8, length), lambda h: (clip(h), 0, 0)),
+            pl.BlockSpec(
+                (1, length, HEAD_SIZE),
+                lambda h: (lax.rem(clip(h), n_ctx), 0, lax.div(clip(h), n_ctx)),
+            ),
+            whole((span, width)),
+            anywhere,
         ],
-        out_specs=pl.BlockSpec((n_fsdp, 1, capacity, width), lambda g: (0, g, 0, 0)),
-        out_shape=jax.ShapeDtypeStruct((n_fsdp, n_ctx, capacity, width), BF),
-    )(select, rows)
+        out_shape=[
+            shape((heads, 8, length), F32),
+            shape((n_ctx, length, heads // n_ctx * HEAD_SIZE), BF),
+            shape((span, width), F32),
+            shape((n_fsdp, n_ctx, capacity, width), BF),
+        ],
+        scratch_shapes=[
+            vmem((length, HEAD_SIZE), BF),
+            vmem((HEAD_SIZE, length), BF),
+            vmem((length, heads * HEAD_SIZE), BF),
+            vmem((heads * HEAD_SIZE, width), BF),
+            vmem((n_ctx, span, width), BF),
+            vmem((n_ctx, span, width), BF),
+            vmem((n_ctx, span, width), BF),
+            vmem((n_ctx, span, width), BF),
+            vmem((n_ctx, n_fsdp, capacity, width), BF),
+            dma((2,)),
+            dma((n_ctx,)),
+            dma((n_ctx,)),
+            dma((n_ctx,)),
+            dma((n_ctx, n_fsdp)),
+            dma((n_ctx, n_fsdp)),
+            dma((n_ctx, 4)),
+            dma((n_ctx, 4)),
+            dma((n_ctx, 4)),
+            dma((n_ctx, 4)),
+        ],
+        compiler_params=pltpu.CompilerParams(
+            collective_id=4, has_side_effects=True, vmem_limit_bytes=60 * 2**20
+        ),
+        cost_estimate=pl.CostEstimate(
+            flops=4 * heads * length * length * HEAD_SIZE,
+            bytes_accessed=400 * 2**20,
+            transcendentals=heads * length * length,
+        ),
+    )(qkv, qkv, qkv, cosine, sine, gains, own, key_blocks, select, grad, w_out)
 
 
 def on_device(
@@ -1073,9 +1277,7 @@
     table = jnp.concatenate(
         [expert_ids[0].T, drop_order[0], jnp.zeros((7, span), jnp.int32)], axis=0
     )
-    grad_all = gather_ctx(cotangent[0])
     inputs_all, tables, packed_all = run_first_gather(n_ctx, n_fsdp, inputs[0], table, packed)
-    w_out, grad_all = lax.optimization_barrier((w_out, grad_all))
     out_all = lax.all_gather(w_out, "fsdp", axis=0, tiled=True)
     out_here = lax.dynamic_slice_in_dim(out_all, ctx * q_width, q_width, axis=0)
     inputs_all = inputs_all.reshape(length, width)
@@ -1106,14 +1308,10 @@
         place[:, :, None, :] == jnp.arange(capacity, dtype=jnp.int32)[None, None, :, None]
     ).astype(BF)
 
-    fused = capacity % 16 == 0 and 2 * experts <= AUX
+    fused = capacity % 16 == 0 and 2 * experts <= AUX and experts == QUERY_HEADS
     select_rows = select.reshape(n_ctx, n_fsdp * capacity, span)
 
     def dispatch(rows):
-        if fused:
-            return route(
-                run_pick_rows(select_rows, rows.reshape(n_ctx, span, width), n_fsdp)
-            ).reshape(slots, width)
         picked = jnp.einsum(
             "gjkt,gtd->jgkd", select, rows.reshape(n_ctx, span, width), preferred_element_type=F32
         ).astype(BF)
@@ -1135,16 +1333,32 @@
     sine = jnp.concatenate([-jnp.sin(angles), jnp.sin(angles)], axis=1)
     own_blocks = jnp.broadcast_to(block_ids, (8, length))
     key_blocks = block_ids.reshape(length, 1)
-    mixed, totals, dealt = run_attention(
-        qkv, heads, n_ctx, cosine, sine, gains, own_blocks, key_blocks
-    )
     piece = QUERY_HEADS * HEAD_SIZE // experts
     groups = n_fsdp // n_ctx
-    if piece != HEAD_SIZE:
+    if fused:
+        totals, dealt, attn_out, grad_rows = run_attention_exchange(
+            qkv,
+            heads,
+            n_ctx,
+            n_fsdp,
+            cosine,
+            sine,
+            gains,
+            own_blocks,
+            key_blocks,
+            select_rows,
+            cotangent[0],
+            out_all,
+        )
+        grad_rows = grad_rows.reshape(slots, width)
+    else:
+        mixed, totals, _ = run_attention(
+            qkv, heads, n_ctx, cosine, sine, gains, own_blocks, key_blocks
+        )
+        attn_out = scatter_ctx(nn(mixed, out_here))
+        grad_rows = dispatch(gather_ctx(cotangent[0]))
         dealt = mixed.reshape(length, groups, n_ctx, piece).transpose(2, 0, 1, 3)
         dealt = dealt.reshape(n_ctx, length, groups * piece)
-    grad_rows = dispatch(grad_all)
-    attn_out = scatter_ctx(nn(mixed, out_here))
 
     x = inputs[0].astype(F32)
     resid = x + attn_out.astype(F32)
@@ -1233,18 +1447,17 @@
     ffn_gain_grad = jnp.sum(d_normed * resid * r_ffn, axis=0)
     d_attn = gather_ctx(d_resid.astype(BF))
     y_all = combine(y).astype(BF)
-    d_attn, y_all = lax.optimization_barrier((d_attn, y_all))
+    d_attn, gate_grad, up_grad, down_grad = lax.optimization_barrier(
+        (d_attn, gate_grad, up_grad, down_grad)
+    )
     d_mixed = nt(d_attn, out_here).astype(BF)
 
     moe = scatter_ctx(y_all).astype(F32)
-    output = (resid + moe).astype(BF)[None]
-
     out_grad = jnp.einsum("ntk,td->nkd", dealt, d_attn, preferred_element_type=F32).astype(BF)
 
     dq, dkv, dgains = run_attention_back(
         qkv, d_mixed, totals, heads, cosine, sine, gains, own_blocks, key_blocks
     )
-    dq, moe = lax.optimization_barrier((dq, moe))
     d_qkv = jnp.concatenate([dq, dkv], axis=1)
     d_hidden = nt(d_qkv, w_qkv)
     attn_gain_grad = jnp.sum(d_hidden * x_all * r_all, axis=0)
@@ -1264,14 +1477,16 @@
         ],
         axis=1,
     )
-    d_hidden, shared_grad, rest, out_grad = run_last_reduce(
+    d_hidden, moe = lax.optimization_barrier((d_hidden.astype(BF), moe))
+    d_hidden = scatter_ctx(d_hidden).astype(F32)
+    shared_grad, rest, out_grad = run_last_reduce(
         n_ctx,
         n_fsdp,
-        d_hidden.astype(BF).reshape(n_ctx, span, width),
         [tn(hidden, d_qkv).astype(BF), extra_grad, out_grad.reshape(n_fsdp * piece, width)],
     )
     out_grad = out_grad.reshape(n_ctx * piece, width).astype(F32)
     rest = rest.astype(F32).sum(axis=0)
+    output = (resid + moe).astype(BF)[None]
     r_attn = inverse_rms(x)
     n = d_hidden * gain_attn
     input_grad = d_resid + r_attn * n - x * r_attn**3 * jnp.mean(n * x, axis=-1, keepdims=True)

time: 1120 us -> 1010 us (0.902); the launches traced: 1100 us -> 1010 us
  waiting for transfers between devices: 266 us -> 110 us
  Pallas kernels: 612 us -> 705 us
  matrix products: 114 us -> 98 us
    all_gather x2 -> x1, waiting for transfers between devices: 85.1 us -> 0.02 us  [gather_ctx(): return lax.all_gather(array, 'ctx', axis=0, tiled=True)]
    pallas_call x3 -> x2, Pallas kernels: 206 us -> 289 us  [the longest x1 146 us: run_attention_exchange(): pl.pallas_call(functools.partial(attention_exchange, n_ctx, n_fsdp, heads...]
    reduce_scatter x2, waiting for transfers between devices: 48.3 us -> 0.02 us  [scatter_ctx(): lax.psum_scatter(array.astype(BF), 'ctx', scatter_dimension=0, tiled=True)]
    all_to_all x2 -> x1, waiting for transfers between devices: 132 us -> 109 us  [route(): return lax.all_to_all(rows, 'fsdp', split_axis=0, concat_axis=0, tiled=True)]
    dot_general x3 -> x2, matrix products: 23.2 us -> 11.5 us  [nn(): lax.dot_general(a, b, (((1,), (0,)), ((), ())), preferred_element_type=F32)]
  transfers between devices with their start and end apart: 7 -> 5, of which waited for: 4 -> 1; matrix products, arithmetic and copies ran while one was open for 16% -> 15% of each run, Pallas kernels for 29% -> 26%
where the time goes in v3:
time: 1010 us
  Pallas kernels  705 us (70%)
  waiting for transfers between devices  110 us (11%)
  matrix products  98 us (10%)
  local copies, waits for them, and re-layouts  40.2 us (4%)
  other arithmetic  35.5 us (4%)
  between operations  14.8 us (1%)
    pallas_call x1, Pallas kernels, run_expert_exchange(): pl.pallas_call(functools.partial(expert_exchange, n_ctx, n_fsdp), in_spec...  291 us
    pallas_call x1, Pallas kernels, run_attention_exchange(): pl.pallas_call(functools.partial(attention_exchange, n_ctx, n_fsdp, heads...  146 us
    pallas_call x1, Pallas kernels, run_last_reduce(): pl.pallas_call(functools.partial(last_reduce, n_ctx, n_fsdp), in_specs=[a...  143 us
    all_to_all x1, waiting for transfers between devices, route(): return lax.all_to_all(rows, 'fsdp', split_axis=0, concat_axis=0, tiled=True)  109 us
    pallas_call x1, Pallas kernels, run_first_gather(): pl.pallas_call(functools.partial(first_gather, n_ctx, n_fsdp), in_specs=[...  83.2 us
    dot_general x5, matrix products, tn(): lax.dot_general(a, b, (((0,), (0,)), ((), ())), preferred_element_type=F32)  46.2 us
    pallas_call x1, Pallas kernels, run_attention_back(): pl.pallas_call(functools.partial(attention_backward, heads), grid=(heads,...  36.9 us
    dot_general x3, matrix products, nt(): lax.dot_general(a, b, (((1,), (1,)), ((), ())), preferred_element_type=F32)  21 us
  transfers between devices with their start and end apart: 5, of which 1 were waited for; matrix products, arithmetic and copies ran while one was open for 15% of the time, Pallas kernels for 26%

profile of v3, /device:TPU:0, one launch (start us, length us, event | category | flops | bytes accessed | tf_op | source)
XLA Modules:
  0.0 1011.0 jit_solution(8192831610481653483)
XLA Ops:
  12.9 1.1 concatenate.23.packed_ref
  14.7 83.2 %shard_map.272 = (bf16[4,256,2048]{2,1,0:T(8,128)(2,1)}, s32[4,16,256]{2,1,0:T(8,128)}, bf16[8,256,1408]{2,1,0:T(8,128)(2,1)}) custom-call(bf16[256,2048]{1,0:T(8,128)(2,1)} %bitcast.104, s32[16,256]{1,0:T(8,128)} %add_add_fusion.table_ref, bf16[256,1408]{1,0:T(8,128)(2,1)} %concatenate.23.packed_ref), custom_call_target="tpu_custom_call" | custom-call | bytes 209715200 | tf_op jit(solution)/shard_map/pallas_call | solution.py:462
  99.4 1.1 slice.98
  100.7 3.3 fusion.6
  104.8 1.7 eq.53
  106.5 2.1 copy.161
  108.7 1.3 compare_convert_fusion
  110.0 2.5 copy.164.sel_ref
  112.5 2.8 fusion.42
  115.3 1.3 copy.160
  117.4 2.0 copy.162.cos_ref
  119.5 1.0 copy.163.key_ref
  120.8 2.2 pad_maximum_fusion.sin_ref
  123.6 1.3 fusion.66.selt_ref
  124.9 1.0 fusion.8
  126.0 2.0 copy-done.17
  128.0 9.7 fusion.13.q_ref.k_ref.v_ref
  138.3 146.2 %shard_map.273 = (f32[8,8,1024]{2,1,0:T(8,128)}, bf16[4,1024,256]{2,1,0:T(8,128)(2,1)}, f32[256,2048]{1,0:T(8,128)}, bf16[8,4,80,2048]{3,2,1,0:T(8,128)(2,1)}) custom-call(f32[1024,1280]{1,0:T(8,128)} %fusion.13.q_ref.k_ref.v_ref, f32[1024,1280]{1,0:T(8,128)} %fusion.13.q_ref.k_ref.v_ref, f32[1024,1280]{1,0:T(8,128)} %fusion.13.q_ref.k_ref.v_ref, ...), custom_call_target="tpu_custom_call" | custom-call | flops 4294967296 | bytes 419430400 | tf_op jit(solution)/shard_map/pallas_call | solution.py:1158
  284.5 1.9 multiply_reduce_fusion.2
  286.8 1.5 fusion.50
  288.7 1.9 concatenate.26.x_ref
  290.6 291.2 %shard_map.274 = (bf16[8,4,80,2176]{3,2,1,0:T(8,128)(2,1)}, bf16[4,8,80,2176]{3,2,1,0:T(8,128)(2,1)}, bf16[4,256,2176]{2,1,0:T(8,128)(2,1)}, bf16[8,4,80,768]{3,...) custom-call(bf16[256,2176]{1,0:T(8,128)(2,1)} %concatenate.26.x_ref,, ...), custom_call_target="tpu_custom_call" | custom-call | flops 48318382080 | bytes 629145600 | tf_op jit(solution)/shard_map/pallas_call | solution.py:809
  581.8 7.2 all-to-all-start
  589.1 3.1 convert_reduce_fusion
  592.8 1.8 multiply_reduce_fusion
  594.6 2.3 fusion.49
  597.0 109.3 %all-to-all-done = bf16[8,4,80,2048]{3,2,1,0:T(8,128)(2,1)} async-done(((bf16[8,4,80,2048]{3,2,1,0:T(8,128)(2,1)}), bf16[8,4,80,2048]{3,2,1,0:T(8,128)(2,1)}, u32[]{:S(2)}, u32[]{:S(2)}) %all-to-all-start) | async-done | bytes 10485792 | tf_op jit(solution)/shard_map/all_to_all | solution.py:1255
  706.2 9.5 bitcast_convert_fusion
  716.2 14.2 %convolution_bitcast_fusion = f32[768,2048]{1,0:T(8,128)} fusion(bf16[8,4,80,768]{3,2,1,0:T(8,128)(2,1)} %get-tuple-element.50, bf16[8,4,80,2048]{3,2,1,0:T(8,128)(2,1)} %get-tuple-element.44.grad_ref), kind=kOutput, calls=%fused_computation.25 | convolution fusion | flops 8053063680 | bytes 20709376 | tf_op jit(solution)/shard_map/dot_general | solution.py:33
  730.4 13.3 %fusion.2 = f32[2048,768]{1,0:T(8,128)} fusion(bf16[2560,768]{1,0:T(8,128)(2,1)S(1)} %bitcast.150, bf16[2560,2176]{1,0:T(8,128)(2,1)} %bitcast.142), kind=kOutput, calls=%fused_computation.2 | convolution fusion | flops 8053063680 | bytes 20709376 | tf_op jit(solution)/shard_map/dot_general | solution.py:33
  743.7 10.8 %fusion.4 = f32[2048,768]{1,0:T(8,128)} fusion(bf16[2560,768]{1,0:T(8,128)(2,1)S(1)} %bitcast.149, bf16[2560,2176]{1,0:T(8,128)(2,1)S(1)} %bitcast.145), kind=kOutput, calls=%fused_computation.4 | convolution fusion | flops 8053063680 | bytes 20709376 | tf_op jit(solution)/shard_map/dot_general | solution.py:33
  754.7 9.5 fusion.29.grad_ref
  764.2 36.9 %shard_map.275 = (bf16[1024,1024]{1,0:T(8,128)(2,1)S(1)}, bf16[1024,256]{1,0:T(8,128)(2,1)S(1)}, f32[8,128]{1,0:T(8,128)S(1)}) custom-call(f32[1024,1280]{1,0:T(8,128)} %fusion.13.q_ref.k_ref.v_ref, f32[1024,1280]{1,0:T(8,128)} %fusion.13.q_ref.k_ref.v_ref, f32[1024,1280]{1,0:T(8,128)} %fusion.13.q_ref.k_ref.v_ref, bf16[1024,1024]{1,0:T(8,128)(2,1)} %fusion.29.grad_ref, ...), custom_call_target="tpu_custom_call" | custom-call | flops 10737418240 | bytes 10485760 | tf_op jit(solution)/shard_map/pallas_call | solution.py:221
  801.4 1.5 copy-done.21
  802.9 1.4 copy-done.11
  804.3 10.0 fusion.10
  814.3 2.9 convert_element_type.120
  819.6 2.3 concatenate.28
  821.9 9.5 fusion.21
  831.5 7.5 convolution_convert_fusion
  839.0 142.6 %shard_map.276 = (bf16[4,256,1280]{2,1,0:T(8,128)(2,1)}, bf16[4,256,128]{2,1,0:T(8,128)(2,1)}, bf16[4,128,2048]{2,1,0:T(8,128)(2,1)}) custom-call(bf16[4,2,256,1280]{3,2,1,0:T(8,128)(2,1)} %bitcast.106, bf16[4,2,256,128]{3,2,1,0:T(8,128)(2,1)} %bitcast.111, bf16[4,2,128,2048]{3,2,1,0:T(8,128)(2,1)} %bitcast.108), custom_call_target="tpu_custom_call" | custom-call | bytes 419430400 | tf_op jit(solution)/shard_map/pallas_call | solution.py:955
  981.6 4.4 shard_map.277
  986.1 1.3 convert_bitcast_fusion
  988.4 2.0 copy.179
  993.8 2.8 bitcast_convert_fusion.1
  997.5 1.2 fusion.34
  998.8 1.9 fusion.24
  1000.8 3.5 fusion.35
  (157 shorter events, 20.8 us)
Async XLA Ops:
  7.2 5.6 copy-start
  7.2 6.8 copy-start.27
  7.2 6.8 copy-start.31
  7.2 130.5 %all-gather.3.cloned.1.call-start = ((), (), s32[]{:S(2)}) async-start(), calls=%async_computation.3 | async-start | bytes 18874368 | tf_op jit(solution)/shard_map/all_gather | solution.py:1281
  100.7 5.8 copy-start.23
  104.0 20.9 %copy-start.29 = (f32[1,2,4,128]{3,1,2,0:T(2,128)}, f32[1,2,4,128]{3,1,2,0:T(2,128)S(1)}, u32[]{:S(2)}) copy-start(f32[1,2,4,128]{3,1,2,0:T(2,128)S(1)} %copy.188) | copy-start | bytes 12292
  104.1 20.8 %copy-start.25 = (f32[1,2048]{1,0:T(1,128)}, f32[1,2048]{1,0:T(1,128)S(1)}, u32[]{:S(2)}) copy-start(f32[1,2048]{1,0:T(1,128)S(1)} %get-tuple-element.157) | copy-start | bytes 24580
  110.0 9.5 copy-start.28
  120.5 4.4 copy-start.10
  125.9 2.0 copy-start.17
  138.3 146.2 %copy-start.12 = (bf16[1,256,2048]{2,1,0:T(8,128)(2,1)S(1)}, bf16[1,256,2048]{2,1,0:T(8,128)(2,1)}, u32[]{:S(2)}) copy-start(bf16[1,256,2048]{2,1,0:T(8,128)(2,1)} %param.17) | copy-start | bytes 3145732
  286.5 308.1 %copy-start.8 = (f32[256,2048]{1,0:T(8,128)}, f32[256,2048]{1,0:T(8,128)S(1)}, u32[]{:S(2)}) copy-start(f32[256,2048]{1,0:T(8,128)S(1)} %get-tuple-element.151) | copy-start | bytes 6291460
  286.7 295.1 %copy-start.14 = (bf16[256,2048]{1,0:T(8,128)(2,1)}, bf16[256,2048]{1,0:T(8,128)(2,1)S(1)}, u32[]{:S(2)}) copy-start(bf16[256,2048]{1,0:T(8,128)(2,1)S(1)} %multiply_convert_fusion) | copy-start | bytes 3145732
  581.8 124.4 %all-to-all-start = ((bf16[8,4,80,2048]{3,2,1,0:T(8,128)(2,1)}), bf16[8,4,80,2048]{3,2,1,0:T(8,128)(2,1)}, u32[]{:S(2)}, u32[]{:S(2)}) async-start(bf16[8,4,80,2048]{3,2,1,0:T(8,128)(2,1)} %get-tuple-element.55), calls=%async_computation | async-start | bytes 20971520 | tf_op jit(solution)/shard_map/all_to_all | solution.py:1255
  589.1 165.6 %all-gather.5.cloned.1.call-start = ((), (), s32[]{:S(2)}) async-start(), calls=%async_computation.4 | async-start | bytes 5242880 | tf_op jit(solution)/shard_map/all_gather | solution.py:1249
  592.7 1.8 copy-start.19
  596.9 217.4 %reduce-scatter.3.cloned.1.call-start = ((), (), s32[]{:S(2)}) async-start(), calls=%async_computation.5 | async-start | bytes 5242880 | tf_op jit(solution)/shard_map/reduce_scatter | solution.py:1252
  715.7 283.0 %reduce-scatter.5.cloned.1.call-start = ((), (), s32[]{:S(2)}) async-start(), calls=%async_computation.6 | async-start | bytes 5242880 | tf_op jit(solution)/shard_map/reduce_scatter | solution.py:1252
  716.2 14.2 %copy-start.33 = (bf16[8,4,80,768]{3,2,1,0:T(8,128)(2,1)S(1)}, bf16[8,4,80,768]{3,2,1,0:T(8,128)(2,1)}, u32[]{:S(2)}) copy-start(bf16[8,4,80,768]{3,2,1,0:T(8,128)(2,1)} %get-tuple-element.49) | copy-start | bytes 11796484
  716.2 27.5 %slice-start = ((s8[11141120]{0:T(1024)(128)(4,1)}), s8[4194304]{0:T(1024)(128)(4,1)S(1)}, s32[]{:S(2)}) async-start(s8[11141120]{0:T(1024)(128)(4,1)} %bitcast.143), calls=%async_computation.7 | async-start | bytes 8388608
  716.2 27.5 %slice-start.1 = ((s8[11141120]{0:T(1024)(128)(4,1)}), s8[4194304]{0:T(1024)(128)(4,1)S(1)}, s32[]{:S(2)}) async-start(s8[11141120]{0:T(1024)(128)(4,1)} %bitcast.143), calls=%async_computation.8 | async-start | bytes 8388608
  730.4 13.3 %slice-start.2 = ((s8[11141120]{0:T(1024)(128)(4,1)}), s8[2752512]{0:T(1024)(128)(4,1)S(1)}, s32[]{:S(2)}) async-start(s8[11141120]{0:T(1024)(128)(4,1)} %bitcast.143), calls=%async_computation.9 | async-start | bytes 5505024
  730.4 13.3 %copy-start.32 = (bf16[8,4,80,768]{3,2,1,0:T(8,128)(2,1)S(1)}, bf16[8,4,80,768]{3,2,1,0:T(8,128)(2,1)}, u32[]{:S(2)}) copy-start(bf16[8,4,80,768]{3,2,1,0:T(8,128)(2,1)} %get-tuple-element.48) | copy-start | bytes 11796484
  754.6 9.6 copy-start.2
  754.6 9.5 copy-start.3
  754.6 9.5 copy-start.4
  754.6 9.5 copy-start.5
  754.6 9.5 copy-start.6
  754.6 9.5 copy-start.7
  801.1 3.1 copy-start.11
  801.1 3.1 copy-start.30
  801.4 1.5 copy-start.21
  814.3 3.0 copy-start.15
  821.9 9.6 copy-start.18
  821.9 9.6 copy-start.22
  986.1 5.5 copy-start.24
  986.1 7.7 copy-start.20
  993.8 2.8 copy-start.9
  993.8 3.7 copy-start.16
  997.5 1.3 copy-start.13
  997.5 1.3 copy-start.26
  998.8 5.4 copy-start.1
Sparse Core Ops, SparseCore 0:
  9.9 118.5 all-gather.2
  597.0 92.1 all-gather.4
  715.8 84.8 reduce-scatter.2
  817.4 94.5 reduce-scatter.4

commit v4 on v3

--- a/solution.py
+++ b/solution.py
@@ -2,6 +2,7 @@
 
 import jax
 import jax.numpy as jnp
+import numpy as np
 from jax import lax
 from jax.experimental import pallas as pl
 from jax.experimental.pallas import tpu as pltpu
@@ -698,9 +699,19 @@
                 y = nn(low_inner, w_down[:, at : at + TILE]) * gate
                 y_out[sources, :, at : at + TILE] = y.astype(BF).reshape(half, capacity, TILE)
 
-        back_kept(step, group).start()
-        for offset in range(1, n_fsdp):
-            back_copy(step, group, offset).start()
+        def send_back(step, group):
+            back_kept(step, group).start()
+            for offset in range(1, n_fsdp):
+                back_copy(step, group, offset).start()
+
+        @pl.when(step > 0)
+        def _():
+            send_back(step, group)
+
+        @pl.when(step == n_ctx - 1)
+        def _():
+            send_back(0, ctx)
+
         for copy in outputs(group):
             copy.start()
 
@@ -771,7 +782,7 @@
 
         @pl.when(tick >= 3)
         def _():
-            combine(tick - 3)
+            combine(lax.rem(tick - 2, n_ctx))
 
     pltpu.make_async_copy(held.at[ctx], part_ref.at[ctx], part_arrived.at[ctx]).wait()
     for step in range(1, n_ctx):
@@ -1318,7 +1329,9 @@
         return route(picked).reshape(slots, width)
 
     def combine(rows):
-        back = route(rows.reshape(n_fsdp, n_ctx, capacity, width))
+        return gather_slots(route(rows.reshape(n_fsdp, n_ctx, capacity, width)))
+
+    def gather_slots(back):
         return jnp.einsum("gjkt,jgkd->gtd", select, back, preferred_element_type=F32).reshape(
             length, width
         )
@@ -1327,10 +1340,12 @@
     r_all = inverse_rms(x_all)
     hidden = (x_all * r_all * gain_attn).astype(BF)
     qkv = nn(hidden, w_qkv)
-    exponent = jnp.arange(HALF, dtype=F32) * (2.0 / HEAD_SIZE)
-    angles = jnp.arange(length, dtype=F32)[:, None] * (ROPE_BASE ** (-exponent))[None, :]
-    cosine = jnp.tile(jnp.cos(angles), (1, 2))
-    sine = jnp.concatenate([-jnp.sin(angles), jnp.sin(angles)], axis=1)
+    exponent = np.arange(HALF, dtype=np.float32) * np.float32(2.0 / HEAD_SIZE)
+    angles = np.arange(length, dtype=np.float32)[:, None] * (
+        np.float32(ROPE_BASE) ** (-exponent)
+    )
+    cosine = jnp.asarray(np.tile(np.cos(angles), (1, 2)))
+    sine = jnp.asarray(np.concatenate([-np.sin(angles), np.sin(angles)], axis=1))
     own_blocks = jnp.broadcast_to(block_ids, (8, length))
     key_blocks = block_ids.reshape(length, 1)
     piece = QUERY_HEADS * HEAD_SIZE // experts
@@ -1446,12 +1461,14 @@
     d_resid = grad + r_ffn * n - resid * r_ffn**3 * jnp.mean(n * resid, axis=-1, keepdims=True)
     ffn_gain_grad = jnp.sum(d_normed * resid * r_ffn, axis=0)
     d_attn = gather_ctx(d_resid.astype(BF))
-    y_all = combine(y).astype(BF)
-    d_attn, gate_grad, up_grad, down_grad = lax.optimization_barrier(
-        (d_attn, gate_grad, up_grad, down_grad)
-    )
+    y_back = route(y.reshape(n_fsdp, n_ctx, capacity, width))
+    y_back, gate_grad, up_grad, down_grad = lax.optimization_barrier(
+        (y_back, gate_grad, up_grad, down_grad)
+    )
+    y_all = gather_slots(y_back).astype(BF)
+    d_attn, y_all = lax.optimization_barrier((d_attn, y_all))
+
     d_mixed = nt(d_attn, out_here).astype(BF)
-
     moe = scatter_ctx(y_all).astype(F32)
     out_grad = jnp.einsum("ntk,td->nkd", dealt, d_attn, preferred_element_type=F32).astype(BF)
 
@@ -1477,12 +1494,13 @@
         ],
         axis=1,
     )
-    d_hidden, moe = lax.optimization_barrier((d_hidden.astype(BF), moe))
+    shared_grad = tn(hidden, d_qkv).astype(BF)
+    d_hidden, moe, shared_grad, out_grad = lax.optimization_barrier(
+        (d_hidden.astype(BF), moe, shared_grad, out_grad)
+    )
     d_hidden = scatter_ctx(d_hidden).astype(F32)
     shared_grad, rest, out_grad = run_last_reduce(
-        n_ctx,
-        n_fsdp,
-        [tn(hidden, d_qkv).astype(BF), extra_grad, out_grad.reshape(n_fsdp * piece, width)],
+        n_ctx, n_fsdp, [shared_grad, extra_grad, out_grad.reshape(n_fsdp * piece, width)]
     )
     out_grad = out_grad.reshape(n_ctx * piece, width).astype(F32)
     rest = rest.astype(F32).sum(axis=0)

time: 1010 us -> 940 us (0.931)
  waiting for transfers between devices: 110 us -> 76.6 us
  Pallas kernels: 705 us -> 675 us
    all_to_all x1, waiting for transfers between devices: 109 us -> 70.6 us  [route(): return lax.all_to_all(rows, 'fsdp', split_axis=0, concat_axis=0, tiled=True)]
    pallas_call x1, Pallas kernels: 291 us -> 263 us  [run_expert_exchange(): pl.pallas_call(functools.partial(expert_exchange, n_ctx, n_fsdp), in_spec...]
  transfers between devices with their start and end apart: 5 -> 5, of which waited for: 1 -> 2; matrix products, arithmetic and copies ran while one was open for 15% -> 15% of each run, Pallas kernels for 26% -> 30%
where the time goes in v4:
time: 940 us; the launch traced here: 934 us
  Pallas kernels  675 us (72%)
  matrix products  89.8 us (10%)
  waiting for transfers between devices  76.6 us (8%)
  other arithmetic  34.7 us (4%)
  local copies, waits for them, and re-layouts  34.1 us (4%)
  between operations  14.7 us (2%)
    pallas_call x1, Pallas kernels, run_expert_exchange(): pl.pallas_call(functools.partial(expert_exchange, n_ctx, n_fsdp), in_spec...  263 us
    pallas_call x1, Pallas kernels, run_last_reduce(): pl.pallas_call(functools.partial(last_reduce, n_ctx, n_fsdp), in_specs=[a...  152 us
    pallas_call x1, Pallas kernels, run_attention_exchange(): pl.pallas_call(functools.partial(attention_exchange, n_ctx, n_fsdp, heads...  136 us
    pallas_call x1, Pallas kernels, run_first_gather(): pl.pallas_call(functools.partial(first_gather, n_ctx, n_fsdp), in_specs=[...  83.2 us
    all_to_all x1, waiting for transfers between devices, route(): return lax.all_to_all(rows, 'fsdp', split_axis=0, concat_axis=0, tiled=True)  70.6 us
    dot_general x5, matrix products, tn(): lax.dot_general(a, b, (((0,), (0,)), ((), ())), preferred_element_type=F32)  46.2 us
    pallas_call x1, Pallas kernels, run_attention_back(): pl.pallas_call(functools.partial(attention_backward, heads), grid=(heads,...  37 us
  transfers between devices with their start and end apart: 5, of which 2 were waited for; matrix products, arithmetic and copies ran while one was open for 15% of the time, Pallas kernels for 30%

profile of v4, /device:TPU:0, one launch (start us, length us, event | category | flops | bytes accessed | tf_op | source)
XLA Modules:
  0.0 933.7 jit_solution(2624016652727880373)
XLA Ops:
  11.0 0.8 copy.118
  11.9 0.9 constant_dynamic-slice_fusion
  12.9 1.1 concatenate.20.packed_ref
  14.7 83.2 %shard_map.290 = (bf16[4,256,2048]{2,1,0:T(8,128)(2,1)}, s32[4,16,256]{2,1,0:T(8,128)}, bf16[8,256,1408]{2,1,0:T(8,128)(2,1)}) custom-call(bf16[256,2048]{1,0:T(8,128)(2,1)} %bitcast.103, s32[16,256]{1,0:T(8,128)} %add_add_fusion.table_ref, bf16[256,1408]{1,0:T(8,128)(2,1)} %concatenate.20.packed_ref), custom_call_target="tpu_custom_call" | custom-call | bytes 209715200 | tf_op jit(solution)/shard_map/pallas_call | solution.py:463
  99.4 1.1 slice.98
  100.7 3.3 fusion.6
  104.8 1.7 eq.53
  106.5 2.1 copy.124
  108.7 1.3 compare_convert_fusion
  110.0 2.4 copy.126.sel_ref
  112.4 1.0 copy.125.key_ref
  114.4 1.3 fusion.63.selt_ref
  115.7 3.9 fusion.8
  119.6 2.0 copy-done.15
  121.6 7.3 fusion.13.q_ref.k_ref.v_ref
  129.5 136.2 %shard_map.291 = (f32[8,8,1024]{2,1,0:T(8,128)}, bf16[4,1024,256]{2,1,0:T(8,128)(2,1)}, f32[256,2048]{1,0:T(8,128)}, bf16[8,4,80,2048]{3,2,1,0:T(8,128)(2,1)}) custom-call(f32[1024,1280]{1,0:T(8,128)} %fusion.13.q_ref.k_ref.v_ref, f32[1024,1280]{1,0:T(8,128)} %fusion.13.q_ref.k_ref.v_ref, f32[1024,1280]{1,0:T(8,128)} %fusion.13.q_ref.k_ref.v_ref, ...), custom_call_target="tpu_custom_call" | custom-call | flops 4294967296 | bytes 419430400 | tf_op jit(solution)/shard_map/pallas_call | solution.py:1169
  265.7 1.9 multiply_reduce_fusion.2
  267.9 1.5 fusion.47
  269.8 1.9 concatenate.22.x_ref
  271.7 262.5 %shard_map.292 = (bf16[8,4,80,2176]{3,2,1,0:T(8,128)(2,1)}, bf16[4,8,80,2176]{3,2,1,0:T(8,128)(2,1)}, bf16[4,256,2176]{2,1,0:T(8,128)(2,1)}, bf16[8,4,80,768]{3,...) custom-call(bf16[256,2176]{1,0:T(8,128)(2,1)} %concatenate.22.x_ref,, ...), custom_call_target="tpu_custom_call" | custom-call | flops 48318382080 | bytes 629145600 | tf_op jit(solution)/shard_map/pallas_call | solution.py:820
  534.3 8.1 all-to-all-start
  542.4 3.1 convert_reduce_fusion
  546.1 1.8 multiply_reduce_fusion
  547.9 2.3 fusion.46
  550.5 14.1 %convolution_bitcast_fusion = f32[768,2048]{1,0:T(8,128)} fusion(bf16[8,4,80,768]{3,2,1,0:T(8,128)(2,1)} %get-tuple-element.55, bf16[8,4,80,2048]{3,2,1,0:T(8,128)(2,1)} %get-tuple-element.48.grad_ref), kind=kOutput, calls=%fused_computation.25 | convolution fusion | flops 8053063680 | bytes 20709376 | tf_op jit(solution)/shard_map/dot_general | solution.py:34
  564.6 13.3 %fusion.2 = f32[2048,768]{1,0:T(8,128)} fusion(bf16[2560,768]{1,0:T(8,128)(2,1)S(1)} %bitcast.152, bf16[2560,2176]{1,0:T(8,128)(2,1)} %bitcast.144), kind=kOutput, calls=%fused_computation.2 | convolution fusion | flops 8053063680 | bytes 20709376 | tf_op jit(solution)/shard_map/dot_general | solution.py:34
  577.9 11.1 %fusion.4 = f32[2048,768]{1,0:T(8,128)} fusion(bf16[2560,768]{1,0:T(8,128)(2,1)S(1)} %bitcast.151, bf16[2560,2176]{1,0:T(8,128)(2,1)S(1)} %bitcast.147), kind=kOutput, calls=%fused_computation.4 | convolution fusion | flops 8053063680 | bytes 20709376 | tf_op jit(solution)/shard_map/dot_general | solution.py:34
  588.9 70.6 %all-to-all-done = bf16[8,4,80,2048]{3,2,1,0:T(8,128)(2,1)} async-done(((bf16[8,4,80,2048]{3,2,1,0:T(8,128)(2,1)}), bf16[8,4,80,2048]{3,2,1,0:T(8,128)(2,1)}, u32[]{:S(2)}, u32[]{:S(2)}) %all-to-all-start) | async-done | bytes 10485792 | tf_op jit(solution)/shard_map/all_to_all | solution.py:1266
  659.6 9.5 %bitcast_convert_fusion = bf16[4,256,2048]{2,1,0:T(8,128)(2,1)} fusion(bf16[8,4,80,2048]{3,2,1,0:T(8,128)(2,1)} %all-to-all-done, s32[4,8,256]{2,1,0:T(8,128)S(1)} %fusion.33), kind=kOutput, calls=%fused_computation.7 | convolution fusion | flops 2687107072 | bytes 14712832 | tf_op jit(solution)/shard_map/gjkt,jgkd->gtd/dot_general | solution.py:1335
  669.2 9.5 %fusion.29.grad_ref = bf16[1024,1024]{1,0:T(8,128)(2,1)} fusion(bf16[1024,2048]{1,0:T(8,128)(2,1)} %all-gather.5.cloned.1.call-done, bf16[4096,2048]{1,0:T(8,128)(2,1)} %all-gather.3.cloned.1.call-done.out_ref, s32[]{:T(128)S(6)} %select_n.20), kind=kOutput, calls=%fused_computation.48 | convolution fusion | flops 4296015872 | bytes 10485764 | tf_op jit(solution)/shard_map/dot_general | solution.py:26
  678.7 37.0 %shard_map.293 = (bf16[1024,1024]{1,0:T(8,128)(2,1)S(1)}, bf16[1024,256]{1,0:T(8,128)(2,1)S(1)}, f32[8,128]{1,0:T(8,128)S(1)}) custom-call(f32[1024,1280]{1,0:T(8,128)} %fusion.13.q_ref.k_ref.v_ref, f32[1024,1280]{1,0:T(8,128)} %fusion.13.q_ref.k_ref.v_ref, f32[1024,1280]{1,0:T(8,128)} %fusion.13.q_ref.k_ref.v_ref, bf16[1024,1024]{1,0:T(8,128)(2,1)} %fusion.29.grad_ref, ...), custom_call_target="tpu_custom_call" | custom-call | flops 10737418240 | bytes 10485760 | tf_op jit(solution)/shard_map/pallas_call | solution.py:222
  716.0 1.9 copy-done.28
  717.9 6.2 fusion.21
  724.1 7.5 convolution_convert_fusion
  731.7 7.5 fusion.10
  739.2 5.3 reduce-scatter.3.cloned.1.call-done
  744.5 2.8 convert_element_type.120
  749.5 2.3 concatenate.24
  751.9 152.2 %shard_map.294 = (bf16[4,256,1280]{2,1,0:T(8,128)(2,1)}, bf16[4,256,128]{2,1,0:T(8,128)(2,1)}, bf16[4,128,2048]{2,1,0:T(8,128)(2,1)}) custom-call(bf16[4,2,256,1280]{3,2,1,0:T(8,128)(2,1)} %bitcast.105, bf16[4,2,256,128]{3,2,1,0:T(8,128)(2,1)} %bitcast.110, bf16[4,2,128,2048]{3,2,1,0:T(8,128)(2,1)} %bitcast.106), custom_call_target="tpu_custom_call" | custom-call | bytes 419430400 | tf_op jit(solution)/shard_map/pallas_call | solution.py:966
  904.1 4.2 shard_map.295
  908.3 1.3 convert_bitcast_fusion
  909.6 1.0 copy.138
  910.6 2.0 copy.140
  912.8 1.0 copy.141
  916.1 2.8 fusion.34
  918.9 2.7 bitcast_convert_fusion.1
  921.6 1.9 fusion.24
  923.5 3.5 fusion.35
  (157 shorter events, 15.0 us)
Async XLA Ops:
  7.2 5.6 copy-start
  7.2 6.8 copy-start.23
  7.2 6.8 copy-start.27
  7.2 121.7 %all-gather.3.cloned.1.call-start = ((), (), s32[]{:S(2)}) async-start(), calls=%async_computation.3 | async-start | bytes 18874368 | tf_op jit(solution)/shard_map/all_gather | solution.py:1292
  100.7 5.8 copy-start.19
  104.0 11.7 %copy-start.25 = (f32[1,2,4,128]{3,1,2,0:T(2,128)}, f32[1,2,4,128]{3,1,2,0:T(2,128)S(1)}, u32[]{:S(2)}) copy-start(f32[1,2,4,128]{3,1,2,0:T(2,128)S(1)} %copy.149) | copy-start | bytes 12292
  104.1 11.6 %copy-start.21 = (f32[1,2048]{1,0:T(1,128)}, f32[1,2048]{1,0:T(1,128)S(1)}, u32[]{:S(2)}) copy-start(f32[1,2048]{1,0:T(1,128)S(1)} %get-tuple-element.151) | copy-start | bytes 24580
  108.7 3.7 copy-start.24
  114.4 7.2 slice-start
  115.7 5.9 slice-start.1
  119.6 2.0 copy-start.15
  129.5 136.2 %copy-start.11 = (bf16[1,256,2048]{2,1,0:T(8,128)(2,1)S(1)}, bf16[1,256,2048]{2,1,0:T(8,128)(2,1)}, u32[]{:S(2)}) copy-start(bf16[1,256,2048]{2,1,0:T(8,128)(2,1)} %param.19) | copy-start | bytes 3145732
  267.6 280.3 %copy-start.8 = (f32[256,2048]{1,0:T(8,128)}, f32[256,2048]{1,0:T(8,128)S(1)}, u32[]{:S(2)}) copy-start(f32[256,2048]{1,0:T(8,128)S(1)} %get-tuple-element.145) | copy-start | bytes 6291460
  267.9 266.4 %copy-start.13 = (bf16[256,2048]{1,0:T(8,128)(2,1)}, bf16[256,2048]{1,0:T(8,128)(2,1)S(1)}, u32[]{:S(2)}) copy-start(bf16[256,2048]{1,0:T(8,128)(2,1)S(1)} %multiply_convert_fusion) | copy-start | bytes 3145732
  534.3 125.3 %all-to-all-start = ((bf16[8,4,80,2048]{3,2,1,0:T(8,128)(2,1)}), bf16[8,4,80,2048]{3,2,1,0:T(8,128)(2,1)}, u32[]{:S(2)}, u32[]{:S(2)}) async-start(bf16[8,4,80,2048]{3,2,1,0:T(8,128)(2,1)} %get-tuple-element.51), calls=%async_computation | async-start | bytes 20971520 | tf_op jit(solution)/shard_map/all_to_all | solution.py:1266
  542.4 126.6 %all-gather.5.cloned.1.call-start = ((), (), s32[]{:S(2)}) async-start(), calls=%async_computation.4 | async-start | bytes 5242880 | tf_op jit(solution)/shard_map/all_gather | solution.py:1260
  546.1 1.8 copy-start.17
  550.2 194.2 %reduce-scatter.3.cloned.1.call-start = ((), (), s32[]{:S(2)}) async-start(), calls=%async_computation.5 | async-start | bytes 5242880 | tf_op jit(solution)/shard_map/reduce_scatter | solution.py:1263
  550.5 14.1 %copy-start.30 = (bf16[8,4,80,768]{3,2,1,0:T(8,128)(2,1)S(1)}, bf16[8,4,80,768]{3,2,1,0:T(8,128)(2,1)}, u32[]{:S(2)}) copy-start(bf16[8,4,80,768]{3,2,1,0:T(8,128)(2,1)} %get-tuple-element.54) | copy-start | bytes 11796484
  550.5 27.4 %slice-start.4 = ((s8[11141120]{0:T(1024)(128)(4,1)}), s8[4194304]{0:T(1024)(128)(4,1)S(1)}, s32[]{:S(2)}) async-start(s8[11141120]{0:T(1024)(128)(4,1)} %bitcast.145), calls=%async_computation.11 | async-start | bytes 8388608
  550.5 27.4 %slice-start.5 = ((s8[11141120]{0:T(1024)(128)(4,1)}), s8[4194304]{0:T(1024)(128)(4,1)S(1)}, s32[]{:S(2)}) async-start(s8[11141120]{0:T(1024)(128)(4,1)} %bitcast.145), calls=%async_computation.12 | async-start | bytes 8388608
  564.6 13.3 %slice-start.6 = ((s8[11141120]{0:T(1024)(128)(4,1)}), s8[2752512]{0:T(1024)(128)(4,1)S(1)}, s32[]{:S(2)}) async-start(s8[11141120]{0:T(1024)(128)(4,1)} %bitcast.145), calls=%async_computation.13 | async-start | bytes 5505024
  564.6 13.3 %copy-start.29 = (bf16[8,4,80,768]{3,2,1,0:T(8,128)(2,1)S(1)}, bf16[8,4,80,768]{3,2,1,0:T(8,128)(2,1)}, u32[]{:S(2)}) copy-start(bf16[8,4,80,768]{3,2,1,0:T(8,128)(2,1)} %get-tuple-element.53) | copy-start | bytes 11796484
  669.0 9.6 %copy-start.2 = (s32[1024,1]{1,0:T(8,128)S(1)}, s32[1024,1]{1,0:T(8,128)}, u32[]{:S(2)}) copy-start(s32[1024,1]{1,0:T(8,128)} %copy.125.key_ref) | copy-start | bytes 12292
  669.1 9.6 %copy-start.3 = (f32[1024,128]{1,0:T(8,128)S(1)}, f32[1024,128]{1,0:T(8,128)}, u32[]{:S(2)}) copy-start(f32[1024,128]{1,0:T(8,128)} %constant.63.clone.cos_ref) | copy-start | bytes 1572868
  669.1 9.6 %copy-start.4 = (f32[1024,128]{1,0:T(8,128)S(1)}, f32[1024,128]{1,0:T(8,128)}, u32[]{:S(2)}) copy-start(f32[1024,128]{1,0:T(8,128)} %constant.64.clone.sin_ref) | copy-start | bytes 1572868
  669.1 9.6 %copy-start.5 = (s32[8,1024]{1,0:T(8,128)S(1)}, s32[8,1024]{1,0:T(8,128)}, u32[]{:S(2)}) copy-start(s32[8,1024]{1,0:T(8,128)} %broadcast_in_dim.78.own_ref) | copy-start | bytes 98308
  669.1 9.6 %copy-start.6 = (f32[8,128]{1,0:T(8,128)S(1)}, f32[8,128]{1,0:T(8,128)}, u32[]{:S(2)}) copy-start(f32[8,128]{1,0:T(8,128)} %maximum_convert_fusion.gains_ref) | copy-start | bytes 12292
  669.1 9.6 %copy-start.7 = (f32[8,8,1024]{2,1,0:T(8,128)S(1)}, f32[8,8,1024]{2,1,0:T(8,128)}, u32[]{:S(2)}) copy-start(f32[8,8,1024]{2,1,0:T(8,128)} %get-tuple-element.58.total_ref) | copy-start | bytes 786436
  669.1 252.5 %reduce-scatter.5.cloned.1.call-start = ((), (), s32[]{:S(2)}) async-start(), calls=%async_computation.6 | async-start | bytes 5242880 | tf_op jit(solution)/shard_map/reduce_scatter | solution.py:1263
  678.7 37.3 %copy-start.31 = (bf16[4,1024,256]{2,1,0:T(8,128)(2,1)S(1)}, bf16[4,1024,256]{2,1,0:T(8,128)(2,1)}, u32[]{:S(2)}) copy-start(bf16[4,1024,256]{2,1,0:T(8,128)(2,1)} %get-tuple-element.62) | copy-start | bytes 6291460
  715.7 2.2 copy-start.28
  717.9 6.2 copy-start.16
  717.9 13.7 %slice-start.2 = ((s8[5767168]{0:T(1024)(128)(4,1)}), s8[4194304]{0:T(1024)(128)(4,1)S(1)}, s32[]{:S(2)}) async-start(s8[5767168]{0:T(1024)(128)(4,1)} %bitcast.128), calls=%async_computation.9 | async-start | bytes 8388608
  724.1 7.5 copy-start.10
  724.1 7.5 slice-start.3
  724.1 7.5 copy-start.26
  739.2 8.1 copy-start.14
  908.3 5.5 copy-start.20
  908.3 7.7 copy-start.9
  914.6 4.3 copy-start.18
  918.9 2.7 copy-start.12
  918.9 2.7 copy-start.22
  921.6 5.4 copy-start.1
Sparse Core Ops, SparseCore 0:
  9.9 118.5 all-gather.2
  550.4 82.5 all-gather.4
  669.2 75.2 reduce-scatter.2
  747.4 103.5 reduce-scatter.4

commit v5 on v4

--- a/solution.py
+++ b/solution.py
@@ -976,19 +976,100 @@
     )(*grads)
 
 
-def widen_columns(in_ref, out_ref):
-    out_ref[...] = in_ref[0].astype(F32)
-
-
-def run_widen_columns(blocks, columns):
-    n, rows, _ = blocks.shape
+def finish(
+    n_ctx,
+    share,
+    experts,
+    shared_ref,
+    rest_ref,
+    out_ref,
+    dh_ref,
+    x_ref,
+    resid_grad_ref,
+    resid_ref,
+    moe_ref,
+    gain_ref,
+    query_ref,
+    key_ref,
+    value_ref,
+    out_grad_ref,
+    input_grad_ref,
+    output_ref,
+    router_ref,
+    gains_ref,
+):
+    q_width = shared_ref.shape[2] - 2 * HEAD_SIZE
+    for block in range(n_ctx):
+        query_ref[:, block * q_width : (block + 1) * q_width] = shared_ref[
+            block, :, :q_width
+        ].astype(F32)
+    for target, at in ((key_ref, q_width), (value_ref, q_width + HEAD_SIZE)):
+        for kv in range(KEY_VALUE_HEADS):
+            total = shared_ref[kv * share, :, at : at + HEAD_SIZE].astype(F32)
+            for block in range(kv * share + 1, (kv + 1) * share):
+                total = total + shared_ref[block, :, at : at + HEAD_SIZE].astype(F32)
+            target[:, kv * HEAD_SIZE : (kv + 1) * HEAD_SIZE] = total
+    out_grad_ref[...] = out_ref[0].astype(F32)
+    x = x_ref[...].astype(F32)
+    r = inverse_rms(x)
+    n = dh_ref[...].astype(F32) * gain_ref[...]
+    input_grad_ref[...] = (
+        resid_grad_ref[...] + r * n - x * (r * r * r) * jnp.mean(n * x, axis=-1, keepdims=True)
+    ).astype(BF)
+    output_ref[...] = (resid_ref[...] + moe_ref[...].astype(F32)).astype(BF)
+
+    @pl.when(pl.program_id(0) == n_ctx - 1)
+    def _():
+        rest = rest_ref[0].astype(F32)
+        for block in range(1, n_ctx):
+            rest = rest + rest_ref[block].astype(F32)
+        router_ref[...] = rest[:, :experts]
+        gains_ref[...] = rest.T[experts : experts + 8]
+
+
+def run_finish(
+    n_ctx, experts, shared, rest, out_grad, d_hidden, x, resid_grad, resid, moe, gain
+):
+    _, rows, wide = shared.shape
+    span, width = x.shape
+    _, piece, _ = out_grad.shape
+    shape = jax.ShapeDtypeStruct
+    part, tokens = rows // n_ctx, span // n_ctx
+    whole = lambda dims: pl.BlockSpec(dims, lambda i: (0,) * len(dims))
+    by_rows = lambda count, columns: pl.BlockSpec((count, columns), lambda i: (i, 0))
+    q_columns, kv_columns = QUERY_HEADS * HEAD_SIZE, KEY_VALUE_HEADS * HEAD_SIZE
     return pl.pallas_call(
-        widen_columns,
-        grid=(n,),
-        in_specs=[pl.BlockSpec((1, rows, columns), lambda i: (i, 0, 0))],
-        out_specs=pl.BlockSpec((rows, columns), lambda i: (0, i)),
-        out_shape=jax.ShapeDtypeStruct((rows, n * columns), F32),
-    )(blocks)
+        functools.partial(finish, n_ctx, n_ctx // KEY_VALUE_HEADS, experts),
+        grid=(n_ctx,),
+        in_specs=[
+            pl.BlockSpec((n_ctx, part, wide), lambda i: (0, i, 0)),
+            whole(rest.shape),
+            pl.BlockSpec((1, piece, width), lambda i: (i, 0, 0)),
+        ]
+        + [by_rows(tokens, width)] * 5
+        + [whole((1, width))],
+        out_specs=[
+            by_rows(part, q_columns),
+            by_rows(part, kv_columns),
+            by_rows(part, kv_columns),
+            by_rows(piece, width),
+            by_rows(tokens, width),
+            by_rows(tokens, width),
+            whole((rows, experts)),
+            whole((8, rows)),
+        ],
+        out_shape=[
+            shape((rows, q_columns), F32),
+            shape((rows, kv_columns), F32),
+            shape((rows, kv_columns), F32),
+            shape((n_ctx * piece, width), F32),
+            shape((span, width), BF),
+            shape((span, width), BF),
+            shape((rows, experts), F32),
+            shape((8, rows), F32),
+        ],
+        compiler_params=pltpu.CompilerParams(vmem_limit_bytes=48 * 2**20),
+    )(shared, rest, out_grad, d_hidden, x, resid_grad, resid, moe, gain)
 
 
 def attention_exchange(
@@ -1254,7 +1335,7 @@
     own_rows = w_query.shape[0]
     q_width = heads * HEAD_SIZE
     qkv_width = q_width + 2 * HEAD_SIZE
-    extra_width = -(-(experts + 4) // 128) * 128
+    extra_width = -(-(experts + 8) // 128) * 128
 
     def gather_ctx(array):
         return lax.all_gather(array, "ctx", axis=0, tiled=True)
@@ -1469,7 +1550,7 @@
     d_attn, y_all = lax.optimization_barrier((d_attn, y_all))
 
     d_mixed = nt(d_attn, out_here).astype(BF)
-    moe = scatter_ctx(y_all).astype(F32)
+    moe = scatter_ctx(y_all)
     out_grad = jnp.einsum("ntk,td->nkd", dealt, d_attn, preferred_element_type=F32).astype(BF)
 
     dq, dkv, dgains = run_attention_back(
@@ -1498,39 +1579,38 @@
     d_hidden, moe, shared_grad, out_grad = lax.optimization_barrier(
         (d_hidden.astype(BF), moe, shared_grad, out_grad)
     )
-    d_hidden = scatter_ctx(d_hidden).astype(F32)
+    d_hidden = scatter_ctx(d_hidden)
     shared_grad, rest, out_grad = run_last_reduce(
         n_ctx, n_fsdp, [shared_grad, extra_grad, out_grad.reshape(n_fsdp * piece, width)]
     )
-    out_grad = out_grad.reshape(n_ctx * piece, width).astype(F32)
-    rest = rest.astype(F32).sum(axis=0)
-    output = (resid + moe).astype(BF)[None]
-    r_attn = inverse_rms(x)
-    n = d_hidden * gain_attn
-    input_grad = d_resid + r_attn * n - x * r_attn**3 * jnp.mean(n * x, axis=-1, keepdims=True)
-    input_grad = input_grad.astype(BF)[None]
-
-    query_grad = run_widen_columns(shared_grad, q_width)
-
-    def kv_grad(at):
-        parts = shared_grad[:, :, at : at + HEAD_SIZE].astype(F32)
-        parts = parts.reshape(KEY_VALUE_HEADS, share, own_rows, HEAD_SIZE).sum(axis=1)
-        return parts.transpose(1, 0, 2).reshape(own_rows, KEY_VALUE_HEADS * HEAD_SIZE)
-
-    key_grad, value_grad = kv_grad(q_width), kv_grad(q_width + HEAD_SIZE)
+    query_grad, key_grad, value_grad, out_grad, input_grad, output, router_grad, gain_grads = (
+        run_finish(
+            n_ctx,
+            experts,
+            shared_grad,
+            rest,
+            out_grad,
+            d_hidden,
+            inputs[0],
+            d_resid,
+            resid,
+            moe,
+            gain_attn,
+        )
+    )
     head_rows = HEAD_SIZE // n_fsdp
     return (
-        output,
-        input_grad,
-        rest[:, experts],
+        output[None],
+        input_grad[None],
+        gain_grads[0],
         query_grad,
         key_grad,
         value_grad,
-        rest[:head_rows, experts + 2],
-        rest[:head_rows, experts + 3],
+        gain_grads[2, :head_rows],
+        gain_grads[3, :head_rows],
         out_grad,
-        rest[:, experts + 1],
-        rest[:, :experts],
+        gain_grads[1],
+        router_grad,
         gate_grad[None],
         up_grad[None],
         down_grad[None],

time: 940 us -> 934 us (level)
  other arithmetic: 34.7 us -> 19.6 us
  transfers between devices with their start and end apart: 5 -> 5, of which waited for: 2 -> 2; matrix products, arithmetic and copies ran while one was open for 15% -> 13% of each run, Pallas kernels for 30% -> 30%
where the time goes in v5:
time: 934 us; the launch traced here: 927 us
  Pallas kernels  682 us (73%)
  matrix products  87.5 us (9%)
  waiting for transfers between devices  77.9 us (8%)
  local copies, waits for them, and re-layouts  36.9 us (4%)
  other arithmetic  19.6 us (2%)
  between operations  14.9 us (2%)
    pallas_call x1, Pallas kernels, run_expert_exchange(): pl.pallas_call(functools.partial(expert_exchange, n_ctx, n_fsdp), in_spec...  263 us
    pallas_call x1, Pallas kernels, run_last_reduce(): pl.pallas_call(functools.partial(last_reduce, n_ctx, n_fsdp), in_specs=[a...  155 us
    pallas_call x1, Pallas kernels, run_attention_exchange(): pl.pallas_call(functools.partial(attention_exchange, n_ctx, n_fsdp, heads...  136 us
    pallas_call x1, Pallas kernels, run_first_gather(): pl.pallas_call(functools.partial(first_gather, n_ctx, n_fsdp), in_specs=[...  83.2 us
    all_to_all x1, waiting for transfers between devices, route(): return lax.all_to_all(rows, 'fsdp', split_axis=0, concat_axis=0, tiled=True)  71.8 us
    dot_general x5, matrix products, tn(): lax.dot_general(a, b, (((0,), (0,)), ((), ())), preferred_element_type=F32)  46.1 us
    pallas_call x1, Pallas kernels, run_attention_back(): pl.pallas_call(functools.partial(attention_backward, heads), grid=(heads,...  37 us
  transfers between devices with their start and end apart: 5, of which 2 were waited for; matrix products, arithmetic and copies ran while one was open for 13% of the time, Pallas kernels for 30%

profile of v5, /device:TPU:0, one launch (start us, length us, event | category | flops | bytes accessed | tf_op | source)
XLA Modules:
  0.0 927.4 jit_solution(13425652098371761386)
XLA Ops:
  9.5 0.8 broadcast_in_dim.86
  10.3 0.8 broadcast_in_dim.87
  11.0 0.8 copy.67
  11.9 0.9 constant_dynamic-slice_fusion
  12.9 1.1 concatenate.20.packed_ref
  14.7 83.2 %shard_map.290 = (bf16[4,256,2048]{2,1,0:T(8,128)(2,1)}, s32[4,16,256]{2,1,0:T(8,128)}, bf16[8,256,1408]{2,1,0:T(8,128)(2,1)}) custom-call(bf16[256,2048]{1,0:T(8,128)(2,1)} %bitcast.94, s32[16,256]{1,0:T(8,128)} %add_add_fusion.table_ref, bf16[256,1408]{1,0:T(8,128)(2,1)} %concatenate.20.packed_ref), custom_call_target="tpu_custom_call" | custom-call | bytes 209715200 | tf_op jit(solution)/shard_map/pallas_call | solution.py:463
  97.9 0.8 slice.72
  98.6 0.8 slice.73
  99.4 1.1 slice.86
  100.7 3.1 fusion.6
  104.6 1.7 eq.53
  106.3 2.1 copy.73
  108.5 1.3 compare_convert_fusion
  109.8 2.5 copy.75.sel_ref
  112.3 1.0 copy.74.key_ref
  114.2 1.3 fusion.57.selt_ref
  115.5 3.9 fusion.8
  119.4 2.0 copy-done.20
  121.4 7.3 fusion.11.q_ref.k_ref.v_ref
  129.4 136.3 %shard_map.291 = (f32[8,8,1024]{2,1,0:T(8,128)}, bf16[4,1024,256]{2,1,0:T(8,128)(2,1)}, f32[256,2048]{1,0:T(8,128)}, bf16[8,4,80,2048]{3,2,1,0:T(8,128)(2,1)}) custom-call(f32[1024,1280]{1,0:T(8,128)} %fusion.11.q_ref.k_ref.v_ref, f32[1024,1280]{1,0:T(8,128)} %fusion.11.q_ref.k_ref.v_ref, f32[1024,1280]{1,0:T(8,128)} %fusion.11.q_ref.k_ref.v_ref, ...), custom_call_target="tpu_custom_call" | custom-call | flops 4294967296 | bytes 419430400 | tf_op jit(solution)/shard_map/pallas_call | solution.py:1250
  265.7 1.9 multiply_reduce_fusion.2
  267.9 1.2 copy-done.18
  270.0 3.0 concatenate.22.x_ref
  273.0 262.5 %shard_map.292 = (bf16[8,4,80,2176]{3,2,1,0:T(8,128)(2,1)}, bf16[4,8,80,2176]{3,2,1,0:T(8,128)(2,1)}, bf16[4,256,2176]{2,1,0:T(8,128)(2,1)}, bf16[8,4,80,768]{3,...) custom-call(bf16[256,2176]{1,0:T(8,128)(2,1)} %concatenate.22.x_ref,, ...), custom_call_target="tpu_custom_call" | custom-call | flops 48318382080 | bytes 629145600 | tf_op jit(solution)/shard_map/pallas_call | solution.py:820
  535.6 8.1 all-to-all-start
  543.7 3.1 convert_reduce_fusion
  547.4 0.8 multiply_reduce_fusion
  548.2 2.3 fusion.39
  550.8 14.1 %convolution_bitcast_fusion = f32[768,2048]{1,0:T(8,128)} fusion(bf16[8,4,80,768]{3,2,1,0:T(8,128)(2,1)} %get-tuple-element.63, bf16[8,4,80,2048]{3,2,1,0:T(8,128)(2,1)} %get-tuple-element.56.grad_ref), kind=kOutput, calls=%fused_computation.25 | convolution fusion | flops 8053063680 | bytes 20709376 | tf_op jit(solution)/shard_map/dot_general | solution.py:34
  564.9 13.3 %fusion.2 = f32[2048,768]{1,0:T(8,128)} fusion(bf16[2560,768]{1,0:T(8,128)(2,1)S(1)} %bitcast.143, bf16[2560,2176]{1,0:T(8,128)(2,1)} %bitcast.135), kind=kOutput, calls=%fused_computation.2 | convolution fusion | flops 8053063680 | bytes 20709376 | tf_op jit(solution)/shard_map/dot_general | solution.py:34
  578.2 10.9 %fusion.4 = f32[2048,768]{1,0:T(8,128)} fusion(bf16[2560,768]{1,0:T(8,128)(2,1)S(1)} %bitcast.142, bf16[2560,2176]{1,0:T(8,128)(2,1)S(1)} %bitcast.138), kind=kOutput, calls=%fused_computation.4 | convolution fusion | flops 8053063680 | bytes 20709376 | tf_op jit(solution)/shard_map/dot_general | solution.py:34
  589.1 71.8 %all-to-all-done = bf16[8,4,80,2048]{3,2,1,0:T(8,128)(2,1)} async-done(((bf16[8,4,80,2048]{3,2,1,0:T(8,128)(2,1)}), bf16[8,4,80,2048]{3,2,1,0:T(8,128)(2,1)}, u32[]{:S(2)}, u32[]{:S(2)}) %all-to-all-start) | async-done | bytes 10485792 | tf_op jit(solution)/shard_map/all_to_all | solution.py:1347
  660.9 9.4 %bitcast_convert_fusion = bf16[4,256,2048]{2,1,0:T(8,128)(2,1)} fusion(bf16[8,4,80,2048]{3,2,1,0:T(8,128)(2,1)} %all-to-all-done, s32[4,8,256]{2,1,0:T(8,128)S(1)} %fusion.28), kind=kOutput, calls=%fused_computation.7 | convolution fusion | flops 2687107072 | bytes 14712832 | tf_op jit(solution)/shard_map/gjkt,jgkd->gtd/dot_general | solution.py:1416
  670.4 9.4 %fusion.24.grad_ref = bf16[1024,1024]{1,0:T(8,128)(2,1)} fusion(bf16[1024,2048]{1,0:T(8,128)(2,1)} %all-gather.5.cloned.1.call-done, bf16[4096,2048]{1,0:T(8,128)(2,1)} %all-gather.3.cloned.1.call-done.out_ref, s32[]{:T(128)S(6)} %select_n.20), kind=kOutput, calls=%fused_computation.37 | convolution fusion | flops 4296015872 | bytes 10485764 | tf_op jit(solution)/shard_map/dot_general | solution.py:26
  679.8 37.0 %shard_map.293 = (bf16[1024,1024]{1,0:T(8,128)(2,1)S(1)}, bf16[1024,256]{1,0:T(8,128)(2,1)S(1)}, f32[8,128]{1,0:T(8,128)S(1)}) custom-call(f32[1024,1280]{1,0:T(8,128)} %fusion.11.q_ref.k_ref.v_ref, f32[1024,1280]{1,0:T(8,128)} %fusion.11.q_ref.k_ref.v_ref, f32[1024,1280]{1,0:T(8,128)} %fusion.11.q_ref.k_ref.v_ref, bf16[1024,1024]{1,0:T(8,128)(2,1)} %fusion.24.grad_ref, ...), custom_call_target="tpu_custom_call" | custom-call | flops 10737418240 | bytes 10485760 | tf_op jit(solution)/shard_map/pallas_call | solution.py:222
  717.1 1.9 copy-done.28
  719.1 6.1 fusion.21
  725.2 7.6 convolution_convert_fusion
  732.8 7.5 fusion.10
  740.4 5.3 reduce-scatter.3.cloned.1.call-done.moe_ref
  748.0 2.3 concatenate.24
  750.4 154.9 %shard_map.294 = (bf16[4,256,1280]{2,1,0:T(8,128)(2,1)}, bf16[4,256,128]{2,1,0:T(8,128)(2,1)}, bf16[4,128,2048]{2,1,0:T(8,128)(2,1)}) custom-call(bf16[4,2,256,1280]{3,2,1,0:T(8,128)(2,1)} %bitcast.98, bf16[4,2,256,128]{3,2,1,0:T(8,128)(2,1)} %bitcast.102, bf16[4,2,128,2048]{3,2,1,0:T(8,128)(2,1)} %bitcast.99), custom_call_target="tpu_custom_call" | custom-call | bytes 419430400 | tf_op jit(solution)/shard_map/pallas_call | solution.py:966
  905.3 1.7 copy-done.5
  907.1 1.2 copy-done.6
  908.3 1.2 copy-done.7
  909.5 0.9 copy-done.10
  910.5 8.2 shard_map.295
  919.7 0.7 copy.87
  (144 shorter events, 11.2 us)
Async XLA Ops:
  7.2 5.6 copy-start
  7.2 6.8 copy-start.23
  7.2 6.8 copy-start.27
  7.2 121.6 %all-gather.3.cloned.1.call-start = ((), (), s32[]{:S(2)}) async-start(), calls=%async_computation.3 | async-start | bytes 18874368 | tf_op jit(solution)/shard_map/all_gather | solution.py:1373
  103.8 11.7 %copy-start.25 = (f32[1,2,4,128]{3,1,2,0:T(2,128)}, f32[1,2,4,128]{3,1,2,0:T(2,128)S(1)}, u32[]{:S(2)}) copy-start(f32[1,2,4,128]{3,1,2,0:T(2,128)S(1)} %copy.96) | copy-start | bytes 12292
  103.9 11.7 %copy-start.12 = (f32[1,2048]{1,0:T(1,128)}, f32[1,2048]{1,0:T(1,128)S(1)}, u32[]{:S(2)}) copy-start(f32[1,2048]{1,0:T(1,128)S(1)} %get-tuple-element.145.gain_ref) | copy-start | bytes 24580
  108.4 3.9 copy-start.24
  114.2 7.2 slice-start
  115.5 5.9 slice-start.1
  119.4 2.0 copy-start.20
  129.4 136.3 %copy-start.2 = (bf16[1,256,2048]{2,1,0:T(8,128)(2,1)S(1)}, bf16[1,256,2048]{2,1,0:T(8,128)(2,1)}, u32[]{:S(2)}) copy-start(bf16[1,256,2048]{2,1,0:T(8,128)(2,1)} %param.19) | copy-start | bytes 3145732
  267.7 280.5 %copy-start.16 = (f32[256,2048]{1,0:T(8,128)}, f32[256,2048]{1,0:T(8,128)S(1)}, u32[]{:S(2)}) copy-start(f32[256,2048]{1,0:T(8,128)S(1)} %get-tuple-element.141.resid_ref) | copy-start | bytes 6291460
  267.9 1.2 copy-start.18
  535.6 125.3 %all-to-all-start = ((bf16[8,4,80,2048]{3,2,1,0:T(8,128)(2,1)}), bf16[8,4,80,2048]{3,2,1,0:T(8,128)(2,1)}, u32[]{:S(2)}, u32[]{:S(2)}) async-start(bf16[8,4,80,2048]{3,2,1,0:T(8,128)(2,1)} %get-tuple-element.59), calls=%async_computation | async-start | bytes 20971520 | tf_op jit(solution)/shard_map/all_to_all | solution.py:1347
  543.7 126.6 %all-gather.5.cloned.1.call-start = ((), (), s32[]{:S(2)}) async-start(), calls=%async_computation.4 | async-start | bytes 5242880 | tf_op jit(solution)/shard_map/all_gather | solution.py:1341
  546.9 1.3 copy-start.22
  550.5 195.2 %reduce-scatter.3.cloned.1.call-start = ((), (), s32[]{:S(2)}) async-start(), calls=%async_computation.5 | async-start | bytes 5242880 | tf_op jit(solution)/shard_map/reduce_scatter | solution.py:1344
  550.8 14.1 %copy-start.30 = (bf16[8,4,80,768]{3,2,1,0:T(8,128)(2,1)S(1)}, bf16[8,4,80,768]{3,2,1,0:T(8,128)(2,1)}, u32[]{:S(2)}) copy-start(bf16[8,4,80,768]{3,2,1,0:T(8,128)(2,1)} %get-tuple-element.62) | copy-start | bytes 11796484
  550.8 27.4 %slice-start.4 = ((s8[11141120]{0:T(1024)(128)(4,1)}), s8[4194304]{0:T(1024)(128)(4,1)S(1)}, s32[]{:S(2)}) async-start(s8[11141120]{0:T(1024)(128)(4,1)} %bitcast.136), calls=%async_computation.11 | async-start | bytes 8388608
  550.8 27.4 %slice-start.5 = ((s8[11141120]{0:T(1024)(128)(4,1)}), s8[4194304]{0:T(1024)(128)(4,1)S(1)}, s32[]{:S(2)}) async-start(s8[11141120]{0:T(1024)(128)(4,1)} %bitcast.136), calls=%async_computation.12 | async-start | bytes 8388608
  564.9 13.3 %slice-start.6 = ((s8[11141120]{0:T(1024)(128)(4,1)}), s8[2752512]{0:T(1024)(128)(4,1)S(1)}, s32[]{:S(2)}) async-start(s8[11141120]{0:T(1024)(128)(4,1)} %bitcast.136), calls=%async_computation.13 | async-start | bytes 5505024
  564.9 13.3 %copy-start.29 = (bf16[8,4,80,768]{3,2,1,0:T(8,128)(2,1)S(1)}, bf16[8,4,80,768]{3,2,1,0:T(8,128)(2,1)}, u32[]{:S(2)}) copy-start(bf16[8,4,80,768]{3,2,1,0:T(8,128)(2,1)} %get-tuple-element.61) | copy-start | bytes 11796484
  670.3 9.5 %copy-start.4 = (s32[1024,1]{1,0:T(8,128)S(1)}, s32[1024,1]{1,0:T(8,128)}, u32[]{:S(2)}) copy-start(s32[1024,1]{1,0:T(8,128)} %copy.74.key_ref) | copy-start | bytes 12292
  670.3 9.5 %copy-start.8 = (f32[1024,128]{1,0:T(8,128)S(1)}, f32[1024,128]{1,0:T(8,128)}, u32[]{:S(2)}) copy-start(f32[1024,128]{1,0:T(8,128)} %constant.61.clone.cos_ref) | copy-start | bytes 1572868
  670.3 9.5 %copy-start.9 = (f32[1024,128]{1,0:T(8,128)S(1)}, f32[1024,128]{1,0:T(8,128)}, u32[]{:S(2)}) copy-start(f32[1024,128]{1,0:T(8,128)} %constant.62.clone.sin_ref) | copy-start | bytes 1572868
  670.3 9.5 %copy-start.11 = (s32[8,1024]{1,0:T(8,128)S(1)}, s32[8,1024]{1,0:T(8,128)}, u32[]{:S(2)}) copy-start(s32[8,1024]{1,0:T(8,128)} %broadcast_in_dim.76.own_ref) | copy-start | bytes 98308
  670.3 9.5 %copy-start.14 = (f32[8,128]{1,0:T(8,128)S(1)}, f32[8,128]{1,0:T(8,128)}, u32[]{:S(2)}) copy-start(f32[8,128]{1,0:T(8,128)} %maximum_convert_fusion.gains_ref) | copy-start | bytes 12292
  670.3 9.5 %copy-start.15 = (f32[8,8,1024]{2,1,0:T(8,128)S(1)}, f32[8,8,1024]{2,1,0:T(8,128)}, u32[]{:S(2)}) copy-start(f32[8,8,1024]{2,1,0:T(8,128)} %get-tuple-element.66.total_ref) | copy-start | bytes 786436
  670.3 234.9 %reduce-scatter.5.cloned.1.call-start = ((), (), s32[]{:S(2)}) async-start(), calls=%async_computation.6 | async-start | bytes 5242880 | tf_op jit(solution)/shard_map/reduce_scatter | solution.py:1344
  679.8 37.3 %copy-start.31 = (bf16[4,1024,256]{2,1,0:T(8,128)(2,1)S(1)}, bf16[4,1024,256]{2,1,0:T(8,128)(2,1)}, u32[]{:S(2)}) copy-start(bf16[4,1024,256]{2,1,0:T(8,128)(2,1)} %get-tuple-element.70) | copy-start | bytes 6291460
  716.9 2.2 copy-start.28
  719.1 6.1 copy-start.21
  719.1 13.7 %slice-start.2 = ((s8[5767168]{0:T(1024)(128)(4,1)}), s8[4194304]{0:T(1024)(128)(4,1)S(1)}, s32[]{:S(2)}) async-start(s8[5767168]{0:T(1024)(128)(4,1)} %bitcast.115), calls=%async_computation.9 | async-start | bytes 8388608
  725.2 7.6 copy-start.17
  725.2 7.6 slice-start.3
  725.2 7.6 copy-start.26
  740.3 5.4 copy-start.19
  750.4 155.0 %copy-start.3 = (bf16[1,256,2048]{2,1,0:T(8,128)(2,1)S(1)}, bf16[1,256,2048]{2,1,0:T(8,128)(2,1)}, u32[]{:S(2)}) copy-start(bf16[1,256,2048]{2,1,0:T(8,128)(2,1)} %param.19) | copy-start | bytes 3145732
  750.4 155.0 %copy-start.13 = (f32[1,2048]{1,0:T(1,128)S(1)}, f32[1,2048]{1,0:T(1,128)}, u32[]{:S(2)}) copy-start(f32[1,2048]{1,0:T(1,128)} %copy-done.12) | copy-start | bytes 24580
  905.3 15.1 %copy-start.1 = (bf16[256,4096]{1,0:T(8,128)(2,1)S(1)}, bf16[256,4096]{1,0:T(8,128)(2,1)}, u32[]{:S(2)}) copy-start(bf16[256,4096]{1,0:T(8,128)(2,1)} %param.24) | copy-start | bytes 6291460
  905.3 1.7 copy-start.5
  907.1 1.2 copy-start.6
  908.3 1.2 copy-start.7
  909.5 0.9 copy-start.10
Sparse Core Ops, SparseCore 0:
  9.9 118.5 all-gather.2
  550.7 82.5 all-gather.4
  670.4 75.2 reduce-scatter.2
  748.5 103.5 reduce-scatter.4

commit v6 on v5

--- a/solution.py
+++ b/solution.py
@@ -508,7 +508,8 @@
     inner_ref,
     dg_ref,
     du_ref,
-    y_ref,
+    y_low_ref,
+    y_high_ref,
     dealt_all,
     w_gate,
     w_up,
@@ -603,7 +604,12 @@
             pltpu.make_async_copy(inner_out, inner_ref.at[:, group], out_sems.at[0]),
             pltpu.make_async_copy(dg_out, dg_ref.at[:, group], out_sems.at[1]),
             pltpu.make_async_copy(du_out, du_ref.at[:, group], out_sems.at[2]),
-            pltpu.make_async_copy(y_out, y_ref.at[:, group], out_sems.at[3]),
+            pltpu.make_async_copy(
+                y_out.at[:, :, : width // 2], y_low_ref.at[:, group], out_sems.at[3]
+            ),
+            pltpu.make_async_copy(
+                y_out.at[:, :, width // 2 :], y_high_ref.at[:, group], out_sems.at[4]
+            ),
         ]
 
     def dispatch(step):
@@ -820,7 +826,7 @@
     return pl.pallas_call(
         functools.partial(expert_exchange, n_ctx, n_fsdp),
         in_specs=[anywhere, inside, inside] + [anywhere] * 5,
-        out_specs=[anywhere] * 8,
+        out_specs=[anywhere] * 9,
         out_shape=[
             shape(slots + (wide,), BF),
             shape((n_ctx, n_fsdp, capacity, wide), BF),
@@ -828,7 +834,8 @@
             shape(slots + (hidden,), BF),
             shape(slots + (hidden,), BF),
             shape(slots + (hidden,), BF),
-            shape(slots + (width,), BF),
+            shape(slots + (width // 2,), BF),
+            shape(slots + (width // 2,), BF),
             shape(dealt.shape, BF),
         ],
         scratch_shapes=[
@@ -856,7 +863,7 @@
             dma((n_ctx,)),
             dma((n_ctx,)),
             dma((n_ctx,)),
-            dma((4,)),
+            dma((5,)),
         ],
         compiler_params=pltpu.CompilerParams(
             collective_id=2, has_side_effects=True, vmem_limit_bytes=60 * 2**20
@@ -987,7 +994,8 @@
     x_ref,
     resid_grad_ref,
     resid_ref,
-    moe_ref,
+    moe_low_ref,
+    moe_high_ref,
     gain_ref,
     query_ref,
     key_ref,
@@ -1016,7 +1024,9 @@
     input_grad_ref[...] = (
         resid_grad_ref[...] + r * n - x * (r * r * r) * jnp.mean(n * x, axis=-1, keepdims=True)
     ).astype(BF)
-    output_ref[...] = (resid_ref[...] + moe_ref[...].astype(F32)).astype(BF)
+    half = resid_ref.shape[1] // 2
+    output_ref[:, :half] = (resid_ref[:, :half] + moe_low_ref[...].astype(F32)).astype(BF)
+    output_ref[:, half:] = (resid_ref[:, half:] + moe_high_ref[...].astype(F32)).astype(BF)
 
     @pl.when(pl.program_id(0) == n_ctx - 1)
     def _():
@@ -1028,7 +1038,7 @@
 
 
 def run_finish(
-    n_ctx, experts, shared, rest, out_grad, d_hidden, x, resid_grad, resid, moe, gain
+    n_ctx, experts, shared, rest, out_grad, d_hidden, x, resid_grad, resid, moe_low, moe_high, gain
 ):
     _, rows, wide = shared.shape
     span, width = x.shape
@@ -1046,7 +1056,8 @@
             whole(rest.shape),
             pl.BlockSpec((1, piece, width), lambda i: (i, 0, 0)),
         ]
-        + [by_rows(tokens, width)] * 5
+        + [by_rows(tokens, width)] * 4
+        + [by_rows(tokens, width // 2)] * 2
         + [whole((1, width))],
         out_specs=[
             by_rows(part, q_columns),
@@ -1069,7 +1080,7 @@
             shape((8, rows), F32),
         ],
         compiler_params=pltpu.CompilerParams(vmem_limit_bytes=48 * 2**20),
-    )(shared, rest, out_grad, d_hidden, x, resid_grad, resid, moe, gain)
+    )(shared, rest, out_grad, d_hidden, x, resid_grad, resid, moe_low, moe_high, gain)
 
 
 def attention_exchange(
@@ -1414,7 +1425,7 @@
 
     def gather_slots(back):
         return jnp.einsum("gjkt,jgkd->gtd", select, back, preferred_element_type=F32).reshape(
-            length, width
+            length, -1
         )
 
     x_all = inputs_all.astype(F32)
@@ -1476,7 +1487,7 @@
             ],
             axis=1,
         )
-        rows, _, parts, inner_low, dg, du, y, dealt = run_expert_exchange(
+        rows, _, parts, inner_low, dg, du, y_low, y_high, dealt = run_expert_exchange(
             n_ctx,
             n_fsdp,
             payload,
@@ -1490,7 +1501,6 @@
         )
         rows = rows.reshape(slots, width + AUX)[:, :width]
         inner_low, dg, du = (array.reshape(slots, -1) for array in (inner_low, dg, du))
-        y = y.reshape(slots, width)
         parts = jnp.sum(parts.astype(F32), axis=0)
         d_gates = parts[:, width : width + experts] + parts[:, width + experts : width + 2 * experts]
         d_logits = gates * (d_gates - jnp.sum(gates * d_gates, axis=-1, keepdims=True))
@@ -1521,6 +1531,8 @@
         du = (d_inner * g * s).astype(BF)
         d_rows = (nt(dg, expert_gate[0]) + nt(du, expert_up[0])).astype(BF)
         y = (nn(inner.astype(BF), expert_down[0]) * slot_gates).astype(BF)
+        y = y.reshape(n_fsdp, n_ctx, capacity, width)
+        y_low, y_high = y[..., : width // 2], y[..., width // 2 :]
         inner_low = (inner * slot_gates).astype(BF)
         d_gates = jnp.einsum(
             "gjkt,jgk->gjt", select.astype(F32), route(slot_dgates), precision=lax.Precision.HIGHEST
@@ -1542,16 +1554,17 @@
     d_resid = grad + r_ffn * n - resid * r_ffn**3 * jnp.mean(n * resid, axis=-1, keepdims=True)
     ffn_gain_grad = jnp.sum(d_normed * resid * r_ffn, axis=0)
     d_attn = gather_ctx(d_resid.astype(BF))
-    y_back = route(y.reshape(n_fsdp, n_ctx, capacity, width))
-    y_back, gate_grad, up_grad, down_grad = lax.optimization_barrier(
-        (y_back, gate_grad, up_grad, down_grad)
-    )
-    y_all = gather_slots(y_back).astype(BF)
-    d_attn, y_all = lax.optimization_barrier((d_attn, y_all))
-
+    y_low, y_high = route(y_low), route(y_high)
+    y_low, d_attn = lax.optimization_barrier((gather_slots(y_low).astype(BF), d_attn))
+    moe_low = scatter_ctx(y_low)
     d_mixed = nt(d_attn, out_here).astype(BF)
-    moe = scatter_ctx(y_all)
     out_grad = jnp.einsum("ntk,td->nkd", dealt, d_attn, preferred_element_type=F32).astype(BF)
+    y_high, d_mixed, out_grad, gate_grad, up_grad, down_grad = lax.optimization_barrier(
+        (y_high, d_mixed, out_grad, gate_grad, up_grad, down_grad)
+    )
+    y_high = gather_slots(y_high).astype(BF)
+    y_high, d_mixed, moe_low = lax.optimization_barrier((y_high, d_mixed, moe_low))
+    moe_high = scatter_ctx(y_high)
 
     dq, dkv, dgains = run_attention_back(
         qkv, d_mixed, totals, heads, cosine, sine, gains, own_blocks, key_blocks
@@ -1576,8 +1589,8 @@
         axis=1,
     )
     shared_grad = tn(hidden, d_qkv).astype(BF)
-    d_hidden, moe, shared_grad, out_grad = lax.optimization_barrier(
-        (d_hidden.astype(BF), moe, shared_grad, out_grad)
+    d_hidden, moe_high, shared_grad, out_grad = lax.optimization_barrier(
+        (d_hidden.astype(BF), moe_high, shared_grad, out_grad)
     )
     d_hidden = scatter_ctx(d_hidden)
     shared_grad, rest, out_grad = run_last_reduce(
@@ -1594,7 +1607,8 @@
             inputs[0],
             d_resid,
             resid,
-            moe,
+            moe_low,
+            moe_high,
             gain_attn,
         )
     )

time: 934 us -> 923 us (0.988)
  waiting for transfers between devices: 77.9 us -> 59 us
    all_to_all x1 -> x2, waiting for transfers between devices: 71.8 us -> 58.2 us  [route(): return lax.all_to_all(rows, 'fsdp', split_axis=0, concat_axis=0, tiled=True)]
  transfers between devices with their start and end apart: 5 -> 7, of which waited for: 2 -> 2; matrix products, arithmetic and copies ran while one was open for 13% -> 14% of each run, Pallas kernels for 30% -> 29%
where the time goes in v6:
time: 923 us; the launch traced here: 917 us
  Pallas kernels  677 us (73%)
  matrix products  95.1 us (10%)
  waiting for transfers between devices  59 us (6%)
  local copies, waits for them, and re-layouts  36.7 us (4%)
  other arithmetic  20.8 us (2%)
  between operations  14.6 us (2%)
  starting transfers between devices  12.9 us (1%)
    pallas_call x1, Pallas kernels, run_expert_exchange(): pl.pallas_call(functools.partial(expert_exchange, n_ctx, n_fsdp), in_spec...  263 us
    pallas_call x1, Pallas kernels, run_last_reduce(): pl.pallas_call(functools.partial(last_reduce, n_ctx, n_fsdp), in_specs=[a...  149 us
    pallas_call x1, Pallas kernels, run_attention_exchange(): pl.pallas_call(functools.partial(attention_exchange, n_ctx, n_fsdp, heads...  137 us
    pallas_call x1, Pallas kernels, run_first_gather(): pl.pallas_call(functools.partial(first_gather, n_ctx, n_fsdp), in_specs=[...  83.2 us
    all_to_all x2, waiting for transfers between devices, route(): return lax.all_to_all(rows, 'fsdp', split_axis=0, concat_axis=0, tiled=True)  58.2 us
    dot_general x5, matrix products, tn(): lax.dot_general(a, b, (((0,), (0,)), ((), ())), preferred_element_type=F32)  51.9 us
    pallas_call x1, Pallas kernels, run_attention_back(): pl.pallas_call(functools.partial(attention_backward, heads), grid=(heads,...  37.3 us
  transfers between devices with their start and end apart: 7, of which 2 were waited for; matrix products, arithmetic and copies ran while one was open for 14% of the time, Pallas kernels for 29%

profile of v6, /device:TPU:0, one launch (start us, length us, event | category | flops | bytes accessed | tf_op | source)
XLA Modules:
  0.0 916.5 jit_solution(11433803467018978982)
XLA Ops:
  11.1 0.8 copy.69
  12.0 0.9 constant_dynamic-slice_fusion
  13.0 1.1 concatenate.20.packed_ref
  14.7 83.2 %shard_map.290 = (bf16[4,256,2048]{2,1,0:T(8,128)(2,1)}, s32[4,16,256]{2,1,0:T(8,128)}, bf16[8,256,1408]{2,1,0:T(8,128)(2,1)}) custom-call(bf16[256,2048]{1,0:T(8,128)(2,1)} %bitcast.98, s32[16,256]{1,0:T(8,128)} %add_add_fusion.table_ref, bf16[256,1408]{1,0:T(8,128)(2,1)} %concatenate.20.packed_ref), custom_call_target="tpu_custom_call" | custom-call | bytes 209715200 | tf_op jit(solution)/shard_map/pallas_call | solution.py:463
  99.4 1.1 slice.86
  100.7 3.1 fusion.4
  104.6 1.7 eq.53
  106.3 2.1 copy.75
  108.6 1.3 compare_convert_fusion
  109.9 2.5 copy.77.sel_ref
  112.4 1.0 copy.76.key_ref
  114.3 1.3 fusion.62.selt_ref
  115.6 3.9 fusion.6
  119.5 2.0 copy-done.19
  121.5 7.3 fusion.13.q_ref.k_ref.v_ref
  129.4 136.6 %shard_map.291 = (f32[8,8,1024]{2,1,0:T(8,128)}, bf16[4,1024,256]{2,1,0:T(8,128)(2,1)}, f32[256,2048]{1,0:T(8,128)}, bf16[8,4,80,2048]{3,2,1,0:T(8,128)(2,1)}) custom-call(f32[1024,1280]{1,0:T(8,128)} %fusion.13.q_ref.k_ref.v_ref, f32[1024,1280]{1,0:T(8,128)} %fusion.13.q_ref.k_ref.v_ref, f32[1024,1280]{1,0:T(8,128)} %fusion.13.q_ref.k_ref.v_ref, ...), custom_call_target="tpu_custom_call" | custom-call | flops 4294967296 | bytes 419430400 | tf_op jit(solution)/shard_map/pallas_call | solution.py:1261
  266.0 1.9 multiply_reduce_fusion.2
  268.0 1.4 multiply_convert_fusion
  269.4 1.7 fusion.46
  271.5 3.0 concatenate.22.x_ref
  274.6 263.4 %shard_map.292 = (bf16[8,4,80,2176]{3,2,1,0:T(8,128)(2,1)}, bf16[4,8,80,2176]{3,2,1,0:T(8,128)(2,1)}, bf16[4,256,2176]{2,1,0:T(8,128)(2,1)}, bf16[8,4,80,768]{3,...) custom-call(bf16[256,2176]{1,0:T(8,128)(2,1)} %concatenate.22.x_ref,, ...), custom_call_target="tpu_custom_call" | custom-call | flops 48318382080 | bytes 629145600 | tf_op jit(solution)/shard_map/pallas_call | solution.py:826
  538.0 3.1 convert_reduce_fusion
  541.6 0.8 multiply_reduce_fusion
  542.5 2.3 fusion.44
  544.8 8.1 all-to-all-start.1
  552.9 14.3 %fusion = f32[2048,768]{1,0:T(8,128)} fusion(bf16[2560,768]{1,0:T(8,128)(2,1)} %bitcast.146, bf16[2560,2176]{1,0:T(8,128)(2,1)} %bitcast.140), kind=kOutput, calls=%fused_computation | convolution fusion | flops 8053063680 | bytes 20709376 | tf_op jit(solution)/shard_map/dot_general | solution.py:34
  567.2 46.7 %all-to-all-done.1 = bf16[8,4,80,1024]{3,2,1,0:T(8,128)(2,1)} async-done(((bf16[8,4,80,1024]{3,2,1,0:T(8,128)(2,1)}), bf16[8,4,80,1024]{3,2,1,0:T(8,128)(2,1)}, u32[]{:S(2)}, u32[]{:S(2)}) %all-to-all-start.1) | async-done | bytes 5242912 | tf_op jit(solution)/shard_map/all_to_all | solution.py:1358
  613.9 4.6 all-to-all-start
  618.6 14.0 %convolution_bitcast_fusion = f32[768,2048]{1,0:T(8,128)} fusion(bf16[8,4,80,768]{3,2,1,0:T(8,128)(2,1)} %get-tuple-element.72, bf16[8,4,80,2048]{3,2,1,0:T(8,128)(2,1)} %get-tuple-element.62.grad_ref), kind=kOutput, calls=%fused_computation.28 | convolution fusion | flops 8053063680 | bytes 20709376 | tf_op jit(solution)/shard_map/dot_general | solution.py:34
  632.5 5.7 bitcast_convert_fusion.1
  638.3 14.5 %fusion.2 = f32[2048,768]{1,0:T(8,128)} fusion(bf16[2560,768]{1,0:T(8,128)(2,1)} %bitcast.145, bf16[2560,2176]{1,0:T(8,128)(2,1)} %bitcast.141), kind=kOutput, calls=%fused_computation.2 | convolution fusion | flops 8053063680 | bytes 20709376 | tf_op jit(solution)/shard_map/dot_general | solution.py:34
  652.8 8.3 fusion.24.grad_ref
  661.2 6.1 fusion.21
  667.3 11.6 %all-to-all-done = bf16[8,4,80,1024]{3,2,1,0:T(8,128)(2,1)} async-done(((bf16[8,4,80,1024]{3,2,1,0:T(8,128)(2,1)}), bf16[8,4,80,1024]{3,2,1,0:T(8,128)(2,1)}, u32[]{:S(2)}, u32[]{:S(2)}) %all-to-all-start) | async-done | bytes 5242912 | tf_op jit(solution)/shard_map/all_to_all | solution.py:1358
  678.9 5.7 bitcast_convert_fusion
  684.7 37.3 %shard_map.293 = (bf16[1024,1024]{1,0:T(8,128)(2,1)S(1)}, bf16[1024,256]{1,0:T(8,128)(2,1)S(1)}, f32[8,128]{1,0:T(8,128)S(1)}) custom-call(f32[1024,1280]{1,0:T(8,128)} %fusion.13.q_ref.k_ref.v_ref, f32[1024,1280]{1,0:T(8,128)} %fusion.13.q_ref.k_ref.v_ref, f32[1024,1280]{1,0:T(8,128)} %fusion.13.q_ref.k_ref.v_ref, bf16[1024,1024]{1,0:T(8,128)(2,1)} %fusion.24.grad_ref, ...), custom_call_target="tpu_custom_call" | custom-call | flops 10737418240 | bytes 10485760 | tf_op jit(solution)/shard_map/pallas_call | solution.py:222
  722.3 2.0 copy-done.20
  724.2 7.5 convolution_convert_fusion
  731.8 7.3 fusion.8
  739.1 1.5 convolution_convert_fusion.1
  742.6 2.5 concatenate.24
  745.1 148.7 %shard_map.294 = (bf16[4,256,1280]{2,1,0:T(8,128)(2,1)}, bf16[4,256,128]{2,1,0:T(8,128)(2,1)}, bf16[4,128,2048]{2,1,0:T(8,128)(2,1)}) custom-call(bf16[4,2,256,1280]{3,2,1,0:T(8,128)(2,1)} %bitcast.102, bf16[4,2,256,128]{3,2,1,0:T(8,128)(2,1)} %bitcast.105, bf16[4,2,128,2048]{3,2,1,0:T(8,128)(2,1)} %bitcast.103), custom_call_target="tpu_custom_call" | custom-call | bytes 419430400 | tf_op jit(solution)/shard_map/pallas_call | solution.py:973
  893.9 1.7 copy-done.5
  895.6 1.2 copy-done.6
  896.9 1.0 copy-done.9
  897.9 1.0 copy-done.10
  899.0 0.9 copy-done.11
  899.9 8.1 shard_map.295
  (137 shorter events, 13.7 us)
Async XLA Ops:
  7.2 5.7 copy-start
  7.2 6.8 copy-start.22
  7.2 6.8 copy-start.26
  7.2 121.6 %all-gather.3.cloned.1.call-start = ((), (), s32[]{:S(2)}) async-start(), calls=%async_computation.5 | async-start | bytes 18874368 | tf_op jit(solution)/shard_map/all_gather | solution.py:1384
  8.0 630.3 %all-gather.5.cloned.1.call-start = ((), (), s32[]{:S(2)}) async-start(), calls=%async_computation.6 | async-start | bytes 5242880 | tf_op jit(solution)/shard_map/all_gather | solution.py:1352
  103.8 11.8 %copy-start.24 = (f32[1,2,4,128]{3,1,2,0:T(2,128)}, f32[1,2,4,128]{3,1,2,0:T(2,128)S(1)}, u32[]{:S(2)}) copy-start(f32[1,2,4,128]{3,1,2,0:T(2,128)S(1)} %copy.100) | copy-start | bytes 12292
  103.9 11.7 %copy-start.13 = (f32[1,2048]{1,0:T(1,128)}, f32[1,2048]{1,0:T(1,128)S(1)}, u32[]{:S(2)}) copy-start(f32[1,2048]{1,0:T(1,128)S(1)} %get-tuple-element.157.gain_ref) | copy-start | bytes 24580
  108.5 3.9 copy-start.23
  114.3 7.2 slice-start
  115.6 5.9 slice-start.1
  119.5 2.0 copy-start.19
  129.4 136.6 %copy-start.2 = (bf16[1,256,2048]{2,1,0:T(8,128)(2,1)S(1)}, bf16[1,256,2048]{2,1,0:T(8,128)(2,1)}, u32[]{:S(2)}) copy-start(bf16[1,256,2048]{2,1,0:T(8,128)(2,1)} %param.19) | copy-start | bytes 3145732
  268.0 274.5 %copy-start.17 = (f32[256,2048]{1,0:T(8,128)}, f32[256,2048]{1,0:T(8,128)S(1)}, u32[]{:S(2)}) copy-start(f32[256,2048]{1,0:T(8,128)S(1)} %get-tuple-element.153.resid_ref) | copy-start | bytes 6291460
  541.2 1.3 copy-start.21
  544.8 69.1 %all-to-all-start.1 = ((bf16[8,4,80,1024]{3,2,1,0:T(8,128)(2,1)}), bf16[8,4,80,1024]{3,2,1,0:T(8,128)(2,1)}, u32[]{:S(2)}, u32[]{:S(2)}) async-start(bf16[8,4,80,1024]{3,2,1,0:T(8,128)(2,1)} %get-tuple-element.65), calls=%async_computation.1 | async-start | bytes 10485760 | tf_op jit(solution)/shard_map/all_to_all | solution.py:1358
  613.9 65.0 %all-to-all-start = ((bf16[8,4,80,1024]{3,2,1,0:T(8,128)(2,1)}), bf16[8,4,80,1024]{3,2,1,0:T(8,128)(2,1)}, u32[]{:S(2)}, u32[]{:S(2)}) async-start(bf16[8,4,80,1024]{3,2,1,0:T(8,128)(2,1)} %get-tuple-element.64), calls=%async_computation | async-start | bytes 10485760 | tf_op jit(solution)/shard_map/all_to_all | solution.py:1358
  618.5 66.0 %reduce-scatter.4.cloned.1.call-start = ((), (), s32[]{:S(2)}) async-start(), calls=%async_computation.7 | async-start | bytes 2621440 | tf_op jit(solution)/shard_map/reduce_scatter | solution.py:1355
  638.2 100.9 %reduce-scatter.6.cloned.1.call-start = ((), (), s32[]{:S(2)}) async-start(), calls=%async_computation.8 | async-start | bytes 2621440 | tf_op jit(solution)/shard_map/reduce_scatter | solution.py:1355
  638.3 14.5 %copy-start.27 = (bf16[1024,2048]{1,0:T(8,128)(2,1)S(1)}, bf16[1024,2048]{1,0:T(8,128)(2,1)}, u32[]{:S(2)}) copy-start(bf16[1024,2048]{1,0:T(8,128)(2,1)} %all-gather.5.cloned.1.call-done) | copy-start | bytes 12582916
  652.8 8.3 copy-start.28
  667.3 17.3 %copy-start.4 = (s32[1024,1]{1,0:T(8,128)S(1)}, s32[1024,1]{1,0:T(8,128)}, u32[]{:S(2)}) copy-start(s32[1024,1]{1,0:T(8,128)} %copy.76.key_ref) | copy-start | bytes 12292
  667.3 17.3 %copy-start.7 = (f32[1024,128]{1,0:T(8,128)S(1)}, f32[1024,128]{1,0:T(8,128)}, u32[]{:S(2)}) copy-start(f32[1024,128]{1,0:T(8,128)} %constant.61.clone.cos_ref) | copy-start | bytes 1572868
  667.3 17.3 %copy-start.8 = (f32[1024,128]{1,0:T(8,128)S(1)}, f32[1024,128]{1,0:T(8,128)}, u32[]{:S(2)}) copy-start(f32[1024,128]{1,0:T(8,128)} %constant.62.clone.sin_ref) | copy-start | bytes 1572868
  667.3 17.4 %copy-start.12 = (s32[8,1024]{1,0:T(8,128)S(1)}, s32[8,1024]{1,0:T(8,128)}, u32[]{:S(2)}) copy-start(s32[8,1024]{1,0:T(8,128)} %broadcast_in_dim.77.own_ref) | copy-start | bytes 98308
  667.3 17.4 %copy-start.15 = (f32[8,128]{1,0:T(8,128)S(1)}, f32[8,128]{1,0:T(8,128)}, u32[]{:S(2)}) copy-start(f32[8,128]{1,0:T(8,128)} %maximum_convert_fusion.gains_ref) | copy-start | bytes 12292
  667.3 17.4 %copy-start.16 = (f32[8,8,1024]{2,1,0:T(8,128)S(1)}, f32[8,8,1024]{2,1,0:T(8,128)}, u32[]{:S(2)}) copy-start(f32[8,8,1024]{2,1,0:T(8,128)} %get-tuple-element.77.total_ref) | copy-start | bytes 786436
  684.6 209.3 %reduce-scatter.8.cloned.1.call-start = ((), (), s32[]{:S(2)}) async-start(), calls=%async_computation.9 | async-start | bytes 5242880 | tf_op jit(solution)/shard_map/reduce_scatter | solution.py:1355
  722.0 2.2 copy-start.20
  722.0 9.7 %slice-start.2 = ((s8[5767168]{0:T(1024)(128)(4,1)}), s8[4194304]{0:T(1024)(128)(4,1)S(1)}, s32[]{:S(2)}) async-start(s8[5767168]{0:T(1024)(128)(4,1)} %bitcast.120), calls=%async_computation.12 | async-start | bytes 8388608
  724.2 7.5 copy-start.18
  724.2 7.5 slice-start.3
  724.2 7.5 copy-start.25
  745.1 148.8 %copy-start.3 = (bf16[1,256,2048]{2,1,0:T(8,128)(2,1)S(1)}, bf16[1,256,2048]{2,1,0:T(8,128)(2,1)}, u32[]{:S(2)}) copy-start(bf16[1,256,2048]{2,1,0:T(8,128)(2,1)} %param.19) | copy-start | bytes 3145732
  745.1 148.8 %copy-start.14 = (f32[1,2048]{1,0:T(1,128)S(1)}, f32[1,2048]{1,0:T(1,128)}, u32[]{:S(2)}) copy-start(f32[1,2048]{1,0:T(1,128)} %copy-done.13) | copy-start | bytes 24580
  893.9 15.9 %copy-start.1 = (bf16[256,4096]{1,0:T(8,128)(2,1)S(1)}, bf16[256,4096]{1,0:T(8,128)(2,1)}, u32[]{:S(2)}) copy-start(bf16[256,4096]{1,0:T(8,128)(2,1)} %param.24) | copy-start | bytes 6291460
  893.9 1.7 copy-start.5
  895.6 1.2 copy-start.6
  896.9 1.0 copy-start.9
  897.9 1.0 copy-start.10
  899.0 0.9 copy-start.11
Sparse Core Ops, SparseCore 0:
  9.9 118.5 all-gather.2
  544.9 85.5 all-gather.4
  638.4 44.5 reduce-scatter.3
  685.2 43.1 reduce-scatter.5
  739.2 101.1 reduce-scatter.7

commit v7 on v6

--- a/solution.py
+++ b/solution.py
@@ -1559,8 +1559,10 @@
     moe_low = scatter_ctx(y_low)
     d_mixed = nt(d_attn, out_here).astype(BF)
     out_grad = jnp.einsum("ntk,td->nkd", dealt, d_attn, preferred_element_type=F32).astype(BF)
-    y_high, d_mixed, out_grad, gate_grad, up_grad, down_grad = lax.optimization_barrier(
-        (y_high, d_mixed, out_grad, gate_grad, up_grad, down_grad)
+    y_high, d_mixed, out_grad, gate_grad, up_grad, down_grad, router_grad = (
+        lax.optimization_barrier(
+            (y_high, d_mixed, out_grad, gate_grad, up_grad, down_grad, router_grad)
+        )
     )
     y_high = gather_slots(y_high).astype(BF)
     y_high, d_mixed, moe_low = lax.optimization_barrier((y_high, d_mixed, moe_low))
@@ -1589,9 +1591,7 @@
         axis=1,
     )
     shared_grad = tn(hidden, d_qkv).astype(BF)
-    d_hidden, moe_high, shared_grad, out_grad = lax.optimization_barrier(
-        (d_hidden.astype(BF), moe_high, shared_grad, out_grad)
-    )
+    d_hidden, moe_high = lax.optimization_barrier((d_hidden.astype(BF), moe_high))
     d_hidden = scatter_ctx(d_hidden)
     shared_grad, rest, out_grad = run_last_reduce(
         n_ctx, n_fsdp, [shared_grad, extra_grad, out_grad.reshape(n_fsdp * piece, width)]

time: 923 us -> 919 us (level)
  transfers between devices with their start and end apart: 7 -> 7, of which waited for: 2 -> 3; matrix products, arithmetic and copies ran while one was open for 14% -> 14% of each run, Pallas kernels for 29% -> 29%
where the time goes in v7:
time: 919 us; the launch traced here: 912 us
  Pallas kernels  668 us (73%)
  matrix products  99.4 us (11%)
  waiting for transfers between devices  58.3 us (6%)
  local copies, waits for them, and re-layouts  37.5 us (4%)
  other arithmetic  20.8 us (2%)
  between operations  14.6 us (2%)
  starting transfers between devices  13.5 us (1%)
    pallas_call x1, Pallas kernels, run_expert_exchange(): pl.pallas_call(functools.partial(expert_exchange, n_ctx, n_fsdp), in_spec...  263 us
    pallas_call x1, Pallas kernels, run_last_reduce(): pl.pallas_call(functools.partial(last_reduce, n_ctx, n_fsdp), in_specs=[a...  140 us
    pallas_call x1, Pallas kernels, run_attention_exchange(): pl.pallas_call(functools.partial(attention_exchange, n_ctx, n_fsdp, heads...  136 us
    pallas_call x1, Pallas kernels, run_first_gather(): pl.pallas_call(functools.partial(first_gather, n_ctx, n_fsdp), in_specs=[...  83.2 us
    dot_general x5, matrix products, tn(): lax.dot_general(a, b, (((0,), (0,)), ((), ())), preferred_element_type=F32)  53.6 us
    all_to_all x2, waiting for transfers between devices, route(): return lax.all_to_all(rows, 'fsdp', split_axis=0, concat_axis=0, tiled=True)  53.1 us
    pallas_call x1, Pallas kernels, run_attention_back(): pl.pallas_call(functools.partial(attention_backward, heads), grid=(heads,...  36.9 us
    dot_general x3, matrix products, nt(): lax.dot_general(a, b, (((1,), (1,)), ((), ())), preferred_element_type=F32)  19.8 us
  transfers between devices with their start and end apart: 7, of which 3 were waited for; matrix products, arithmetic and copies ran while one was open for 14% of the time, Pallas kernels for 29%

profile of v7, /device:TPU:0, one launch (start us, length us, event | category | flops | bytes accessed | tf_op | source)
XLA Modules:
  0.0 912.4 jit_solution(17603499239521695184)
XLA Ops:
  12.0 0.9 constant_dynamic-slice_fusion
  13.0 1.1 concatenate.20.packed_ref
  14.7 83.2 %shard_map.290 = (bf16[4,256,2048]{2,1,0:T(8,128)(2,1)}, s32[4,16,256]{2,1,0:T(8,128)}, bf16[8,256,1408]{2,1,0:T(8,128)(2,1)}) custom-call(bf16[256,2048]{1,0:T(8,128)(2,1)} %bitcast.98, s32[16,256]{1,0:T(8,128)} %add_add_fusion.table_ref, bf16[256,1408]{1,0:T(8,128)(2,1)} %concatenate.20.packed_ref), custom_call_target="tpu_custom_call" | custom-call | bytes 209715200 | tf_op jit(solution)/shard_map/pallas_call | solution.py:463
  99.4 1.1 slice.86
  100.7 3.1 fusion.4
  104.6 1.7 eq.53
  106.3 2.1 copy.75
  108.6 1.3 compare_convert_fusion
  109.9 2.5 copy.77.sel_ref
  112.4 1.0 copy.76.key_ref
  114.3 1.3 fusion.64.selt_ref
  115.6 3.9 fusion.6
  119.5 2.0 copy-done.19
  121.5 7.3 fusion.13.q_ref.k_ref.v_ref
  129.4 136.5 %shard_map.291 = (f32[8,8,1024]{2,1,0:T(8,128)}, bf16[4,1024,256]{2,1,0:T(8,128)(2,1)}, f32[256,2048]{1,0:T(8,128)}, bf16[8,4,80,2048]{3,2,1,0:T(8,128)(2,1)}) custom-call(f32[1024,1280]{1,0:T(8,128)} %fusion.13.q_ref.k_ref.v_ref, f32[1024,1280]{1,0:T(8,128)} %fusion.13.q_ref.k_ref.v_ref, f32[1024,1280]{1,0:T(8,128)} %fusion.13.q_ref.k_ref.v_ref, ...), custom_call_target="tpu_custom_call" | custom-call | flops 4294967296 | bytes 419430400 | tf_op jit(solution)/shard_map/pallas_call | solution.py:1261
  265.9 1.9 multiply_reduce_fusion.2
  267.9 1.4 multiply_convert_fusion
  269.3 1.7 fusion.47
  271.4 3.0 concatenate.22.x_ref
  274.5 263.4 %shard_map.292 = (bf16[8,4,80,2176]{3,2,1,0:T(8,128)(2,1)}, bf16[4,8,80,2176]{3,2,1,0:T(8,128)(2,1)}, bf16[4,256,2176]{2,1,0:T(8,128)(2,1)}, bf16[8,4,80,768]{3,...) custom-call(bf16[256,2176]{1,0:T(8,128)(2,1)} %concatenate.22.x_ref,, ...), custom_call_target="tpu_custom_call" | custom-call | flops 48318382080 | bytes 629145600 | tf_op jit(solution)/shard_map/pallas_call | solution.py:826
  537.9 3.1 convert_reduce_fusion
  542.4 2.3 fusion.44
  544.7 8.1 all-to-all-start.1
  552.8 14.3 %convolution_bitcast_fusion = f32[768,2048]{1,0:T(8,128)} fusion(bf16[8,4,80,768]{3,2,1,0:T(8,128)(2,1)} %get-tuple-element.71, bf16[8,4,80,2048]{3,2,1,0:T(8,128)(2,1)} %get-tuple-element.61.grad_ref), kind=kOutput, calls=%fused_computation.28 | convolution fusion | flops 8053063680 | bytes 20709376 | tf_op jit(solution)/shard_map/dot_general | solution.py:34
  567.1 13.1 %fusion = f32[2048,768]{1,0:T(8,128)} fusion(bf16[2560,768]{1,0:T(8,128)(2,1)S(1)} %bitcast.144, bf16[2560,2176]{1,0:T(8,128)(2,1)} %bitcast.138), kind=kOutput, calls=%fused_computation | convolution fusion | flops 8053063680 | bytes 20709376 | tf_op jit(solution)/shard_map/dot_general | solution.py:34
  580.2 33.6 %all-to-all-done.1 = bf16[8,4,80,1024]{3,2,1,0:T(8,128)(2,1)} async-done(((bf16[8,4,80,1024]{3,2,1,0:T(8,128)(2,1)}), bf16[8,4,80,1024]{3,2,1,0:T(8,128)(2,1)}, u32[]{:S(2)}, u32[]{:S(2)}) %all-to-all-start.1) | async-done | bytes 5242912 | tf_op jit(solution)/shard_map/all_to_all | solution.py:1358
  613.8 4.6 all-to-all-start
  618.7 1.5 fusion.48
  620.2 5.7 bitcast_convert_fusion.1
  625.9 4.5 all-gather.5.cloned.1.call-done
  630.5 14.3 %fusion.2 = f32[2048,768]{1,0:T(8,128)} fusion(bf16[2560,768]{1,0:T(8,128)(2,1)} %bitcast.143, bf16[2560,2176]{1,0:T(8,128)(2,1)} %bitcast.139), kind=kOutput, calls=%fused_computation.2 | convolution fusion | flops 8053063680 | bytes 20709376 | tf_op jit(solution)/shard_map/dot_general | solution.py:34
  644.8 8.3 fusion.24.grad_ref
  653.1 6.2 fusion.21
  659.3 19.5 %all-to-all-done = bf16[8,4,80,1024]{3,2,1,0:T(8,128)(2,1)} async-done(((bf16[8,4,80,1024]{3,2,1,0:T(8,128)(2,1)}), bf16[8,4,80,1024]{3,2,1,0:T(8,128)(2,1)}, u32[]{:S(2)}, u32[]{:S(2)}) %all-to-all-start) | async-done | bytes 5242912 | tf_op jit(solution)/shard_map/all_to_all | solution.py:1358
  678.8 5.6 bitcast_convert_fusion
  685.0 36.9 %shard_map.293 = (bf16[1024,1024]{1,0:T(8,128)(2,1)S(1)}, bf16[1024,256]{1,0:T(8,128)(2,1)S(1)}, f32[8,128]{1,0:T(8,128)S(1)}) custom-call(f32[1024,1280]{1,0:T(8,128)} %fusion.13.q_ref.k_ref.v_ref, f32[1024,1280]{1,0:T(8,128)} %fusion.13.q_ref.k_ref.v_ref, f32[1024,1280]{1,0:T(8,128)} %fusion.13.q_ref.k_ref.v_ref, bf16[1024,1024]{1,0:T(8,128)(2,1)} %fusion.24.grad_ref, ...), custom_call_target="tpu_custom_call" | custom-call | flops 10737418240 | bytes 10485760 | tf_op jit(solution)/shard_map/pallas_call | solution.py:222
  722.1 1.5 copy-done.21
  723.7 1.4 copy-done.18
  725.1 9.8 %fusion.45 = (bf16[1024,2048]{1,0:T(8,128)(2,1)}, bf16[2048]{0:T(1024)(128)(2,1)S(1)}) fusion(f32[1024]{0:T(1024)S(1)} %bitcast.128, bf16[4,256,2048]{2,1,0:T(8,128)(2,1)S(1)} %copy-done.18, bf16[1024,1280]{1,0:T(8,128)(2,1)S(1)} %constant_dynamic-update-slice_fusion, bf16[2048,1408]{1,0:T(8,128)(2,1)} %bitcast.117), kind=kOutput, calls=%fused_computation.87 | convolution fusion | flops 5379192832 | bytes 16261120 | tf_op jit(solution)/shard_map/dot_general | solution.py:26
  736.9 2.3 concatenate.24
  739.2 10.4 %convolution_convert_fusion = bf16[2048,1280]{1,0:T(8,128)(2,1)} fusion(bf16[1024,2048]{1,0:T(8,128)(2,1)} %copy-done.19, bf16[1024,1280]{1,0:T(8,128)(2,1)} %copy-done.21), kind=kOutput, calls=%fused_computation.13 | convolution fusion | flops 5371330560 | bytes 12058624 | tf_op jit(solution)/shard_map/dot_general | solution.py:34
  749.6 140.1 %shard_map.294 = (bf16[4,256,1280]{2,1,0:T(8,128)(2,1)}, bf16[4,256,128]{2,1,0:T(8,128)(2,1)}, bf16[4,128,2048]{2,1,0:T(8,128)(2,1)}) custom-call(bf16[4,2,256,1280]{3,2,1,0:T(8,128)(2,1)} %bitcast.102, bf16[4,2,256,128]{3,2,1,0:T(8,128)(2,1)} %bitcast.105, bf16[4,2,128,2048]{3,2,1,0:T(8,128)(2,1)} %bitcast.103), custom_call_target="tpu_custom_call" | custom-call | bytes 419430400 | tf_op jit(solution)/shard_map/pallas_call | solution.py:973
  889.8 1.7 copy-done.5
  891.5 1.2 copy-done.6
  892.7 1.0 copy-done.9
  893.8 1.0 copy-done.10
  894.8 0.9 copy-done.11
  895.8 8.1 shard_map.295
  (134 shorter events, 15.9 us)
Async XLA Ops:
  7.2 5.7 copy-start
  7.2 6.8 copy-start.22
  7.2 6.8 copy-start.26
  7.2 121.6 %all-gather.3.cloned.1.call-start = ((), (), s32[]{:S(2)}) async-start(), calls=%async_computation.5 | async-start | bytes 18874368 | tf_op jit(solution)/shard_map/all_gather | solution.py:1384
  8.0 622.5 %all-gather.5.cloned.1.call-start = ((), (), s32[]{:S(2)}) async-start(), calls=%async_computation.6 | async-start | bytes 5242880 | tf_op jit(solution)/shard_map/all_gather | solution.py:1352
  103.8 11.8 %copy-start.24 = (f32[1,2,4,128]{3,1,2,0:T(2,128)}, f32[1,2,4,128]{3,1,2,0:T(2,128)S(1)}, u32[]{:S(2)}) copy-start(f32[1,2,4,128]{3,1,2,0:T(2,128)S(1)} %copy.100) | copy-start | bytes 12292
  103.9 11.7 %copy-start.13 = (f32[1,2048]{1,0:T(1,128)}, f32[1,2048]{1,0:T(1,128)S(1)}, u32[]{:S(2)}) copy-start(f32[1,2048]{1,0:T(1,128)S(1)} %get-tuple-element.155.gain_ref) | copy-start | bytes 24580
  108.5 3.9 copy-start.23
  114.3 7.2 slice-start
  115.6 5.9 slice-start.1
  119.5 2.0 copy-start.19
  129.4 136.5 %copy-start.2 = (bf16[1,256,2048]{2,1,0:T(8,128)(2,1)S(1)}, bf16[1,256,2048]{2,1,0:T(8,128)(2,1)}, u32[]{:S(2)}) copy-start(bf16[1,256,2048]{2,1,0:T(8,128)(2,1)} %param.19) | copy-start | bytes 3145732
  267.9 274.5 %copy-start.17 = (f32[256,2048]{1,0:T(8,128)}, f32[256,2048]{1,0:T(8,128)S(1)}, u32[]{:S(2)}) copy-start(f32[256,2048]{1,0:T(8,128)S(1)} %get-tuple-element.151.resid_ref) | copy-start | bytes 6291460
  541.1 1.3 copy-start.20
  544.7 69.1 %all-to-all-start.1 = ((bf16[8,4,80,1024]{3,2,1,0:T(8,128)(2,1)}), bf16[8,4,80,1024]{3,2,1,0:T(8,128)(2,1)}, u32[]{:S(2)}, u32[]{:S(2)}) async-start(bf16[8,4,80,1024]{3,2,1,0:T(8,128)(2,1)} %get-tuple-element.64), calls=%async_computation.1 | async-start | bytes 10485760 | tf_op jit(solution)/shard_map/all_to_all | solution.py:1358
  552.8 14.3 %copy-start.28 = (bf16[8,4,80,768]{3,2,1,0:T(8,128)(2,1)S(1)}, bf16[8,4,80,768]{3,2,1,0:T(8,128)(2,1)}, u32[]{:S(2)}) copy-start(bf16[8,4,80,768]{3,2,1,0:T(8,128)(2,1)} %get-tuple-element.70) | copy-start | bytes 11796484
  613.8 65.0 %all-to-all-start = ((bf16[8,4,80,1024]{3,2,1,0:T(8,128)(2,1)}), bf16[8,4,80,1024]{3,2,1,0:T(8,128)(2,1)}, u32[]{:S(2)}, u32[]{:S(2)}) async-start(bf16[8,4,80,1024]{3,2,1,0:T(8,128)(2,1)} %get-tuple-element.63), calls=%async_computation | async-start | bytes 10485760 | tf_op jit(solution)/shard_map/all_to_all | solution.py:1358
  618.5 66.0 %reduce-scatter.4.cloned.1.call-start = ((), (), s32[]{:S(2)}) async-start(), calls=%async_computation.7 | async-start | bytes 2621440 | tf_op jit(solution)/shard_map/reduce_scatter | solution.py:1355
  630.4 104.4 %reduce-scatter.6.cloned.1.call-start = ((), (), s32[]{:S(2)}) async-start(), calls=%async_computation.8 | async-start | bytes 2621440 | tf_op jit(solution)/shard_map/reduce_scatter | solution.py:1355
  630.5 14.3 %copy-start.27 = (bf16[1024,2048]{1,0:T(8,128)(2,1)S(1)}, bf16[1024,2048]{1,0:T(8,128)(2,1)}, u32[]{:S(2)}) copy-start(bf16[1024,2048]{1,0:T(8,128)(2,1)} %all-gather.5.cloned.1.call-done) | copy-start | bytes 12582916
  644.8 8.3 copy-start.29
  659.3 25.6 %copy-start.4 = (s32[1024,1]{1,0:T(8,128)S(1)}, s32[1024,1]{1,0:T(8,128)}, u32[]{:S(2)}) copy-start(s32[1024,1]{1,0:T(8,128)} %copy.76.key_ref) | copy-start | bytes 12292
  659.3 25.6 %copy-start.7 = (f32[1024,128]{1,0:T(8,128)S(1)}, f32[1024,128]{1,0:T(8,128)}, u32[]{:S(2)}) copy-start(f32[1024,128]{1,0:T(8,128)} %constant.61.clone.cos_ref) | copy-start | bytes 1572868
  659.3 25.6 %copy-start.8 = (f32[1024,128]{1,0:T(8,128)S(1)}, f32[1024,128]{1,0:T(8,128)}, u32[]{:S(2)}) copy-start(f32[1024,128]{1,0:T(8,128)} %constant.62.clone.sin_ref) | copy-start | bytes 1572868
  659.3 25.6 %copy-start.12 = (s32[8,1024]{1,0:T(8,128)S(1)}, s32[8,1024]{1,0:T(8,128)}, u32[]{:S(2)}) copy-start(s32[8,1024]{1,0:T(8,128)} %broadcast_in_dim.77.own_ref) | copy-start | bytes 98308
  659.3 25.6 %copy-start.15 = (f32[8,128]{1,0:T(8,128)S(1)}, f32[8,128]{1,0:T(8,128)}, u32[]{:S(2)}) copy-start(f32[8,128]{1,0:T(8,128)} %maximum_convert_fusion.gains_ref) | copy-start | bytes 12292
  659.3 25.6 %copy-start.16 = (f32[8,8,1024]{2,1,0:T(8,128)S(1)}, f32[8,8,1024]{2,1,0:T(8,128)}, u32[]{:S(2)}) copy-start(f32[8,8,1024]{2,1,0:T(8,128)} %get-tuple-element.76.total_ref) | copy-start | bytes 786436
  684.5 205.3 %reduce-scatter.8.cloned.1.call-start = ((), (), s32[]{:S(2)}) async-start(), calls=%async_computation.9 | async-start | bytes 5242880 | tf_op jit(solution)/shard_map/reduce_scatter | solution.py:1355
  721.9 3.2 copy-start.18
  721.9 3.2 copy-start.25
  722.1 1.6 copy-start.21
  749.6 140.2 %copy-start.3 = (bf16[1,256,2048]{2,1,0:T(8,128)(2,1)S(1)}, bf16[1,256,2048]{2,1,0:T(8,128)(2,1)}, u32[]{:S(2)}) copy-start(bf16[1,256,2048]{2,1,0:T(8,128)(2,1)} %param.19) | copy-start | bytes 3145732
  749.6 140.2 %copy-start.14 = (f32[1,2048]{1,0:T(1,128)S(1)}, f32[1,2048]{1,0:T(1,128)}, u32[]{:S(2)}) copy-start(f32[1,2048]{1,0:T(1,128)} %copy-done.13) | copy-start | bytes 24580
  889.8 15.9 %copy-start.1 = (bf16[256,4096]{1,0:T(8,128)(2,1)S(1)}, bf16[256,4096]{1,0:T(8,128)(2,1)}, u32[]{:S(2)}) copy-start(bf16[256,4096]{1,0:T(8,128)(2,1)} %param.24) | copy-start | bytes 6291460
  889.8 1.7 copy-start.5
  891.5 1.2 copy-start.6
  892.7 1.0 copy-start.9
  893.8 1.0 copy-start.10
  894.8 0.9 copy-start.11
Sparse Core Ops, SparseCore 0:
  9.9 118.5 all-gather.2
  544.8 85.5 all-gather.4
  632.7 42.3 reduce-scatter.3
  684.6 42.3 reduce-scatter.5
  735.0 92.7 reduce-scatter.7

commit v8 on v7

--- a/solution.py
+++ b/solution.py
@@ -139,7 +139,7 @@
 
     queries = norm_rope(q_ref[...], gains_ref[0:1, :], cosine, sine).astype(BF)
     length = queries.shape[0]
-    chunk = 256
+    chunk = 512
     for start in range(0, length, chunk):
         rows = slice(start, start + chunk)
         q_part = queries[rows]

time: 919 us -> 917 us (level)
  transfers between devices with their start and end apart: 7 -> 7, of which waited for: 3 -> 3; matrix products, arithmetic and copies ran while one was open for 14% -> 14% of each run, Pallas kernels for 29% -> 28%
where the time goes in v8:
time: 917 us; the launch traced here: 910 us
  Pallas kernels  666 us (73%)
  matrix products  99.4 us (11%)
  waiting for transfers between devices  58.3 us (6%)
  local copies, waits for them, and re-layouts  37.5 us (4%)
  other arithmetic  20.8 us (2%)
  between operations  14.6 us (2%)
  starting transfers between devices  13.5 us (1%)
    pallas_call x1, Pallas kernels, run_expert_exchange(): pl.pallas_call(functools.partial(expert_exchange, n_ctx, n_fsdp), in_spec...  263 us
    pallas_call x1, Pallas kernels, run_last_reduce(): pl.pallas_call(functools.partial(last_reduce, n_ctx, n_fsdp), in_specs=[a...  140 us
    pallas_call x1, Pallas kernels, run_attention_exchange(): pl.pallas_call(functools.partial(attention_exchange, n_ctx, n_fsdp, heads...  136 us
    pallas_call x1, Pallas kernels, run_first_gather(): pl.pallas_call(functools.partial(first_gather, n_ctx, n_fsdp), in_specs=[...  83.2 us
    dot_general x5, matrix products, tn(): lax.dot_general(a, b, (((0,), (0,)), ((), ())), preferred_element_type=F32)  53.6 us
    all_to_all x2, waiting for transfers between devices, route(): return lax.all_to_all(rows, 'fsdp', split_axis=0, concat_axis=0, tiled=True)  53.1 us
    pallas_call x1, Pallas kernels, run_attention_back(): pl.pallas_call(functools.partial(attention_backward, heads), grid=(heads,...  34.9 us
    dot_general x3, matrix products, nt(): lax.dot_general(a, b, (((1,), (1,)), ((), ())), preferred_element_type=F32)  19.9 us
  transfers between devices with their start and end apart: 7, of which 3 were waited for; matrix products, arithmetic and copies ran while one was open for 14% of the time, Pallas kernels for 28%

profile of v8, /device:TPU:0, one launch (start us, length us, event | category | flops | bytes accessed | tf_op | source)
XLA Modules:
  0.0 910.5 jit_solution(12965427379148718236)
XLA Ops:
  12.0 0.9 constant_dynamic-slice_fusion
  13.0 1.1 concatenate.20.packed_ref
  14.7 83.2 %shard_map.290 = (bf16[4,256,2048]{2,1,0:T(8,128)(2,1)}, s32[4,16,256]{2,1,0:T(8,128)}, bf16[8,256,1408]{2,1,0:T(8,128)(2,1)}) custom-call(bf16[256,2048]{1,0:T(8,128)(2,1)} %bitcast.98, s32[16,256]{1,0:T(8,128)} %add_add_fusion.table_ref, bf16[256,1408]{1,0:T(8,128)(2,1)} %concatenate.20.packed_ref), custom_call_target="tpu_custom_call" | custom-call | bytes 209715200 | tf_op jit(solution)/shard_map/pallas_call | solution.py:463
  99.4 1.1 slice.86
  100.7 3.1 fusion.4
  104.6 1.7 eq.53
  106.3 2.1 copy.75
  108.6 1.3 compare_convert_fusion
  109.9 2.5 copy.77.sel_ref
  112.4 1.0 copy.76.key_ref
  114.3 1.3 fusion.64.selt_ref
  115.6 3.9 fusion.6
  119.5 2.0 copy-done.19
  121.5 7.3 fusion.13.q_ref.k_ref.v_ref
  129.4 136.5 %shard_map.291 = (f32[8,8,1024]{2,1,0:T(8,128)}, bf16[4,1024,256]{2,1,0:T(8,128)(2,1)}, f32[256,2048]{1,0:T(8,128)}, bf16[8,4,80,2048]{3,2,1,0:T(8,128)(2,1)}) custom-call(f32[1024,1280]{1,0:T(8,128)} %fusion.13.q_ref.k_ref.v_ref, f32[1024,1280]{1,0:T(8,128)} %fusion.13.q_ref.k_ref.v_ref, f32[1024,1280]{1,0:T(8,128)} %fusion.13.q_ref.k_ref.v_ref, ...), custom_call_target="tpu_custom_call" | custom-call | flops 4294967296 | bytes 419430400 | tf_op jit(solution)/shard_map/pallas_call | solution.py:1261
  265.9 1.9 multiply_reduce_fusion.2
  267.9 1.4 multiply_convert_fusion
  269.3 1.7 fusion.47
  271.4 3.0 concatenate.22.x_ref
  274.5 263.4 %shard_map.292 = (bf16[8,4,80,2176]{3,2,1,0:T(8,128)(2,1)}, bf16[4,8,80,2176]{3,2,1,0:T(8,128)(2,1)}, bf16[4,256,2176]{2,1,0:T(8,128)(2,1)}, bf16[8,4,80,768]{3,...) custom-call(bf16[256,2176]{1,0:T(8,128)(2,1)} %concatenate.22.x_ref,, ...), custom_call_target="tpu_custom_call" | custom-call | flops 48318382080 | bytes 629145600 | tf_op jit(solution)/shard_map/pallas_call | solution.py:826
  537.9 3.1 convert_reduce_fusion
  542.4 2.3 fusion.44
  544.7 8.1 all-to-all-start.1
  552.8 14.3 %convolution_bitcast_fusion = f32[768,2048]{1,0:T(8,128)} fusion(bf16[8,4,80,768]{3,2,1,0:T(8,128)(2,1)} %get-tuple-element.71, bf16[8,4,80,2048]{3,2,1,0:T(8,128)(2,1)} %get-tuple-element.61.grad_ref), kind=kOutput, calls=%fused_computation.28 | convolution fusion | flops 8053063680 | bytes 20709376 | tf_op jit(solution)/shard_map/dot_general | solution.py:34
  567.1 13.1 %fusion = f32[2048,768]{1,0:T(8,128)} fusion(bf16[2560,768]{1,0:T(8,128)(2,1)S(1)} %bitcast.144, bf16[2560,2176]{1,0:T(8,128)(2,1)} %bitcast.138), kind=kOutput, calls=%fused_computation | convolution fusion | flops 8053063680 | bytes 20709376 | tf_op jit(solution)/shard_map/dot_general | solution.py:34
  580.2 33.6 %all-to-all-done.1 = bf16[8,4,80,1024]{3,2,1,0:T(8,128)(2,1)} async-done(((bf16[8,4,80,1024]{3,2,1,0:T(8,128)(2,1)}), bf16[8,4,80,1024]{3,2,1,0:T(8,128)(2,1)}, u32[]{:S(2)}, u32[]{:S(2)}) %all-to-all-start.1) | async-done | bytes 5242912 | tf_op jit(solution)/shard_map/all_to_all | solution.py:1358
  613.8 4.6 all-to-all-start
  618.7 1.5 fusion.48
  620.2 5.7 bitcast_convert_fusion.1
  625.9 4.5 all-gather.5.cloned.1.call-done
  630.5 14.3 %fusion.2 = f32[2048,768]{1,0:T(8,128)} fusion(bf16[2560,768]{1,0:T(8,128)(2,1)} %bitcast.143, bf16[2560,2176]{1,0:T(8,128)(2,1)} %bitcast.139), kind=kOutput, calls=%fused_computation.2 | convolution fusion | flops 8053063680 | bytes 20709376 | tf_op jit(solution)/shard_map/dot_general | solution.py:34
  644.8 8.3 fusion.24.grad_ref
  653.1 6.2 fusion.21
  659.3 19.5 %all-to-all-done = bf16[8,4,80,1024]{3,2,1,0:T(8,128)(2,1)} async-done(((bf16[8,4,80,1024]{3,2,1,0:T(8,128)(2,1)}), bf16[8,4,80,1024]{3,2,1,0:T(8,128)(2,1)}, u32[]{:S(2)}, u32[]{:S(2)}) %all-to-all-start) | async-done | bytes 5242912 | tf_op jit(solution)/shard_map/all_to_all | solution.py:1358
  678.8 5.6 bitcast_convert_fusion
  685.0 34.9 %shard_map.293 = (bf16[1024,1024]{1,0:T(8,128)(2,1)S(1)}, bf16[1024,256]{1,0:T(8,128)(2,1)S(1)}, f32[8,128]{1,0:T(8,128)S(1)}) custom-call(f32[1024,1280]{1,0:T(8,128)} %fusion.13.q_ref.k_ref.v_ref, f32[1024,1280]{1,0:T(8,128)} %fusion.13.q_ref.k_ref.v_ref, f32[1024,1280]{1,0:T(8,128)} %fusion.13.q_ref.k_ref.v_ref, bf16[1024,1024]{1,0:T(8,128)(2,1)} %fusion.24.grad_ref, ...), custom_call_target="tpu_custom_call" | custom-call | flops 10737418240 | bytes 10485760 | tf_op jit(solution)/shard_map/pallas_call | solution.py:222
  720.2 1.5 copy-done.21
  721.7 1.3 copy-done.18
  723.0 9.8 %fusion.45 = (bf16[1024,2048]{1,0:T(8,128)(2,1)}, bf16[2048]{0:T(1024)(128)(2,1)S(1)}) fusion(f32[1024]{0:T(1024)S(1)} %bitcast.128, bf16[4,256,2048]{2,1,0:T(8,128)(2,1)S(1)} %copy-done.18, bf16[1024,1280]{1,0:T(8,128)(2,1)S(1)} %constant_dynamic-update-slice_fusion, bf16[2048,1408]{1,0:T(8,128)(2,1)} %bitcast.117), kind=kOutput, calls=%fused_computation.87 | convolution fusion | flops 5379192832 | bytes 16261120 | tf_op jit(solution)/shard_map/dot_general | solution.py:26
  734.8 2.3 concatenate.24
  737.2 10.4 %convolution_convert_fusion = bf16[2048,1280]{1,0:T(8,128)(2,1)} fusion(bf16[1024,2048]{1,0:T(8,128)(2,1)} %copy-done.19, bf16[1024,1280]{1,0:T(8,128)(2,1)} %copy-done.21), kind=kOutput, calls=%fused_computation.13 | convolution fusion | flops 5371330560 | bytes 12058624 | tf_op jit(solution)/shard_map/dot_general | solution.py:34
  747.6 140.2 %shard_map.294 = (bf16[4,256,1280]{2,1,0:T(8,128)(2,1)}, bf16[4,256,128]{2,1,0:T(8,128)(2,1)}, bf16[4,128,2048]{2,1,0:T(8,128)(2,1)}) custom-call(bf16[4,2,256,1280]{3,2,1,0:T(8,128)(2,1)} %bitcast.102, bf16[4,2,256,128]{3,2,1,0:T(8,128)(2,1)} %bitcast.105, bf16[4,2,128,2048]{3,2,1,0:T(8,128)(2,1)} %bitcast.103), custom_call_target="tpu_custom_call" | custom-call | bytes 419430400 | tf_op jit(solution)/shard_map/pallas_call | solution.py:973
  887.8 1.7 copy-done.5
  889.6 1.2 copy-done.6
  890.8 1.0 copy-done.9
  891.8 1.0 copy-done.10
  892.9 0.9 copy-done.11
  893.8 8.1 shard_map.295
  (134 shorter events, 15.9 us)
Async XLA Ops:
  7.2 5.7 copy-start
  7.2 6.8 copy-start.22
  7.2 6.8 copy-start.26
  7.2 121.6 %all-gather.3.cloned.1.call-start = ((), (), s32[]{:S(2)}) async-start(), calls=%async_computation.5 | async-start | bytes 18874368 | tf_op jit(solution)/shard_map/all_gather | solution.py:1384
  8.0 622.5 %all-gather.5.cloned.1.call-start = ((), (), s32[]{:S(2)}) async-start(), calls=%async_computation.6 | async-start | bytes 5242880 | tf_op jit(solution)/shard_map/all_gather | solution.py:1352
  103.8 11.8 %copy-start.24 = (f32[1,2,4,128]{3,1,2,0:T(2,128)}, f32[1,2,4,128]{3,1,2,0:T(2,128)S(1)}, u32[]{:S(2)}) copy-start(f32[1,2,4,128]{3,1,2,0:T(2,128)S(1)} %copy.100) | copy-start | bytes 12292
  103.9 11.7 %copy-start.13 = (f32[1,2048]{1,0:T(1,128)}, f32[1,2048]{1,0:T(1,128)S(1)}, u32[]{:S(2)}) copy-start(f32[1,2048]{1,0:T(1,128)S(1)} %get-tuple-element.155.gain_ref) | copy-start | bytes 24580
  108.5 3.9 copy-start.23
  114.3 7.2 slice-start
  115.6 5.9 slice-start.1
  119.5 2.0 copy-start.19
  129.4 136.5 %copy-start.2 = (bf16[1,256,2048]{2,1,0:T(8,128)(2,1)S(1)}, bf16[1,256,2048]{2,1,0:T(8,128)(2,1)}, u32[]{:S(2)}) copy-start(bf16[1,256,2048]{2,1,0:T(8,128)(2,1)} %param.19) | copy-start | bytes 3145732
  267.9 274.5 %copy-start.17 = (f32[256,2048]{1,0:T(8,128)}, f32[256,2048]{1,0:T(8,128)S(1)}, u32[]{:S(2)}) copy-start(f32[256,2048]{1,0:T(8,128)S(1)} %get-tuple-element.151.resid_ref) | copy-start | bytes 6291460
  541.1 1.3 copy-start.20
  544.7 69.1 %all-to-all-start.1 = ((bf16[8,4,80,1024]{3,2,1,0:T(8,128)(2,1)}), bf16[8,4,80,1024]{3,2,1,0:T(8,128)(2,1)}, u32[]{:S(2)}, u32[]{:S(2)}) async-start(bf16[8,4,80,1024]{3,2,1,0:T(8,128)(2,1)} %get-tuple-element.64), calls=%async_computation.1 | async-start | bytes 10485760 | tf_op jit(solution)/shard_map/all_to_all | solution.py:1358
  552.8 14.3 %copy-start.28 = (bf16[8,4,80,768]{3,2,1,0:T(8,128)(2,1)S(1)}, bf16[8,4,80,768]{3,2,1,0:T(8,128)(2,1)}, u32[]{:S(2)}) copy-start(bf16[8,4,80,768]{3,2,1,0:T(8,128)(2,1)} %get-tuple-element.70) | copy-start | bytes 11796484
  613.8 65.0 %all-to-all-start = ((bf16[8,4,80,1024]{3,2,1,0:T(8,128)(2,1)}), bf16[8,4,80,1024]{3,2,1,0:T(8,128)(2,1)}, u32[]{:S(2)}, u32[]{:S(2)}) async-start(bf16[8,4,80,1024]{3,2,1,0:T(8,128)(2,1)} %get-tuple-element.63), calls=%async_computation | async-start | bytes 10485760 | tf_op jit(solution)/shard_map/all_to_all | solution.py:1358
  618.5 66.0 %reduce-scatter.4.cloned.1.call-start = ((), (), s32[]{:S(2)}) async-start(), calls=%async_computation.7 | async-start | bytes 2621440 | tf_op jit(solution)/shard_map/reduce_scatter | solution.py:1355
  630.4 102.4 %reduce-scatter.6.cloned.1.call-start = ((), (), s32[]{:S(2)}) async-start(), calls=%async_computation.8 | async-start | bytes 2621440 | tf_op jit(solution)/shard_map/reduce_scatter | solution.py:1355
  630.5 14.3 %copy-start.27 = (bf16[1024,2048]{1,0:T(8,128)(2,1)S(1)}, bf16[1024,2048]{1,0:T(8,128)(2,1)}, u32[]{:S(2)}) copy-start(bf16[1024,2048]{1,0:T(8,128)(2,1)} %all-gather.5.cloned.1.call-done) | copy-start | bytes 12582916
  644.8 8.3 copy-start.29
  659.3 25.6 %copy-start.4 = (s32[1024,1]{1,0:T(8,128)S(1)}, s32[1024,1]{1,0:T(8,128)}, u32[]{:S(2)}) copy-start(s32[1024,1]{1,0:T(8,128)} %copy.76.key_ref) | copy-start | bytes 12292
  659.3 25.6 %copy-start.7 = (f32[1024,128]{1,0:T(8,128)S(1)}, f32[1024,128]{1,0:T(8,128)}, u32[]{:S(2)}) copy-start(f32[1024,128]{1,0:T(8,128)} %constant.61.clone.cos_ref) | copy-start | bytes 1572868
  659.3 25.6 %copy-start.8 = (f32[1024,128]{1,0:T(8,128)S(1)}, f32[1024,128]{1,0:T(8,128)}, u32[]{:S(2)}) copy-start(f32[1024,128]{1,0:T(8,128)} %constant.62.clone.sin_ref) | copy-start | bytes 1572868
  659.3 25.6 %copy-start.12 = (s32[8,1024]{1,0:T(8,128)S(1)}, s32[8,1024]{1,0:T(8,128)}, u32[]{:S(2)}) copy-start(s32[8,1024]{1,0:T(8,128)} %broadcast_in_dim.77.own_ref) | copy-start | bytes 98308
  659.3 25.6 %copy-start.15 = (f32[8,128]{1,0:T(8,128)S(1)}, f32[8,128]{1,0:T(8,128)}, u32[]{:S(2)}) copy-start(f32[8,128]{1,0:T(8,128)} %maximum_convert_fusion.gains_ref) | copy-start | bytes 12292
  659.3 25.6 %copy-start.16 = (f32[8,8,1024]{2,1,0:T(8,128)S(1)}, f32[8,8,1024]{2,1,0:T(8,128)}, u32[]{:S(2)}) copy-start(f32[8,8,1024]{2,1,0:T(8,128)} %get-tuple-element.76.total_ref) | copy-start | bytes 786436
  684.5 203.3 %reduce-scatter.8.cloned.1.call-start = ((), (), s32[]{:S(2)}) async-start(), calls=%async_computation.9 | async-start | bytes 5242880 | tf_op jit(solution)/shard_map/reduce_scatter | solution.py:1355
  719.9 3.1 copy-start.18
  719.9 3.1 copy-start.25
  720.1 1.6 copy-start.21
  747.6 140.2 %copy-start.3 = (bf16[1,256,2048]{2,1,0:T(8,128)(2,1)S(1)}, bf16[1,256,2048]{2,1,0:T(8,128)(2,1)}, u32[]{:S(2)}) copy-start(bf16[1,256,2048]{2,1,0:T(8,128)(2,1)} %param.19) | copy-start | bytes 3145732
  747.6 140.2 %copy-start.14 = (f32[1,2048]{1,0:T(1,128)S(1)}, f32[1,2048]{1,0:T(1,128)}, u32[]{:S(2)}) copy-start(f32[1,2048]{1,0:T(1,128)} %copy-done.13) | copy-start | bytes 24580
  887.8 15.9 %copy-start.1 = (bf16[256,4096]{1,0:T(8,128)(2,1)S(1)}, bf16[256,4096]{1,0:T(8,128)(2,1)}, u32[]{:S(2)}) copy-start(bf16[256,4096]{1,0:T(8,128)(2,1)} %param.24) | copy-start | bytes 6291460
  887.8 1.7 copy-start.5
  889.6 1.2 copy-start.6
  890.8 1.0 copy-start.9
  891.8 1.0 copy-start.10
  892.9 0.9 copy-start.11
Sparse Core Ops, SparseCore 0:
  9.9 118.5 all-gather.2
  544.8 85.5 all-gather.4
  632.7 42.3 reduce-scatter.3
  684.6 42.3 reduce-scatter.5
  733.0 92.9 reduce-scatter.7
